TPU v7x, 32 devices: a whole 2x2x4 slice. The times are simulated.
32 devices in a mesh: seqhi: 4 (over x, core), seqlo: 8 (over z, y).
Axes of the slice: x: 2, y: 2, z: 4, core: 2. Of those that a mesh axis runs over, the one named last changes fastest.
Arguments:
- queries: bfloat16 [8192, 2048], P(('seqhi', 'seqlo')), may hold values from -6 to 6
- keys: bfloat16 [8192, 128], P(('seqhi', 'seqlo')), may hold values from -6 to 6
- values: bfloat16 [8192, 128], P(('seqhi', 'seqlo')), may hold values from -6 to 6
- outputs: bfloat16 [8192, 2048], P(('seqhi', 'seqlo')), may hold values from -6 to 6
- out_grad: bfloat16 [8192, 2048], P(('seqhi', 'seqlo')), may hold values from -96 to 96
- lse: float32 [16, 8192], P(None, ('seqhi', 'seqlo')), may hold values from 7 to 9
- sink_keys: bfloat16 [128, 128], replicated, may hold values from -6 to 6
- sink_values: bfloat16 [128, 128], replicated, may hold values from -6 to 6
- window_len: int32 [16], replicated, may hold values from 256 to 2048, as said below
- sink_live: int32 [16], replicated, may hold values from 32 to 128, as said below
Outputs:
- query_grad: float32 [8192, 2048], P(('seqhi', 'seqlo'))
- key_grad: float32 [8192, 128], P(('seqhi', 'seqlo'))
- value_grad: float32 [8192, 128], P(('seqhi', 'seqlo'))
- sink_key_grad: float32 [128, 128], replicated
- sink_value_grad: float32 [128, 128], replicated
Inputs may be any that keep to these rules, and one draw needn't show every extreme that they name: `window_len`: one head's window is exactly 2048. `sink_live`: one head reads all 128 initial keys.
All inputs are finite; a program needn't handle non-finite values.
Results may differ from a plain program's by a relative error of at most 0.0039.
Values may be sent and summed in bfloat16 or wider, within the bound.
No kernel may reach another device: no remote copies, remote signals or barrier semaphores. Data moves between devices by JAX's collectives and lax.ppermute only.
A program may use at most 64 MiB of HBM per device.

v0:
```python
import functools
import math

import jax
import jax.numpy as jnp
from jax import lax
from jax.experimental import pallas as pl
from jax.experimental.pallas import tpu as pltpu
from jax.sharding import PartitionSpec as P

WIN = 2048
AXES = ("seqhi", "seqlo")
LOG2E = math.log2(math.e)
NN = (((1,), (0,)), ((), ()))
NT = (((1,), (1,)), ((), ()))
VMEM_BYTES = 30 * 1024 * 1024
UNROLL = 4
LOW = jnp.bfloat16
VMEM = pl.BlockSpec(memory_space=pltpu.VMEM)
SMEM = pl.BlockSpec(memory_space=pltpu.SMEM)


def dot(left, right, dims=NN):
    return lax.dot_general(left, right, dims, preferred_element_type=jnp.float32)


def rotated(block, distance):
    count = lax.axis_size(AXES)
    return lax.ppermute(block, AXES, [(i, (i + distance) % count) for i in range(count)])


def exchange_sum(block):
    for axis in ("seqlo", "seqhi"):
        count = lax.axis_size(axis)
        if count & (count - 1):
            block = lax.psum(block, axis)
            continue
        step = 1
        while step < count:
            block = block + lax.ppermute(block, axis, [(i, i ^ step) for i in range(count)])
            step *= 2
    return block


def span(index, size):
    return pl.ds(pl.multiple_of(index * size, size), size)


def sink_kernel(
    live_ref, query_ref, grad_ref, out_ref, lse_ref, sink_ref,
    query_t_ref, grad_t_ref, delta_ref, dquery_ref, sink_grad_ref,
    *, heads, width, scale,
):
    rows = query_ref.shape[0]
    sinks = sink_ref.shape[0]
    key, value = sink_ref[:, :width], sink_ref[:, width:]
    key_t = key.T
    sink_grad_ref[...] = jnp.zeros_like(sink_grad_ref)

    def one_head(head):
        lanes = span(head, width)
        strip = span(head, width)
        query_t = query_ref[:, lanes].T
        grad_t = grad_ref[:, lanes].T
        query_t_ref[strip, :] = query_t
        grad_t_ref[strip, :] = grad_t
        product = grad_t.astype(jnp.float32) * out_ref[:, lanes].T.astype(jnp.float32)
        delta = jnp.sum(product, axis=0, keepdims=True)
        delta_ref[pl.ds(head, 1), :] = delta
        probs = jnp.exp2(dot(key, query_t) * (scale * LOG2E) - lse_ref[pl.ds(head, 1), :] * LOG2E)
        at = lax.broadcasted_iota(jnp.int32, (sinks, rows), 0)
        probs = jnp.where(at < live_ref[head], probs, 0.0)
        dscores = (probs * (dot(value, grad_t) - delta)).astype(LOW)
        sink_grad_ref[:width, :] += dot(query_t, dscores, NT) * scale
        sink_grad_ref[width:, :] += dot(grad_t, probs.astype(LOW), NT)
        dquery_ref[strip, :] = dot(key_t, dscores)

    def some_heads(step, carry):
        for part in range(2):
            one_head(2 * step + part)
        return carry

    lax.fori_loop(0, heads // 2, some_heads, 0)


def block_kernel(
    window_ref, device_ref, query_t_ref, grad_t_ref, lse_ref, delta_ref, dquery_in, *rest,
    distances, heads, width, scale, causal,
):
    count = len(distances)
    pair_refs = rest[:count]
    dquery_ref = rest[count]
    out_refs = rest[count + 1 : 2 * count + 1]
    items_ref, pair_ref, key_t_ref, sum_ref, total_ref = rest[2 * count + 1 : 2 * count + 6]
    low_refs = rest[2 * count + 6 :]
    rows = pair_ref.shape[1]
    for slot in range(count):
        pair_ref[slot] = pair_refs[slot][...]
        key_t_ref[slot] = pair_refs[slot][:, :width].T
    sum_ref[...] = jnp.zeros_like(sum_ref)
    if not causal:
        dquery_ref[...] = dquery_in[...]
    dtotal_ref = total_ref if causal else dquery_ref
    if causal:
        total_ref[...] = dquery_in[...]
    for ref in low_refs:
        ref[...] = jnp.zeros_like(ref)

    def list_items(slot, distance, found):
        def one_head(head, found):
            left = window_ref[head] - distance * rows
            needed = (left > 1 - rows) & (device_ref[0] >= distance)

            @pl.when(needed)
            def _():
                items_ref[0, found] = slot
                items_ref[1, found] = head
                items_ref[2, found] = left

            return found + needed.astype(jnp.int32)

        return lax.fori_loop(0, heads, one_head, found)

    found = 0
    for slot, distance in enumerate(distances):
        found = list_items(slot, distance, found)
    steps = lax.div(found + UNROLL - 1, UNROLL)

    def pad_item(index, carry):
        items_ref[0, index] = 0
        items_ref[1, index] = 0
        items_ref[2, index] = -rows
        return carry

    lax.fori_loop(found, steps * UNROLL, pad_item, 0)

    def produce(index, probs_ref, dscores_ref):
        slot, head, left = items_ref[0, index], items_ref[1, index], items_ref[2, index]
        strip = span(head, width)
        scores = dot(pair_ref[slot, :, :width], query_t_ref[strip, :])
        probs = jnp.exp2(scores * (scale * LOG2E) - lse_ref[pl.ds(head, 1), :] * LOG2E)
        key_at = lax.broadcasted_iota(jnp.int32, (rows, 1), 0)
        query_at = lax.broadcasted_iota(jnp.int32, (1, rows), 1)
        keep = query_at - left < key_at
        if causal:
            keep = keep & (key_at <= query_at)
        probs = jnp.where(keep, probs, 0.0)
        dprobs = dot(pair_ref[slot, :, width:], grad_t_ref[strip, :])
        probs_ref[...] = probs.astype(LOW)
        dscores_ref[...] = (probs * (dprobs - delta_ref[pl.ds(head, 1), :])).astype(LOW)

    def consume(index, probs_ref, dscores_ref):
        slot, head = items_ref[0, index], items_ref[1, index]
        strip = span(head, width)
        dscores = dscores_ref[...]
        sum_ref[slot, width:, :] += dot(grad_t_ref[strip, :], probs_ref[...], NT)
        sum_ref[slot, :width, :] += dot(query_t_ref[strip, :], dscores, NT)
        dtotal_ref[strip, :] += dot(key_t_ref[slot], dscores)

    buffers = (low_refs[:2], low_refs[2:])

    def some_items(step, carry):
        for part in range(UNROLL):
            index = step * UNROLL + part
            produce(index, *buffers[part % 2])
            consume(jnp.maximum(index - 1, 0), *buffers[(part + 1) % 2])
        return carry

    lax.fori_loop(0, steps, some_items, 0)

    @pl.when(found > 0)
    def _():
        consume(steps * UNROLL - 1, *buffers[(UNROLL - 1) % 2])

    for slot in range(count):
        out_refs[slot][:width, :] = (sum_ref[slot, :width, :] * scale).astype(out_refs[slot].dtype)
        out_refs[slot][width:, :] = sum_ref[slot, width:, :].astype(out_refs[slot].dtype)
    if causal:

        def turn(head, carry):
            dquery_ref[:, span(head, width)] = total_ref[span(head, width), :].T * scale
            return carry

        lax.fori_loop(0, heads, turn, 0)


def block_call(distances, heads, width, rows, causal, args, pairs):
    count = len(distances)
    wide = heads * width
    kind = jnp.float32 if causal else LOW
    dquery = (rows, wide) if causal else (wide, rows)
    return pl.pallas_call(
        functools.partial(
            block_kernel, distances=distances, heads=heads, width=width, scale=width**-0.5, causal=causal
        ),
        out_shape=(jax.ShapeDtypeStruct(dquery, jnp.float32),)
        + tuple(jax.ShapeDtypeStruct((2 * width, rows), kind) for _ in distances),
        in_specs=[SMEM] * 2 + [VMEM] * (5 + count),
        out_specs=(VMEM,) * (1 + count),
        scratch_shapes=[
            pltpu.SMEM((3, count * heads + UNROLL), jnp.int32),
            pltpu.VMEM((count, rows, 2 * width), LOW),
            pltpu.VMEM((count, width, rows), LOW),
            pltpu.VMEM((count, 2 * width, rows), jnp.float32),
            pltpu.VMEM((wide, rows) if causal else (8, rows), jnp.float32),
        ]
        + [pltpu.VMEM((rows, rows), LOW)] * 4,
        compiler_params=pltpu.CompilerParams(vmem_limit_bytes=VMEM_BYTES),
        cost_estimate=pl.CostEstimate(flops=1, bytes_accessed=1, transcendentals=0),
        name="blocks_" + "_".join(str(d) for d in distances),
    )(*args, *pairs)


def join_kernel(own_ref, *rest, width):
    key_ref, value_ref = rest[-2:]
    total = own_ref[...]
    for ref in rest[:-2]:
        total = total + ref[...].astype(jnp.float32)
    turned = total.T
    key_ref[...] = turned[:, :width]
    value_ref[...] = turned[:, width:]


def on_device(
    queries, keys, values, outputs, out_grad, lse, sink_keys, sink_values, window_len, sink_live
):
    rows = queries.shape[0]
    heads = lse.shape[0]
    width = keys.shape[1]
    sinks = sink_keys.shape[0]
    wide = heads * width
    reach = WIN // rows
    device = lax.axis_index(AXES).astype(jnp.int32).reshape(1)
    own_pair = jnp.concatenate([keys, values], axis=1)
    sink_pair = jnp.concatenate([sink_keys, sink_values], axis=1)
    order = [d for d in (2, 4, 6, 8, 1, 7, 3, 5) if d <= reach]
    order += [d for d in range(1, reach + 1) if d not in order]
    groups = [tuple(order[i : i + 2]) for i in range(0, len(order), 2)]
    arrived = {d: rotated(own_pair, d) for d in order}

    query_t, grad_t, delta, dquery, sink_grad = pl.pallas_call(
        functools.partial(sink_kernel, heads=heads, width=width, scale=width**-0.5),
        out_shape=(
            jax.ShapeDtypeStruct((wide, rows), LOW),
            jax.ShapeDtypeStruct((wide, rows), LOW),
            jax.ShapeDtypeStruct((heads, rows), jnp.float32),
            jax.ShapeDtypeStruct((wide, rows), jnp.float32),
            jax.ShapeDtypeStruct((2 * width, sinks), jnp.float32),
        ),
        in_specs=[SMEM] + [VMEM] * 5,
        out_specs=(VMEM,) * 5,
        compiler_params=pltpu.CompilerParams(vmem_limit_bytes=VMEM_BYTES),
        cost_estimate=pl.CostEstimate(flops=1, bytes_accessed=1, transcendentals=0),
        name="sink_keys_part",
    )(sink_live, queries, out_grad, outputs, lse, sink_pair)

    sink_total = exchange_sum(sink_grad)
    returned = []
    for group in groups:
        args = (window_len, device, query_t, grad_t, lse, delta, dquery)
        results = block_call(group, heads, width, rows, False, args, [arrived[d] for d in group])
        dquery = results[0]
        for distance, block in zip(group, results[1:]):
            returned.append(rotated(block, -distance))
    args = (window_len, device, query_t, grad_t, lse, delta, dquery)
    dquery, own_grad = block_call((0,), heads, width, rows, True, args, [own_pair])
    key_grad, value_grad = pl.pallas_call(
        functools.partial(join_kernel, width=width),
        out_shape=(jax.ShapeDtypeStruct((rows, width), jnp.float32),) * 2,
        in_specs=[VMEM] * (1 + len(returned)),
        out_specs=(VMEM,) * 2,
        compiler_params=pltpu.CompilerParams(vmem_limit_bytes=VMEM_BYTES),
        name="join",
    )(own_grad, *returned)
    return (dquery, key_grad, value_grad, sink_total[:width].T, sink_total[width:].T)


def solution(mesh):
    split = P(AXES, None)
    return jax.shard_map(
        on_device,
        mesh=mesh,
        in_specs=(split,) * 5 + (P(None, AXES),) + (P(),) * 4,
        out_specs=(split,) * 3 + (P(),) * 2,
        check_vma=False,
    )
```

profile of v0, /device:TPU:0, one launch (start us, length us, event | category | flops | bytes accessed | tf_op | source)
XLA Modules:
  0.0 88.3 jit_solution(8540988068456784711)
XLA Ops:
  1.5 1.2 %copy-done.2 = bf16[256,2048]{1,0:T(8,128)(2,1)S(1)} copy-done((bf16[256,2048]{1,0:T(8,128)(2,1)S(1)}, bf16[256,2048]{1,0:T(8,128)(2,1)}, u32[]{:S(2)}) %copy-start.2) | copy-done | bytes 1048600
  2.7 1.2 %copy-done.3 = bf16[256,2048]{1,0:T(8,128)(2,1)S(1)} copy-done((bf16[256,2048]{1,0:T(8,128)(2,1)S(1)}, bf16[256,2048]{1,0:T(8,128)(2,1)}, u32[]{:S(2)}) %copy-start.3) | copy-done | bytes 1048600
  3.9 1.2 %copy-done.4 = bf16[256,2048]{1,0:T(8,128)(2,1)S(1)} copy-done((bf16[256,2048]{1,0:T(8,128)(2,1)S(1)}, bf16[256,2048]{1,0:T(8,128)(2,1)}, u32[]{:S(2)}) %copy-start.4) | copy-done | bytes 1048600
  6.5 6.1 %sink_keys_part.1 = (bf16[2048,256]{1,0:T(8,128)(2,1)S(1)}, bf16[2048,256]{1,0:T(8,128)(2,1)S(1)}, f32[16,256]{1,0:T(8,128)S(1)}, f32[2048,256]{1,0:T(8,128)S(1)}, f32[256,128]{1,0:T(8,128)S(1)}) custom-call(s32[16]{0:T(128)S(1)} %copy-done.8, bf16[256,2048]{1,0:T(8,128)(2,1)S(1)} %copy-done.2, bf16[256,2048]{1,0:T(8,128)(2,1)S(1)} %copy-done.3, ...), custom_call_target="tpu_custom_call" | custom-call | flops 1 | bytes 1 | tf_op jit(solution)/shard_map/sink_keys_part/pallas_call | solution.py:241
  12.7 1.3 %copy-done = f32[2048,256]{1,0:T(8,128)} copy-done((f32[2048,256]{1,0:T(8,128)}, f32[2048,256]{1,0:T(8,128)S(1)}, u32[]{:S(2)}) %copy-start) | copy-done | bytes 2097176
  14.0 3.0 %collective-permute-start.16 = (f32[256,128]{1,0:T(8,128)S(1)}, f32[256,128]{1,0:T(8,128)S(1)}, u32[]{:S(2)}, u32[]{:S(2)}) collective-permute-start(f32[256,128]{1,0:T(8,128)S(1)} %get-tuple-element.46), channel_id=1, source_target_pairs={{0,1},{1,0},{2,3},{3,2},{4,5},{5,4},{6,7},{7,6},{8,9},{9,8},{10,11... | collective-permute-start | bytes 393224 | tf_op jit(solution)/shard_map/ppermute | solution.py:40
  17.1 3.7 %collective-permute-start.2 = (bf16[256,256]{1,0:T(8,128)(2,1)S(1)}, bf16[256,256]{1,0:T(8,128)(2,1)S(1)}, u32[]{:S(2)}, u32[]{:S(2)}) collective-permute-start(bf16[256,256]{1,0:T(8,128)(2,1)S(1)} %constant_dynamic-update-slice_fusion.rest_0_), channel_id=1, source_target_pairs={{0,6},{1,7},{2,8},{3,9},{4,10},{5,11},{6,12},{7,13},{8,14},{9,15},... | collective-permute-start | bytes 393224 | tf_op jit(solution)/shard_map/ppermute | solution.py:29
  21.3 1.6 %collective-permute-start.17 = (f32[256,128]{1,0:T(8,128)S(1)}, f32[256,128]{1,0:T(8,128)S(1)}, u32[]{:S(2)}, u32[]{:S(2)}) collective-permute-start(f32[256,128]{1,0:T(8,128)S(1)} %add.19), channel_id=1, source_target_pairs={{0,2},{1,3},{2,0},{3,1},{4,6},{5,7},{6,4},{7,5},{8,10},{9,11},{10,... | collective-permute-start | bytes 393224 | tf_op jit(solution)/shard_map/ppermute | solution.py:40
  23.4 2.6 %collective-permute-start.5 = (bf16[256,256]{1,0:T(8,128)(2,1)S(1)}, bf16[256,256]{1,0:T(8,128)(2,1)S(1)}, u32[]{:S(2)}, u32[]{:S(2)}) collective-permute-start(bf16[256,256]{1,0:T(8,128)(2,1)S(1)} %constant_dynamic-update-slice_fusion.rest_0_), channel_id=1, source_target_pairs={{0,7},{1,8},{2,9},{3,10},{4,11},{5,12},{6,13},{7,14},{8,15},{9,16}... | collective-permute-start | bytes 393224 | tf_op jit(solution)/shard_map/ppermute | solution.py:29
  26.0 4.8 %collective-permute-done.1.rest_1_ = bf16[256,256]{1,0:T(8,128)(2,1)S(1)} collective-permute-done((bf16[256,256]{1,0:T(8,128)(2,1)S(1)}, bf16[256,256]{1,0:T(8,128)(2,1)S(1)}, u32[]{:S(2)}, u32[]{:S(2)}) %collective-permute-start.1) | collective-permute-done | bytes 131104 | tf_op jit(solution)/shard_map/ppermute | solution.py:29
  30.8 3.5 %collective-permute-start.6 = (bf16[256,256]{1,0:T(8,128)(2,1)S(1)}, bf16[256,256]{1,0:T(8,128)(2,1)S(1)}, u32[]{:S(2)}, u32[]{:S(2)}) collective-permute-start(bf16[256,256]{1,0:T(8,128)(2,1)S(1)} %constant_dynamic-update-slice_fusion.rest_0_), channel_id=1, source_target_pairs={{0,3},{1,4},{2,5},{3,6},{4,7},{5,8},{6,9},{7,10},{8,11},{9,12},{10... | collective-permute-start | bytes 393224 | tf_op jit(solution)/shard_map/ppermute | solution.py:29
  34.4 1.9 %collective-permute-start.18 = (f32[256,128]{1,0:T(8,128)S(1)}, f32[256,128]{1,0:T(8,128)}, u32[]{:S(2)}, u32[]{:S(2)}) collective-permute-start(f32[256,128]{1,0:T(8,128)S(1)} %add.20), channel_id=1, source_target_pairs={{0,4},{1,5},{2,6},{3,7},{4,0},{5,1},{6,2},{7,3},{8,12},{9,13},{10,... | collective-permute-start | bytes 393224 | tf_op jit(solution)/shard_map/ppermute | solution.py:40
  36.3 1.6 %copy-done.1 = f32[2048,256]{1,0:T(8,128)S(1)} copy-done((f32[2048,256]{1,0:T(8,128)S(1)}, f32[2048,256]{1,0:T(8,128)}, u32[]{:S(2)}) %copy-start.1) | copy-done | bytes 2097176
  39.1 1.2 %blocks_6_8.1 = (f32[2048,256]{1,0:T(8,128)S(1)}, bf16[256,256]{1,0:T(8,128)(2,1)S(1)}, bf16[256,256]{1,0:T(8,128)(2,1)S(1)}) custom-call(s32[16]{0:T(128)S(1)} %copy-done.7, s32[1]{0:T(128)} %bitcast.device_ref, bf16[2048,256]{1,0:T(8,128)(2,1)S(1)} %get-tuple-element.26.query_t_ref, bf16[2048,256]{1,0:T(8,128)(2,1)S(1)} %get-tuple-element.27.grad_t_ref, ...), custom_call_target="tpu_custom_call" | custom-call | flops 1 | bytes 1 | tf_op jit(solution)/shard_map/blocks_6_8/pallas_call | solution.py:192
  40.3 1.2 %blocks_1_7.1 = (f32[2048,256]{1,0:T(8,128)S(1)}, bf16[256,256]{1,0:T(8,128)(2,1)S(1)}, bf16[256,256]{1,0:T(8,128)(2,1)S(1)}) custom-call(s32[16]{0:T(128)S(1)} %copy-done.7, s32[1]{0:T(128)} %bitcast.device_ref, bf16[2048,256]{1,0:T(8,128)(2,1)S(1)} %get-tuple-element.26.query_t_ref, bf16[2048,256]{1,0:T(8,128)(2,1)S(1)} %get-tuple-element.27.grad_t_ref, ...), custom_call_target="tpu_custom_call" | custom-call | flops 1 | bytes 1 | tf_op jit(solution)/shard_map/blocks_1_7/pallas_call | solution.py:192
  41.5 7.0 %collective-permute-done.6.rest_0_ = bf16[256,256]{1,0:T(8,128)(2,1)S(1)} collective-permute-done((bf16[256,256]{1,0:T(8,128)(2,1)S(1)}, bf16[256,256]{1,0:T(8,128)(2,1)S(1)}, u32[]{:S(2)}, u32[]{:S(2)}) %collective-permute-start.6) | collective-permute-done | bytes 131104 | tf_op jit(solution)/shard_map/ppermute | solution.py:29
  48.4 1.2 %blocks_3_5.1 = (f32[2048,256]{1,0:T(8,128)S(1)}, bf16[256,256]{1,0:T(8,128)(2,1)S(1)}, bf16[256,256]{1,0:T(8,128)(2,1)S(1)}) custom-call(s32[16]{0:T(128)S(1)} %copy-done.7, s32[1]{0:T(128)} %bitcast.device_ref, bf16[2048,256]{1,0:T(8,128)(2,1)S(1)} %get-tuple-element.26.query_t_ref, bf16[2048,256]{1,0:T(8,128)(2,1)S(1)} %get-tuple-element.27.grad_t_ref, ...), custom_call_target="tpu_custom_call" | custom-call | flops 1 | bytes 1 | tf_op jit(solution)/shard_map/blocks_3_5/pallas_call | solution.py:192
  49.6 10.9 %collective-permute-start.14 = (bf16[256,256]{1,0:T(8,128)(2,1)S(1)}, bf16[256,256]{1,0:T(8,128)(2,1)S(1)}, u32[]{:S(2)}, u32[]{:S(2)}) collective-permute-start(bf16[256,256]{1,0:T(8,128)(2,1)S(1)} %get-tuple-element.42), channel_id=1, source_target_pairs={{0,29},{1,30},{2,31},{3,0},{4,1},{5,2},{6,3},{7,4},{8,5},{9,6},{10... | collective-permute-start | bytes 393224 | tf_op jit(solution)/shard_map/ppermute | solution.py:29
  60.5 1.9 %collective-permute-start.15 = (bf16[256,256]{1,0:T(8,128)(2,1)S(1)}, bf16[256,256]{1,0:T(8,128)(2,1)S(1)}, u32[]{:S(2)}, u32[]{:S(2)}) collective-permute-start(bf16[256,256]{1,0:T(8,128)(2,1)S(1)} %get-tuple-element.43), channel_id=1, source_target_pairs={{0,27},{1,28},{2,29},{3,30},{4,31},{5,0},{6,1},{7,2},{8,3},{9,4},{... | collective-permute-start | bytes 393224 | tf_op jit(solution)/shard_map/ppermute | solution.py:29
  62.5 3.9 %collective-permute-start.12 = (bf16[256,256]{1,0:T(8,128)(2,1)S(1)}, bf16[256,256]{1,0:T(8,128)(2,1)S(1)}, u32[]{:S(2)}, u32[]{:S(2)}) collective-permute-start(bf16[256,256]{1,0:T(8,128)(2,1)S(1)} %get-tuple-element.40), channel_id=1, source_target_pairs={{0,31},{1,0},{2,1},{3,2},{4,3},{5,4},{6,5},{7,6},{8,7},{9,8},{10,9... | collective-permute-start | bytes 393224 | tf_op jit(solution)/shard_map/ppermute | solution.py:29
  67.5 5.1 %collective-permute-start.10 = (bf16[256,256]{1,0:T(8,128)(2,1)S(1)}, bf16[256,256]{1,0:T(8,128)(2,1)S(1)}, u32[]{:S(2)}, u32[]{:S(2)}) collective-permute-start(bf16[256,256]{1,0:T(8,128)(2,1)S(1)} %get-tuple-element.38), channel_id=1, source_target_pairs={{0,26},{1,27},{2,28},{3,29},{4,30},{5,31},{6,0},{7,1},{8,2},{9,3},... | collective-permute-start | bytes 393224 | tf_op jit(solution)/shard_map/ppermute | solution.py:29
  73.7 2.9 %collective-permute-start.8 = (bf16[256,256]{1,0:T(8,128)(2,1)S(1)}, bf16[256,256]{1,0:T(8,128)(2,1)S(1)}, u32[]{:S(2)}, u32[]{:S(2)}) collective-permute-start(bf16[256,256]{1,0:T(8,128)(2,1)S(1)} %get-tuple-element.36), channel_id=1, source_target_pairs={{0,30},{1,31},{2,0},{3,1},{4,2},{5,3},{6,4},{7,5},{8,6},{9,7},{10,... | collective-permute-start | bytes 393224 | tf_op jit(solution)/shard_map/ppermute | solution.py:29
  77.6 6.9 %blocks_0.1 = (f32[256,2048]{1,0:T(8,128)}, f32[256,256]{1,0:T(8,128)S(1)}) custom-call(s32[16]{0:T(128)S(1)} %copy-done.7, s32[1]{0:T(128)} %bitcast.device_ref, bf16[2048,256]{1,0:T(8,128)(2,1)S(1)} %get-tuple-element.26.query_t_ref, bf16[2048,256]{1,0:T(8,128)(2,1)S(1)} %get-tuple-element.27.grad_t_ref, f32[16,256]{1,0:T(8,128)S(1)} %copy-done.6, ...), custom_call_target="tpu_custom_call" | custom-call | flops 1 | bytes 1 | tf_op jit(solution)/shard_map/blocks_0/pallas_call | solution.py:192
  84.5 1.5 %collective-permute-done.9.rest_1_ = bf16[256,256]{1,0:T(8,128)(2,1)S(1)} collective-permute-done((bf16[256,256]{1,0:T(8,128)(2,1)S(1)}, bf16[256,256]{1,0:T(8,128)(2,1)S(1)}, u32[]{:S(2)}, u32[]{:S(2)}) %collective-permute-start.9) | collective-permute-done | bytes 131104 | tf_op jit(solution)/shard_map/ppermute | solution.py:29
  (58 shorter events, 9.9 us)
Async XLA Ops:
  0.6 16.3 %copy-start.10 = (bf16[256,128]{1,0:T(8,128)(2,1)S(1)}, bf16[256,128]{1,0:T(8,128)(2,1)}, u32[]{:S(2)}) copy-start(bf16[256,128]{1,0:T(8,128)(2,1)} %param.12) | copy-start | bytes 196612
  6.5 29.8 %copy-start.6 = (f32[16,256]{1,0:T(8,128)S(1)}, f32[16,256]{1,0:T(8,128)}, u32[]{:S(2)}) copy-start(f32[16,256]{1,0:T(8,128)} %lse_ref.11) | copy-start | bytes 49156
  6.5 29.8 %copy-start.7 = (s32[16]{0:T(128)S(1)}, s32[16]{0:T(128)}, u32[]{:S(2)}) copy-start(s32[16]{0:T(128)} %window_ref.9) | copy-start | bytes 196
  14.0 7.3 %collective-permute-start.16 = (f32[256,128]{1,0:T(8,128)S(1)}, f32[256,128]{1,0:T(8,128)S(1)}, u32[]{:S(2)}, u32[]{:S(2)}) collective-permute-start(f32[256,128]{1,0:T(8,128)S(1)} %get-tuple-element.46), channel_id=1, source_target_pairs={{0,1},{1,0},{2,3},{3,2},{4,5},{5,4},{6,7},{7,6},{8,9},{9,8},{10,11... | collective-permute-start | bytes 393224 | tf_op jit(solution)/shard_map/ppermute | solution.py:40
  17.0 6.4 %collective-permute-start.3 = (bf16[256,256]{1,0:T(8,128)(2,1)S(1)}, bf16[256,256]{1,0:T(8,128)(2,1)S(1)}, u32[]{:S(2)}, u32[]{:S(2)}) collective-permute-start(bf16[256,256]{1,0:T(8,128)(2,1)S(1)} %constant_dynamic-update-slice_fusion.rest_0_), channel_id=1, source_target_pairs={{0,8},{1,9},{2,10},{3,11},{4,12},{5,13},{6,14},{7,15},{8,16},{9,17... | collective-permute-start | bytes 393224 | tf_op jit(solution)/shard_map/ppermute | solution.py:29
  17.1 8.9 %collective-permute-start.2 = (bf16[256,256]{1,0:T(8,128)(2,1)S(1)}, bf16[256,256]{1,0:T(8,128)(2,1)S(1)}, u32[]{:S(2)}, u32[]{:S(2)}) collective-permute-start(bf16[256,256]{1,0:T(8,128)(2,1)S(1)} %constant_dynamic-update-slice_fusion.rest_0_), channel_id=1, source_target_pairs={{0,6},{1,7},{2,8},{3,9},{4,10},{5,11},{6,12},{7,13},{8,14},{9,15},... | collective-permute-start | bytes 393224 | tf_op jit(solution)/shard_map/ppermute | solution.py:29
  20.7 10.1 %collective-permute-start.1 = (bf16[256,256]{1,0:T(8,128)(2,1)S(1)}, bf16[256,256]{1,0:T(8,128)(2,1)S(1)}, u32[]{:S(2)}, u32[]{:S(2)}) collective-permute-start(bf16[256,256]{1,0:T(8,128)(2,1)S(1)} %constant_dynamic-update-slice_fusion.rest_0_), channel_id=1, source_target_pairs={{0,4},{1,5},{2,6},{3,7},{4,8},{5,9},{6,10},{7,11},{8,12},{9,13},{1... | collective-permute-start | bytes 393224 | tf_op jit(solution)/shard_map/ppermute | solution.py:29
  21.3 9.5 %collective-permute-start.17 = (f32[256,128]{1,0:T(8,128)S(1)}, f32[256,128]{1,0:T(8,128)S(1)}, u32[]{:S(2)}, u32[]{:S(2)}) collective-permute-start(f32[256,128]{1,0:T(8,128)S(1)} %add.19), channel_id=1, source_target_pairs={{0,2},{1,3},{2,0},{3,1},{4,6},{5,7},{6,4},{7,5},{8,10},{9,11},{10,... | collective-permute-start | bytes 393224 | tf_op jit(solution)/shard_map/ppermute | solution.py:40
  23.0 11.4 %collective-permute-start = (bf16[256,256]{1,0:T(8,128)(2,1)S(1)}, bf16[256,256]{1,0:T(8,128)(2,1)S(1)}, u32[]{:S(2)}, u32[]{:S(2)}) collective-permute-start(bf16[256,256]{1,0:T(8,128)(2,1)S(1)} %constant_dynamic-update-slice_fusion.rest_0_), channel_id=1, source_target_pairs={{0,2},{1,3},{2,4},{3,5},{4,6},{5,7},{6,8},{7,9},{8,10},{9,11},{10,... | collective-permute-start | bytes 393224 | tf_op jit(solution)/shard_map/ppermute | solution.py:29
  23.4 16.8 %collective-permute-start.5 = (bf16[256,256]{1,0:T(8,128)(2,1)S(1)}, bf16[256,256]{1,0:T(8,128)(2,1)S(1)}, u32[]{:S(2)}, u32[]{:S(2)}) collective-permute-start(bf16[256,256]{1,0:T(8,128)(2,1)S(1)} %constant_dynamic-update-slice_fusion.rest_0_), channel_id=1, source_target_pairs={{0,7},{1,8},{2,9},{3,10},{4,11},{5,12},{6,13},{7,14},{8,15},{9,16}... | collective-permute-start | bytes 393224 | tf_op jit(solution)/shard_map/ppermute | solution.py:29
  26.0 14.3 %collective-permute-start.4 = (bf16[256,256]{1,0:T(8,128)(2,1)S(1)}, bf16[256,256]{1,0:T(8,128)(2,1)S(1)}, u32[]{:S(2)}, u32[]{:S(2)}) collective-permute-start(bf16[256,256]{1,0:T(8,128)(2,1)S(1)} %constant_dynamic-update-slice_fusion.rest_0_), channel_id=1, source_target_pairs={{0,1},{1,2},{2,3},{3,4},{4,5},{5,6},{6,7},{7,8},{8,9},{9,10},{10,1... | collective-permute-start | bytes 393224 | tf_op jit(solution)/shard_map/ppermute | solution.py:29
  30.8 10.6 %collective-permute-start.7 = (bf16[256,256]{1,0:T(8,128)(2,1)S(1)}, bf16[256,256]{1,0:T(8,128)(2,1)S(1)}, u32[]{:S(2)}, u32[]{:S(2)}) collective-permute-start(bf16[256,256]{1,0:T(8,128)(2,1)S(1)} %constant_dynamic-update-slice_fusion.rest_0_), channel_id=1, source_target_pairs={{0,5},{1,6},{2,7},{3,8},{4,9},{5,10},{6,11},{7,12},{8,13},{9,14},{... | collective-permute-start | bytes 393224 | tf_op jit(solution)/shard_map/ppermute | solution.py:29
  30.8 17.6 %collective-permute-start.6 = (bf16[256,256]{1,0:T(8,128)(2,1)S(1)}, bf16[256,256]{1,0:T(8,128)(2,1)S(1)}, u32[]{:S(2)}, u32[]{:S(2)}) collective-permute-start(bf16[256,256]{1,0:T(8,128)(2,1)S(1)} %constant_dynamic-update-slice_fusion.rest_0_), channel_id=1, source_target_pairs={{0,3},{1,4},{2,5},{3,6},{4,7},{5,8},{6,9},{7,10},{8,11},{9,12},{10... | collective-permute-start | bytes 393224 | tf_op jit(solution)/shard_map/ppermute | solution.py:29
  34.4 32.0 %collective-permute-start.18 = (f32[256,128]{1,0:T(8,128)S(1)}, f32[256,128]{1,0:T(8,128)}, u32[]{:S(2)}, u32[]{:S(2)}) collective-permute-start(f32[256,128]{1,0:T(8,128)S(1)} %add.20), channel_id=1, source_target_pairs={{0,4},{1,5},{2,6},{3,7},{4,0},{5,1},{6,2},{7,3},{8,12},{9,13},{10,... | collective-permute-start | bytes 393224 | tf_op jit(solution)/shard_map/ppermute | solution.py:40
  49.6 17.9 %collective-permute-start.14 = (bf16[256,256]{1,0:T(8,128)(2,1)S(1)}, bf16[256,256]{1,0:T(8,128)(2,1)S(1)}, u32[]{:S(2)}, u32[]{:S(2)}) collective-permute-start(bf16[256,256]{1,0:T(8,128)(2,1)S(1)} %get-tuple-element.42), channel_id=1, source_target_pairs={{0,29},{1,30},{2,31},{3,0},{4,1},{5,2},{6,3},{7,4},{8,5},{9,6},{10... | collective-permute-start | bytes 393224 | tf_op jit(solution)/shard_map/ppermute | solution.py:29
  60.5 12.1 %collective-permute-start.15 = (bf16[256,256]{1,0:T(8,128)(2,1)S(1)}, bf16[256,256]{1,0:T(8,128)(2,1)S(1)}, u32[]{:S(2)}, u32[]{:S(2)}) collective-permute-start(bf16[256,256]{1,0:T(8,128)(2,1)S(1)} %get-tuple-element.43), channel_id=1, source_target_pairs={{0,27},{1,28},{2,29},{3,30},{4,31},{5,0},{6,1},{7,2},{8,3},{9,4},{... | collective-permute-start | bytes 393224 | tf_op jit(solution)/shard_map/ppermute | solution.py:29
  62.5 11.2 %collective-permute-start.12 = (bf16[256,256]{1,0:T(8,128)(2,1)S(1)}, bf16[256,256]{1,0:T(8,128)(2,1)S(1)}, u32[]{:S(2)}, u32[]{:S(2)}) collective-permute-start(bf16[256,256]{1,0:T(8,128)(2,1)S(1)} %get-tuple-element.40), channel_id=1, source_target_pairs={{0,31},{1,0},{2,1},{3,2},{4,3},{5,4},{6,5},{7,6},{8,7},{9,8},{10,9... | collective-permute-start | bytes 393224 | tf_op jit(solution)/shard_map/ppermute | solution.py:29
  67.3 9.3 %collective-permute-start.19 = (f32[256,128]{1,0:T(8,128)S(1)}, f32[256,128]{1,0:T(8,128)S(1)}, u32[]{:S(2)}, u32[]{:S(2)}) collective-permute-start(f32[256,128]{1,0:T(8,128)S(1)} %add.21), channel_id=1, source_target_pairs={{0,8},{8,0},{16,24},{24,16},{1,9},{9,1},{17,25},{25,17},{2,10},{10... | collective-permute-start | bytes 393224 | tf_op jit(solution)/shard_map/ppermute | solution.py:40
  67.4 9.3 %collective-permute-start.13 = (bf16[256,256]{1,0:T(8,128)(2,1)S(1)}, bf16[256,256]{1,0:T(8,128)(2,1)S(1)}, u32[]{:S(2)}, u32[]{:S(2)}) collective-permute-start(bf16[256,256]{1,0:T(8,128)(2,1)S(1)} %get-tuple-element.41), channel_id=1, source_target_pairs={{0,25},{1,26},{2,27},{3,28},{4,29},{5,30},{6,31},{7,0},{8,1},{9,2}... | collective-permute-start | bytes 393224 | tf_op jit(solution)/shard_map/ppermute | solution.py:29
  67.5 16.9 %collective-permute-start.10 = (bf16[256,256]{1,0:T(8,128)(2,1)S(1)}, bf16[256,256]{1,0:T(8,128)(2,1)S(1)}, u32[]{:S(2)}, u32[]{:S(2)}) collective-permute-start(bf16[256,256]{1,0:T(8,128)(2,1)S(1)} %get-tuple-element.38), channel_id=1, source_target_pairs={{0,26},{1,27},{2,28},{3,29},{4,30},{5,31},{6,0},{7,1},{8,2},{9,3},... | collective-permute-start | bytes 393224 | tf_op jit(solution)/shard_map/ppermute | solution.py:29
  72.6 11.8 %collective-permute-start.11 = (bf16[256,256]{1,0:T(8,128)(2,1)S(1)}, bf16[256,256]{1,0:T(8,128)(2,1)S(1)}, u32[]{:S(2)}, u32[]{:S(2)}) collective-permute-start(bf16[256,256]{1,0:T(8,128)(2,1)S(1)} %get-tuple-element.39), channel_id=1, source_target_pairs={{0,24},{1,25},{2,26},{3,27},{4,28},{5,29},{6,30},{7,31},{8,0},{9,1... | collective-permute-start | bytes 393224 | tf_op jit(solution)/shard_map/ppermute | solution.py:29
  73.7 10.8 %collective-permute-start.8 = (bf16[256,256]{1,0:T(8,128)(2,1)S(1)}, bf16[256,256]{1,0:T(8,128)(2,1)S(1)}, u32[]{:S(2)}, u32[]{:S(2)}) collective-permute-start(bf16[256,256]{1,0:T(8,128)(2,1)S(1)} %get-tuple-element.36), channel_id=1, source_target_pairs={{0,30},{1,31},{2,0},{3,1},{4,2},{5,3},{6,4},{7,5},{8,6},{9,7},{10,... | collective-permute-start | bytes 393224 | tf_op jit(solution)/shard_map/ppermute | solution.py:29
  76.6 9.3 %collective-permute-start.9 = (bf16[256,256]{1,0:T(8,128)(2,1)S(1)}, bf16[256,256]{1,0:T(8,128)(2,1)S(1)}, u32[]{:S(2)}, u32[]{:S(2)}) collective-permute-start(bf16[256,256]{1,0:T(8,128)(2,1)S(1)} %get-tuple-element.37), channel_id=1, source_target_pairs={{0,28},{1,29},{2,30},{3,31},{4,0},{5,1},{6,2},{7,3},{8,4},{9,5},{1... | collective-permute-start | bytes 393224 | tf_op jit(solution)/shard_map/ppermute | solution.py:29
  76.7 10.2 %collective-permute-start.20 = (f32[256,128]{1,0:T(8,128)S(1)}, f32[256,128]{1,0:T(8,128)S(1)}, u32[]{:S(2)}, u32[]{:S(2)}) collective-permute-start(f32[256,128]{1,0:T(8,128)S(1)} %add.22), channel_id=1, source_target_pairs={{0,16},{8,24},{16,0},{24,8},{1,17},{9,25},{17,1},{25,9},{2,18},{10... | collective-permute-start | bytes 393224 | tf_op jit(solution)/shard_map/ppermute | solution.py:40
  (8 other events, 24.3 us)
where the time goes:
time: 88 us; the launch traced here: 88.3 us
  starting transfers between devices  44.4 us (50%)
  Pallas kernels  18.5 us (21%)
  waiting for transfers between devices  13.4 us (15%)
  local copies, waits for them, and re-layouts  9.46 us (11%)
  other arithmetic  1.8 us (2%)
    ppermute x16, starting transfers between devices, rotated(): lax.ppermute(block, AXES, [(i, (i + distance) % count) for i in range(cou...  36.9 us
    ppermute x16, waiting for transfers between devices, rotated(): lax.ppermute(block, AXES, [(i, (i + distance) % count) for i in range(cou...  13.3 us
    pallas_call x5, Pallas kernels, block_call(): pl.pallas_call(functools.partial(block_kernel, distances=distances, heads...  11.5 us
    unnamed x25, local copies, waits for them, and re-layouts  9.43 us
    ppermute x5, starting transfers between devices, exchange_sum(): lax.ppermute(block, axis, [(i, i ^ step) for i in range(count)])  7.51 us
    pallas_call x1, Pallas kernels, on_device(): pl.pallas_call(functools.partial(sink_kernel, heads=heads, width=width, s...  6.13 us
  transfers between devices with their start and end apart: 21, of which 3 were waited for; matrix products, arithmetic and copies ran while one was open for 1% of the time, Pallas kernels for 14%

commit v1 on v0

v1 whole, which is shorter than its diff:
```python
import functools
import math

import jax
import jax.numpy as jnp
from jax import lax
from jax.experimental import pallas as pl
from jax.experimental.pallas import tpu as pltpu
from jax.sharding import PartitionSpec as P

WIN = 2048
AXES = ("seqhi", "seqlo")
LOG2E = math.log2(math.e)
NN = (((1,), (0,)), ((), ()))
NT = (((1,), (1,)), ((), ()))
VMEM_BYTES = 22 * 1024 * 1024
UNROLL = 4
LOW = jnp.bfloat16
VMEM = pl.BlockSpec(memory_space=pltpu.VMEM)
SMEM = pl.BlockSpec(memory_space=pltpu.SMEM)
HBM = pl.BlockSpec(memory_space=pltpu.HBM)
ANY = pl.BlockSpec(memory_space=pl.ANY)


def dot(left, right, dims=NN):
    return lax.dot_general(left, right, dims, preferred_element_type=jnp.float32)


def rotated(block, distance):
    count = lax.axis_size(AXES)
    return lax.ppermute(block, AXES, [(i, (i + distance) % count) for i in range(count)])


def swapped(block, move):
    flips = dict.fromkeys(AXES, 0)
    for axis, step in move:
        flips[axis] ^= step
    sizes = [lax.axis_size(axis) for axis in AXES]
    route = []
    for i in range(sizes[0] * sizes[1]):
        high, low = divmod(i, sizes[1])
        route.append((i, (high ^ flips[AXES[0]]) * sizes[1] + (low ^ flips[AXES[1]])))
    return lax.ppermute(block, AXES, route)


def exchange_rounds():
    rounds = []
    for axis in AXES:
        step = 1
        while step < lax.axis_size(axis):
            rounds.append((axis, step))
            step *= 2
    return rounds


def span(index, size):
    return pl.ds(pl.multiple_of(index * size, size), size)


def sink_kernel(
    table_ref, key_ref, value_ref, query_ref, grad_ref, out_ref, lse_in, sink_key_ref, sink_value_ref,
    turned_ref, row_ref, dquery_ref, sink_grad_ref, own_ref,
    *, heads, width, scale,
):
    rows = query_ref.shape[0]
    sinks = sink_key_ref.shape[0]
    sink_grad_ref[...] = jnp.zeros_like(sink_grad_ref)
    own_ref[:, :width] = key_ref[...]
    own_ref[:, width:] = value_ref[...]
    row_ref[:heads, :] = lse_in[...] * LOG2E
    key, value = sink_key_ref[...], sink_value_ref[...]
    key_t = key.T

    def one_head(head):
        strip = span(head, width)
        query_t = query_ref[:, strip].T
        grad_t = grad_ref[:, strip].T
        turned_ref[strip, :] = query_t
        turned_ref[span(heads + head, width), :] = grad_t
        product = grad_t.astype(jnp.float32) * out_ref[:, strip].T.astype(jnp.float32)
        delta = jnp.sum(product, axis=0, keepdims=True)
        row_ref[pl.ds(heads + head, 1), :] = delta
        probs = jnp.exp2(dot(key, query_t) * (scale * LOG2E) - row_ref[pl.ds(head, 1), :])
        at = lax.broadcasted_iota(jnp.int32, (sinks, rows), 0)
        probs = jnp.where(at < table_ref[heads + head], probs, 0.0)
        dscores = (probs * (dot(value, grad_t) - delta)).astype(LOW)
        sink_grad_ref[:width, :] += dot(query_t, dscores, NT) * scale
        sink_grad_ref[width:, :] += dot(grad_t, probs.astype(LOW), NT)
        dquery_ref[strip, :] = dot(key_t, dscores)

    def some_heads(step, carry):
        for part in range(UNROLL):
            one_head(UNROLL * step + part)
        return carry

    lax.fori_loop(0, heads // UNROLL, some_heads, 0)


def sum_of(refs):
    total = refs[0][...].astype(jnp.float32)
    for ref in refs[1:]:
        total = total + ref[...].astype(jnp.float32)
    return total


def mark_kernel(window_ref, live_ref, device_ref, block_ref, table_ref, same_ref):
    heads = window_ref.shape[0]
    for head in range(heads):
        table_ref[head] = window_ref[head]
        table_ref[heads + head] = live_ref[head]
    table_ref[2 * heads] = device_ref[0]


def fold_kernel(device_ref, first_ref, second_ref, other_ref, *refs, rows, terms, odd_only):
    outs = refs[terms:]
    outs[0][...] = (first_ref[...] + other_ref[:, :rows].astype(jnp.float32)).astype(LOW)
    other = other_ref[:, rows:].astype(jnp.float32)
    if odd_only:
        odd = jnp.full(other.shape, device_ref[device_ref.shape[0] - 1] & 1, jnp.int32) == 1
        other = jnp.where(odd, other, 0.0)
    outs[1][...] = (second_ref[...] + other).astype(LOW)
    if terms:
        outs[2][...] = sum_of(refs[:terms]).astype(LOW)


def send_kernel(device_ref, own_ref, two_ref, four_ref, six_ref, eight_ref, *refs):
    near_ref, far_ref, sum_ref = refs[-3:]
    rows = own_ref.shape[0]
    odd = jnp.full(own_ref.shape, device_ref[device_ref.shape[0] - 1] & 1, jnp.int32) == 1
    near_ref[:rows, :] = two_ref[...]
    near_ref[rows:, :] = four_ref[...]
    far_ref[:rows, :] = six_ref[...]
    far_ref[rows:, :] = jnp.where(odd, eight_ref[...], own_ref[...])
    sum_ref[...] = sum_of(refs[:-3])


def local(distances, device):
    return [
        jnp.where(device & 1 == 1, distance[1], distance[0]) if isinstance(distance, tuple) else distance
        for distance in distances
    ]


def block_kernel(*refs, layout, groups, heads, width, scale):
    refs = list(refs)

    def take(count):
        taken = refs[:count]
        del refs[:count]
        return taken

    pairs, sink_count, back_count, joined, last = layout
    table_ref, turned_ref, row_ref = take(3)
    device = table_ref[2 * heads]
    distances = local([distance for pair in pairs for distance in pair], device)
    pair_refs = take(len(pairs))
    sink_refs = take(sink_count)
    back_refs = take(back_count)
    part_refs = take(1 + len(groups)) if last else []
    take(1)
    dquery_ref = take(1)[0]
    out_refs = take(1 if joined else len(distances))
    sink_out_refs = take(1 if sink_count else 0)
    items_ref, pair_ref, key_t_ref, sum_ref = take(4)
    low_refs = take(4)
    total_ref, total_sems = take(2) if last else (None, None)
    rows = pair_ref.shape[1]

    slot = 0
    for ref, members in zip(pair_refs, pairs):
        for place in range(len(members)):
            block = ref[place * rows : (place + 1) * rows, :]
            pair_ref[slot] = block
            key_t_ref[slot] = block[:, :width].T
            slot += 1
    sum_ref[...] = jnp.zeros_like(sum_ref)
    for ref in low_refs:
        ref[...] = jnp.zeros_like(ref)

    def needed(head, distance):
        return (table_ref[head] - distance * rows > 1 - rows) & (device >= distance)

    def list_head(head, found):
        before = found
        for slot, distance in enumerate(distances):
            items_ref[0, found] = slot
            items_ref[1, found] = head
            items_ref[2, found] = table_ref[head] - distance * rows
            items_ref[3, found] = (found == before).astype(jnp.int32)
            found = found + needed(head, distance).astype(jnp.int32)
        return found

    found = lax.fori_loop(0, heads, list_head, 0)
    steps = lax.div(found + UNROLL - 1, UNROLL)

    def pad_item(index, carry):
        items_ref[0, index] = 0
        items_ref[1, index] = 0
        items_ref[2, index] = -rows
        items_ref[3, index] = 0
        return carry

    lax.fori_loop(found, steps * UNROLL, pad_item, 0)

    def produce(index, probs_ref, dscores_ref):
        slot, head, left = items_ref[0, index], items_ref[1, index], items_ref[2, index]
        strip = span(head, width)
        scores = dot(pair_ref[slot, :, :width], turned_ref[strip, :])
        probs = jnp.exp2(scores * (scale * LOG2E) - row_ref[pl.ds(head, 1), :])
        key_at = lax.broadcasted_iota(jnp.int32, (rows, 1), 0)
        query_at = lax.broadcasted_iota(jnp.int32, (1, rows), 1)
        keep = query_at - left < key_at
        if last:
            keep = keep & (key_at <= query_at)
        probs = jnp.where(keep, probs, 0.0)
        dprobs = dot(pair_ref[slot, :, width:], turned_ref[span(heads + head, width), :])
        probs_ref[...] = probs.astype(LOW)
        dscores_ref[...] = (probs * (dprobs - row_ref[pl.ds(heads + head, 1), :])).astype(LOW)

    def consume(index, probs_ref, dscores_ref):
        slot, head = items_ref[0, index], items_ref[1, index]
        strip = span(head, width)
        dscores = dscores_ref[...]
        sum_ref[slot, width:, :] += dot(turned_ref[span(heads + head, width), :], probs_ref[...], NT)
        sum_ref[slot, :width, :] += dot(turned_ref[strip, :], dscores, NT)
        dquery = dot(key_t_ref[slot], dscores)
        if last:
            dquery = dquery + part_refs[0][strip, :]
            for ref, group in zip(part_refs[1:], groups):
                touched = functools.reduce(jnp.logical_or, [needed(head, distance) for distance in local(group, device)])
                dquery = dquery + jnp.where(touched, ref[strip, :], 0.0)
            total_ref[:, strip] = dquery.T * scale
        else:
            dquery_ref[strip, :] = dquery + jnp.where(items_ref[3, index] == 1, 0.0, dquery_ref[strip, :])

    buffers = (low_refs[:2], low_refs[2:])

    def total_copy(step):
        lanes = span(step, UNROLL * width)
        return pltpu.make_async_copy(total_ref.at[:, lanes], dquery_ref.at[:, lanes], total_sems.at[step])

    def some_items(step, carry):
        for part in range(UNROLL):
            index = step * UNROLL + part
            produce(index, *buffers[part % 2])
            consume(jnp.maximum(index - 1, 0), *buffers[(part + 1) % 2])
        if last:
            pl.when(step > 0)(lambda: total_copy(step - 1).start())
        return carry

    lax.fori_loop(0, steps, some_items, 0)

    @pl.when(found > 0)
    def _():
        consume(steps * UNROLL - 1, *buffers[(UNROLL - 1) % 2])

    if last:
        total_copy(heads // UNROLL - 1).start()
    for slot in range(len(distances)):
        grads = (sum_ref[slot, :width, :] * scale, sum_ref[slot, width:, :])
        for half, grad in enumerate(grads):
            strip = slice(half * width, (half + 1) * width)
            for ref in back_refs:
                grad = grad + ref[strip, :].astype(jnp.float32)
            if joined:
                out_refs[0][strip, slot * rows : (slot + 1) * rows] = grad.astype(out_refs[0].dtype)
            else:
                out_refs[slot][strip, :] = grad.astype(out_refs[slot].dtype)
    if sink_count:
        sink_out_refs[0][...] = sum_of(sink_refs)
    if last:
        for step in range(heads // UNROLL):
            total_copy(step).wait()


def block_call(pairs, pair_arrays, shared, after, sinks=(), backs=(), parts=(), groups=(), last=False, kind=LOW, joined=False):
    table, turned, row_terms = shared
    wide, rows = turned.shape[0] // 2, turned.shape[1]
    heads = row_terms.shape[0] // 2
    width = wide // heads
    distances = [distance for pair in pairs for distance in pair]
    count = len(distances)
    shape = jax.ShapeDtypeStruct
    outs = [shape((rows, wide) if last else (wide, rows), jnp.float32)]
    outs += [shape((2 * width, count * rows), kind)] if joined else [shape((2 * width, rows), kind)] * count
    if sinks:
        outs.append(shape(sinks[0].shape, jnp.float32))
    arrays = [turned, row_terms, *pair_arrays, *sinks, *backs, *parts, after]
    layout = (pairs, len(sinks), len(backs), joined, last)
    return pl.pallas_call(
        functools.partial(
            block_kernel, layout=layout, groups=groups, heads=heads, width=width, scale=width**-0.5
        ),
        out_shape=outs,
        in_specs=[SMEM] + [VMEM] * (len(arrays) - 1) + [ANY],
        out_specs=[HBM if last else VMEM] + [VMEM] * (len(outs) - 1),
        scratch_shapes=[
            pltpu.SMEM((4, count * heads + UNROLL), jnp.int32),
            pltpu.VMEM((count, rows, 2 * width), LOW),
            pltpu.VMEM((count, width, rows), LOW),
            pltpu.VMEM((count, 2 * width, rows), jnp.float32),
        ]
        + [pltpu.VMEM((rows, rows), LOW)] * 4
        + ([pltpu.VMEM((rows, wide), jnp.float32), pltpu.SemaphoreType.DMA((heads // UNROLL,))] if last else []),
        compiler_params=pltpu.CompilerParams(vmem_limit_bytes=VMEM_BYTES),
        cost_estimate=pl.CostEstimate(
            flops=10 * count * rows * rows * wide, bytes_accessed=2 * rows * wide, transcendentals=0
        ),
        name="blocks_" + "_".join(str(d[0] if isinstance(d, tuple) else d) for d in distances),
    )(table, *arrays)


def join_kernel(device_ref, own_ref, other_ref, *refs, backs, width):
    key_ref, value_ref, sink_key_ref, sink_value_ref = refs[-4:]
    rows = own_ref.shape[1]
    odd = jnp.full(own_ref.shape, device_ref[device_ref.shape[0] - 1] & 1, jnp.int32) == 1
    total = own_ref[...] + jnp.where(odd, 0.0, other_ref[:, rows:].astype(jnp.float32))
    turned = (total + sum_of(refs[:backs])).T
    key_ref[...] = turned[:, :width]
    value_ref[...] = turned[:, width:]
    turned = sum_of(refs[backs:-4]).T
    sink_key_ref[...] = turned[:, :width]
    sink_value_ref[...] = turned[:, width:]


def on_device(
    queries, keys, values, outputs, out_grad, lse, sink_keys, sink_values, window_len, sink_live
):
    rows = queries.shape[0]
    heads = lse.shape[0]
    width = keys.shape[1]
    sinks = sink_keys.shape[0]
    wide = heads * width
    shape = jax.ShapeDtypeStruct
    device = lax.axis_index(AXES).astype(jnp.int32).reshape(1)
    own_pair = jnp.concatenate([keys, values], axis=1)
    table, own_pair = pl.pallas_call(
        mark_kernel,
        out_shape=(shape((2 * heads + 1,), jnp.int32), shape(own_pair.shape, LOW)),
        in_specs=[SMEM] * 3 + [ANY],
        out_specs=(SMEM, ANY),
        input_output_aliases={3: 1},
        compiler_params=pltpu.CompilerParams(vmem_limit_bytes=1024 * 1024),
        cost_estimate=pl.CostEstimate(flops=2 * 10**10, bytes_accessed=1, transcendentals=0),
        name="mark",
    )(window_len, sink_live, device, own_pair)
    even = {d: rotated(own_pair, d) for d in (2, 4, 6, 8)}

    turned, row_terms, dquery, sink_grad, own_held = pl.pallas_call(
        functools.partial(sink_kernel, heads=heads, width=width, scale=width**-0.5),
        out_shape=(
            shape((2 * wide, rows), LOW),
            shape((2 * heads, rows), jnp.float32),
            shape((wide, rows), jnp.float32),
            shape((2 * width, sinks), jnp.float32),
            shape((rows, 2 * width), LOW),
        ),
        in_specs=[SMEM] + [VMEM] * 8,
        out_specs=(VMEM,) * 5,
        compiler_params=pltpu.CompilerParams(vmem_limit_bytes=VMEM_BYTES),
        cost_estimate=pl.CostEstimate(flops=10**10, bytes_accessed=10**6, transcendentals=0),
        name="sink_keys_part",
    )(table, keys, values, queries, out_grad, outputs, lse, sink_keys, sink_values)

    rounds = exchange_rounds()

    def sink_terms(count):
        moves = [()]
        for _ in range(min(count, len(rounds))):
            here = rounds.pop(0)
            moves = moves + [move + (here,) for move in moves]
        return [sink_grad] + [swapped(sink_grad, move) for move in moves[1:]]

    near, far, sink_grad = pl.pallas_call(
        send_kernel,
        out_shape=(shape((2 * rows, 2 * width), LOW),) * 2 + (shape(sink_grad.shape, jnp.float32),),
        in_specs=[SMEM] + [VMEM] * (7 if rounds else 6),
        out_specs=(VMEM,) * 3,
        compiler_params=pltpu.CompilerParams(vmem_limit_bytes=VMEM_BYTES),
        name="send_blocks",
    )(table, own_held, even[2], even[4], even[6], even[8], *sink_terms(1))
    partner = ((AXES[-1], 1),)
    near_odd, far_odd = swapped(near, partner), swapped(far, partner)

    shared = (table, turned, row_terms)
    parts = [dquery]
    sums = sink_terms(2)
    full = jnp.float32
    near_pair, far_pair = ((1, 3), (3, 5)), ((5, 7), (7, 1))
    part, grad_2, grad_4 = block_call([(2,), (4,)], [even[2], even[4]], shared, dquery, kind=full)
    parts.append(part)

    part, odd, sink_grad = block_call([near_pair], [near_odd], shared, part, sinks=sums, joined=True)
    parts.append(part)
    sums = sink_terms(1)
    near_other = swapped(odd, partner)

    part, odd = block_call([far_pair], [far_odd], shared, part, joined=True)
    parts.append(part)
    far_other = swapped(odd, partner)

    part, grad_6, grad_8 = block_call([(6,), (8,)], [even[6], even[8]], shared, part, kind=full)
    parts.append(part)

    def fold(first, second, other, terms=(), odd_only=False):
        outs = [shape(first.shape, LOW)] * 2 + ([shape(sink_grad.shape, LOW)] if terms else [])
        return pl.pallas_call(
            functools.partial(fold_kernel, rows=rows, terms=len(terms), odd_only=odd_only),
            out_shape=outs,
            in_specs=[SMEM] + [VMEM] * (3 + len(terms)),
            out_specs=[VMEM] * len(outs),
            compiler_params=pltpu.CompilerParams(vmem_limit_bytes=VMEM_BYTES),
            name="fold",
        )(table, first, second, other, *terms)

    grad_2, grad_4, sink_grad = fold(grad_2, grad_4, near_other, sums)
    sums = sink_terms(1)
    backs = [rotated(grad_2, -2), rotated(grad_4, -4)]
    grad_6, grad_8 = fold(grad_6, grad_8, far_other, odd_only=True)
    backs += [rotated(grad_6, -6), rotated(grad_8, -8)]
    dquery, own_grad = block_call(
        [(0,)], [own_held], shared, grad_8, parts=parts, kind=full, last=True,
        groups=((2, 4), near_pair, far_pair, (6, 8)),
    )
    while rounds:
        sink_grad = sum(sums)
        sums = sink_terms(1)
    key_grad, value_grad, sink_key_grad, sink_value_grad = pl.pallas_call(
        functools.partial(join_kernel, backs=len(backs), width=width),
        out_shape=(shape((rows, width), jnp.float32),) * 2 + (shape((sinks, width), jnp.float32),) * 2,
        in_specs=[SMEM] + [VMEM] * (2 + len(backs) + len(sums)),
        out_specs=(VMEM,) * 4,
        compiler_params=pltpu.CompilerParams(vmem_limit_bytes=VMEM_BYTES),
        name="join",
    )(table, own_grad, far_other, *backs, *sums)
    return (dquery, key_grad, value_grad, sink_key_grad, sink_value_grad)


def solution(mesh):
    split = P(AXES, None)
    return jax.shard_map(
        on_device,
        mesh=mesh,
        in_specs=(split,) * 5 + (P(None, AXES),) + (P(),) * 4,
        out_specs=(split,) * 3 + (P(),) * 2,
        check_vma=False,
    )
```

time: 88 us -> 74.9 us (0.85); the launches traced: 88.3 us -> 74.2 us
  starting transfers between devices: 44.4 us -> 31.4 us
  local copies, waits for them, and re-layouts: 9.46 us -> 1.35 us
  waiting for transfers between devices: 13.4 us -> 20.4 us
  other arithmetic: 1.8 us -> 0.89 us
    ppermute x16 -> x8, starting transfers between devices: 36.9 us -> 17.2 us  [rotated(): lax.ppermute(block, AXES, [(i, (i + distance) % count) for i in range(cou...]
    ppermute x5 -> x10, waiting for transfers between devices: 0.01 us -> 15.4 us  [swapped(): return lax.ppermute(block, AXES, route)]
    ppermute x16 -> x8, waiting for transfers between devices: 13.3 us -> 5.08 us  [rotated(): lax.ppermute(block, AXES, [(i, (i + distance) % count) for i in range(cou...]
    unnamed x25 -> x20, local copies, waits for them, and re-layouts: 9.43 us -> 1.35 us
    ppermute x5 -> x10, starting transfers between devices: 7.51 us -> 14.2 us  [swapped(): return lax.ppermute(block, AXES, route)]
    pallas_call x6 -> x10, Pallas kernels: 12.4 us -> 13.8 us  [the longest x5 9.49 us: block_call(): pl.pallas_call(functools.partial(block_kernel, layout=layout, groups=grou...]
    add x5 -> x0, other arithmetic: 0.98 us -> none  [exchange_sum(): block + lax.ppermute(block, axis, [(i, i ^ step) for i in range(count)])]
  transfers between devices with their start and end apart: 21 -> 18, of which waited for: 3 -> 6; matrix products, arithmetic and copies ran while one was open for 1% -> 0% of each run, Pallas kernels for 14% -> 22%
where the time goes in v1:
time: 74.9 us; the launch traced here: 74.2 us
  starting transfers between devices  31.4 us (42%)
  waiting for transfers between devices  20.4 us (27%)
  Pallas kernels  19.3 us (26%)
  local copies, waits for them, and re-layouts  1.35 us (2%)
  other arithmetic  0.89 us (1%)
  between operations  0.85 us (1%)
    ppermute x8, starting transfers between devices, rotated(): lax.ppermute(block, AXES, [(i, (i + distance) % count) for i in range(cou...  17.2 us
    ppermute x10, waiting for transfers between devices, swapped(): return lax.ppermute(block, AXES, route)  15.4 us
    ppermute x10, starting transfers between devices, swapped(): return lax.ppermute(block, AXES, route)  14.2 us
    pallas_call x5, Pallas kernels, block_call(): pl.pallas_call(functools.partial(block_kernel, layout=layout, groups=grou...  9.49 us
    pallas_call x1, Pallas kernels, on_device(): pl.pallas_call(functools.partial(sink_kernel, heads=heads, width=width, s...  5.42 us
    ppermute x8, waiting for transfers between devices, rotated(): lax.ppermute(block, AXES, [(i, (i + distance) % count) for i in range(cou...  5.08 us
  transfers between devices with their start and end apart: 18, of which 6 were waited for; matrix products, arithmetic and copies ran while one was open for 0% of the time, Pallas kernels for 22%

profile of v1, /device:TPU:0, one launch (start us, length us, event | category | flops | bytes accessed | tf_op | source)
XLA Modules:
  0.0 74.2 jit_solution(4288708211926682198)
XLA Ops:
  2.9 1.2 %mark.1 = (s32[33]{0:T(128)S(1)}, bf16[256,256]{1,0:T(8,128)(2,1)S(1)}) custom-call(s32[16]{0:T(128)S(1)} %copy-done.8, s32[16]{0:T(128)S(1)} %copy-done.9, s32[1]{0:T(128)} %bitcast.device_ref, bf16[256,256]{1,0:T(8,128)(2,1)S(1)} %pad_maximum_fusion.block_ref), custom_call_target="tpu_custom_call", output_to_operand_aliasing={{1}: (3, {})} | custom-call | flops 20000000000 | bytes 1 | tf_op jit(solution)/shard_map/mark/pallas_call | solution.py:337
  4.6 4.7 %collective-permute-start.2 = (bf16[256,256]{1,0:T(8,128)(2,1)S(1)}, bf16[256,256]{1,0:T(8,128)(2,1)S(1)}, u32[]{:S(2)}, u32[]{:S(2)}) collective-permute-start(bf16[256,256]{1,0:T(8,128)(2,1)S(1)} %get-tuple-element.42), channel_id=1, source_target_pairs={{0,6},{1,7},{2,8},{3,9},{4,10},{5,11},{6,12},{7,13},{8,14},{9,15},... | collective-permute-start | bytes 393224 | tf_op jit(solution)/shard_map/ppermute | solution.py:31
  9.8 1.6 %collective-permute-start = (bf16[256,256]{1,0:T(8,128)(2,1)S(1)}, bf16[256,256]{1,0:T(8,128)(2,1)S(1)}, u32[]{:S(2)}, u32[]{:S(2)}) collective-permute-start(bf16[256,256]{1,0:T(8,128)(2,1)S(1)} %get-tuple-element.42), channel_id=1, source_target_pairs={{0,2},{1,3},{2,4},{3,5},{4,6},{5,7},{6,8},{7,9},{8,10},{9,11},{10,... | collective-permute-start | bytes 393224 | tf_op jit(solution)/shard_map/ppermute | solution.py:31
  11.5 5.4 %sink_keys_part.1 = (bf16[4096,256]{1,0:T(8,128)(2,1)S(1)}, f32[32,256]{1,0:T(8,128)S(1)}, f32[2048,256]{1,0:T(8,128)S(1)}, f32[256,128]{1,0:T(8,128)S(1)}, bf16[256,256]{1,0:T(8,128)(2,1)S(1)}) custom-call(s32[33]{0:T(128)S(1)} %get-tuple-element.37.table_ref.refs_0_.device_ref, bf16[256,128]{1,0:T(8,128)(2,1)S(1)} %copy-done.1, ...), custom_call_target="tpu_custom_call" | custom-call | flops 10000000000 | bytes 1000000 | tf_op jit(solution)/shard_map/sink_keys_part/pallas_call | solution.py:349
  17.0 5.1 %collective-permute-done.1.refs_4_.four_ref = bf16[256,256]{1,0:T(8,128)(2,1)S(1)} collective-permute-done((bf16[256,256]{1,0:T(8,128)(2,1)S(1)}, bf16[256,256]{1,0:T(8,128)(2,1)S(1)}, u32[]{:S(2)}, u32[]{:S(2)}) %collective-permute-start.1) | collective-permute-done | bytes 131104 | tf_op jit(solution)/shard_map/ppermute | solution.py:31
  22.6 1.6 %collective-permute-start.5 = (bf16[512,256]{1,0:T(8,128)(2,1)S(1)}, bf16[512,256]{1,0:T(8,128)(2,1)S(1)}, u32[]{:S(2)}, u32[]{:S(2)}) collective-permute-start(bf16[512,256]{1,0:T(8,128)(2,1)S(1)} %get-tuple-element.45), channel_id=1, source_target_pairs={{0,1},{1,0},{2,3},{3,2},{4,5},{5,4},{6,7},{7,6},{8,9},{9,8},{10,11... | collective-permute-start | bytes 786440 | tf_op jit(solution)/shard_map/ppermute | solution.py:43
  24.2 1.4 %collective-permute-start.8 = (f32[256,128]{1,0:T(8,128)S(1)}, f32[256,128]{1,0:T(8,128)S(1)}, u32[]{:S(2)}, u32[]{:S(2)}) collective-permute-start(f32[256,128]{1,0:T(8,128)S(1)} %get-tuple-element.46.refs_4_), channel_id=1, source_target_pairs={{0,17},{1,16},{2,19},{3,18},{4,21},{5,20},{6,23},{7,22},{8,25},{9,... | collective-permute-start | bytes 393224 | tf_op jit(solution)/shard_map/ppermute | solution.py:43
  25.7 1.5 %collective-permute-start.7 = (f32[256,128]{1,0:T(8,128)S(1)}, f32[256,128]{1,0:T(8,128)S(1)}, u32[]{:S(2)}, u32[]{:S(2)}) collective-permute-start(f32[256,128]{1,0:T(8,128)S(1)} %get-tuple-element.46.refs_4_), channel_id=1, source_target_pairs={{0,1},{1,0},{2,3},{3,2},{4,5},{5,4},{6,7},{7,6},{8,9},{9,8},{10,11... | collective-permute-start | bytes 393224 | tf_op jit(solution)/shard_map/ppermute | solution.py:43
  28.2 1.0 %blocks_2_4.1 = (f32[2048,256]{1,0:T(8,128)S(1)}, f32[256,256]{1,0:T(8,128)S(1)}, f32[256,256]{1,0:T(8,128)S(1)}) custom-call(s32[33]{0:T(128)S(1)} %get-tuple-element.37.table_ref.refs_0_.device_ref, bf16[4096,256]{1,0:T(8,128)(2,1)S(1)} %get-tuple-element.38.refs_1_, f32[32,256]{1,0:T(8,128)S(1)} %get-tuple-element.39.refs_2_, ...), custom_call_target="tpu_custom_call" | custom-call | flops 2684354560 | bytes 1048576 | tf_op jit(solution)/shard_map/blocks_2_4/pallas_call | solution.py:290
  29.3 2.2 %collective-permute-done.8.refs_7_ = f32[256,128]{1,0:T(8,128)S(1)} collective-permute-done((f32[256,128]{1,0:T(8,128)S(1)}, f32[256,128]{1,0:T(8,128)S(1)}, u32[]{:S(2)}, u32[]{:S(2)}) %collective-permute-start.8) | collective-permute-done | bytes 131104 | tf_op jit(solution)/shard_map/ppermute | solution.py:43
  31.5 6.0 %collective-permute-done.7.refs_6_ = f32[256,128]{1,0:T(8,128)S(1)} collective-permute-done((f32[256,128]{1,0:T(8,128)S(1)}, f32[256,128]{1,0:T(8,128)S(1)}, u32[]{:S(2)}, u32[]{:S(2)}) %collective-permute-start.7) | collective-permute-done | bytes 131104 | tf_op jit(solution)/shard_map/ppermute | solution.py:43
  37.5 1.0 %blocks_1_3.1 = (f32[2048,256]{1,0:T(8,128)S(1)}, bf16[256,512]{1,0:T(8,128)(2,1)S(1)}, f32[256,128]{1,0:T(8,128)S(1)}) custom-call(s32[33]{0:T(128)S(1)} %get-tuple-element.37.table_ref.refs_0_.device_ref, bf16[4096,256]{1,0:T(8,128)(2,1)S(1)} %get-tuple-element.38.refs_1_, f32[32,256]{1,0:T(8,128)S(1)} %get-tuple-element.39.refs_2_, ...), custom_call_target="tpu_custom_call" | custom-call | flops 2684354560 | bytes 1048576 | tf_op jit(solution)/shard_map/blocks_1_3/pallas_call | solution.py:290
  38.5 1.6 %collective-permute-start.11 = (bf16[256,512]{1,0:T(8,128)(2,1)S(1)}, bf16[256,512]{1,0:T(8,128)(2,1)S(1)}, u32[]{:S(2)}, u32[]{:S(2)}) collective-permute-start(bf16[256,512]{1,0:T(8,128)(2,1)S(1)} %get-tuple-element.59), channel_id=1, source_target_pairs={{0,1},{1,0},{2,3},{3,2},{4,5},{5,4},{6,7},{7,6},{8,9},{9,8},{10,11... | collective-permute-start | bytes 786440 | tf_op jit(solution)/shard_map/ppermute | solution.py:43
  40.1 2.2 %collective-permute-done.9.refs_3_ = bf16[512,256]{1,0:T(8,128)(2,1)S(1)} collective-permute-done((bf16[512,256]{1,0:T(8,128)(2,1)S(1)}, bf16[512,256]{1,0:T(8,128)(2,1)S(1)}, u32[]{:S(2)}, u32[]{:S(2)}) %collective-permute-start.9) | collective-permute-done | bytes 262176 | tf_op jit(solution)/shard_map/ppermute | solution.py:43
  42.3 1.0 %blocks_5_7.1 = (f32[2048,256]{1,0:T(8,128)S(1)}, bf16[256,512]{1,0:T(8,128)(2,1)S(1)}) custom-call(s32[33]{0:T(128)S(1)} %get-tuple-element.37.table_ref.refs_0_.device_ref, bf16[4096,256]{1,0:T(8,128)(2,1)S(1)} %get-tuple-element.38.refs_1_, f32[32,256]{1,0:T(8,128)S(1)} %get-tuple-element.39.refs_2_, bf16[512,256]{1,0:T(8,128)(2,1)S(1)} %collective-permute-done.9.refs_3_, ...), custom_call_target="tpu_custom_call" | custom-call | flops 2684354560 | bytes 1048576 | tf_op jit(solution)/shard_map/blocks_5_7/pallas_call | solution.py:290
  43.3 4.7 %collective-permute-start.10 = (bf16[256,512]{1,0:T(8,128)(2,1)S(1)}, bf16[256,512]{1,0:T(8,128)(2,1)S(1)}, u32[]{:S(2)}, u32[]{:S(2)}) collective-permute-start(bf16[256,512]{1,0:T(8,128)(2,1)S(1)} %get-tuple-element.53), channel_id=1, source_target_pairs={{0,1},{1,0},{2,3},{3,2},{4,5},{5,4},{6,7},{7,6},{8,9},{9,8},{10,11... | collective-permute-start | bytes 786440 | tf_op jit(solution)/shard_map/ppermute | solution.py:43
  48.6 1.0 %blocks_6_8.1 = (f32[2048,256]{1,0:T(8,128)S(1)}, f32[256,256]{1,0:T(8,128)S(1)}, f32[256,256]{1,0:T(8,128)S(1)}) custom-call(s32[33]{0:T(128)S(1)} %get-tuple-element.37.table_ref.refs_0_.device_ref, bf16[4096,256]{1,0:T(8,128)(2,1)S(1)} %get-tuple-element.38.refs_1_, f32[32,256]{1,0:T(8,128)S(1)} %get-tuple-element.39.refs_2_, ...), custom_call_target="tpu_custom_call" | custom-call | flops 2684354560 | bytes 1048576 | tf_op jit(solution)/shard_map/blocks_6_8/pallas_call | solution.py:290
  49.6 3.5 %collective-permute-done.12.refs_1_ = f32[256,128]{1,0:T(8,128)S(1)} collective-permute-done((f32[256,128]{1,0:T(8,128)S(1)}, f32[256,128]{1,0:T(8,128)S(1)}, u32[]{:S(2)}, u32[]{:S(2)}) %collective-permute-start.12) | collective-permute-done | bytes 131104 | tf_op jit(solution)/shard_map/ppermute | solution.py:43
  53.7 2.5 %collective-permute-start.13 = (bf16[256,256]{1,0:T(8,128)(2,1)S(1)}, bf16[256,256]{1,0:T(8,128)(2,1)S(1)}, u32[]{:S(2)}, u32[]{:S(2)}) collective-permute-start(bf16[256,256]{1,0:T(8,128)(2,1)S(1)} %get-tuple-element.61), channel_id=1, source_target_pairs={{0,30},{1,31},{2,0},{3,1},{4,2},{5,3},{6,4},{7,5},{8,6},{9,7},{10,... | collective-permute-start | bytes 393224 | tf_op jit(solution)/shard_map/ppermute | solution.py:31
  57.6 6.7 %collective-permute-start.15 = (bf16[256,256]{1,0:T(8,128)(2,1)S(1)}, bf16[256,256]{1,0:T(8,128)(2,1)S(1)}, u32[]{:S(2)}, u32[]{:S(2)}) collective-permute-start(bf16[256,256]{1,0:T(8,128)(2,1)S(1)} %get-tuple-element.63), channel_id=1, source_target_pairs={{0,26},{1,27},{2,28},{3,29},{4,30},{5,31},{6,0},{7,1},{8,2},{9,3},... | collective-permute-start | bytes 393224 | tf_op jit(solution)/shard_map/ppermute | solution.py:31
  64.2 1.7 %collective-permute-start.17 = (bf16[256,128]{1,0:T(8,128)(2,1)S(1)}, bf16[256,128]{1,0:T(8,128)(2,1)S(1)}, u32[]{:S(2)}, u32[]{:S(2)}) collective-permute-start(bf16[256,128]{1,0:T(8,128)(2,1)S(1)} %get-tuple-element.64.refs_4_), channel_id=1, source_target_pairs={{0,4},{1,5},{2,6},{3,7},{4,0},{5,1},{6,2},{7,3},{8,12},{9,13},{10,... | collective-permute-start | bytes 196616 | tf_op jit(solution)/shard_map/ppermute | solution.py:43
  65.9 5.4 %blocks_0.1 = (f32[256,2048]{1,0:T(8,128)}, f32[256,256]{1,0:T(8,128)S(1)}) custom-call(s32[33]{0:T(128)S(1)} %get-tuple-element.37.table_ref.refs_0_.device_ref, bf16[4096,256]{1,0:T(8,128)(2,1)S(1)} %get-tuple-element.38.refs_1_, f32[32,256]{1,0:T(8,128)S(1)} %get-tuple-element.39.refs_2_, bf16[256,256]{1,0:T(8,128)(2,1)S(1)} %get-tuple-element.40.own_ref.refs_3_, ...), custom_call_target="tpu_custom_call" | custom-call | flops 1342177280 | bytes 1048576 | tf_op jit(solution)/shard_map/blocks_0/pallas_call | solution.py:290
  71.3 1.5 %collective-permute-done.17.refs_5_ = bf16[256,128]{1,0:T(8,128)(2,1)S(1)} collective-permute-done((bf16[256,128]{1,0:T(8,128)(2,1)S(1)}, bf16[256,128]{1,0:T(8,128)(2,1)S(1)}, u32[]{:S(2)}, u32[]{:S(2)}) %collective-permute-start.17) | collective-permute-done | bytes 65568 | tf_op jit(solution)/shard_map/ppermute | solution.py:43
  72.8 1.4 %join.1 = (f32[256,128]{1,0:T(8,128)}, f32[256,128]{1,0:T(8,128)}, f32[128,128]{1,0:T(8,128)}, f32[128,128]{1,0:T(8,128)}) custom-call(s32[33]{0:T(128)S(1)} %get-tuple-element.37.table_ref.refs_0_.device_ref, f32[256,256]{1,0:T(8,128)S(1)} %get-tuple-element.56.own_ref, bf16[256,512]{1,0:T(8,128)(2,1)S(1)} %collective-permute-done.10.other_ref, ...), custom_call_target="tpu_custom_call" | custom-call | tf_op jit(solution)/shard_map/join/pallas_call | solution.py:428
  (44 shorter events, 7.6 us)
Async XLA Ops:
  2.8 8.6 %copy-start = (bf16[256,128]{1,0:T(8,128)(2,1)S(1)}, bf16[256,128]{1,0:T(8,128)(2,1)}, u32[]{:S(2)}) copy-start(bf16[256,128]{1,0:T(8,128)(2,1)} %value_ref.1) | copy-start | bytes 196612
  2.8 8.6 %copy-start.1 = (bf16[256,128]{1,0:T(8,128)(2,1)S(1)}, bf16[256,128]{1,0:T(8,128)(2,1)}, u32[]{:S(2)}) copy-start(bf16[256,128]{1,0:T(8,128)(2,1)} %key_ref.1) | copy-start | bytes 196612
  2.8 8.6 %copy-start.2 = (bf16[256,2048]{1,0:T(8,128)(2,1)S(1)}, bf16[256,2048]{1,0:T(8,128)(2,1)}, u32[]{:S(2)}) copy-start(bf16[256,2048]{1,0:T(8,128)(2,1)} %query_ref.1) | copy-start | bytes 3145732
  2.9 8.6 %copy-start.3 = (bf16[256,2048]{1,0:T(8,128)(2,1)S(1)}, bf16[256,2048]{1,0:T(8,128)(2,1)}, u32[]{:S(2)}) copy-start(bf16[256,2048]{1,0:T(8,128)(2,1)} %grad_ref.1) | copy-start | bytes 3145732
  2.9 8.6 %copy-start.4 = (bf16[256,2048]{1,0:T(8,128)(2,1)S(1)}, bf16[256,2048]{1,0:T(8,128)(2,1)}, u32[]{:S(2)}) copy-start(bf16[256,2048]{1,0:T(8,128)(2,1)} %out_ref.1) | copy-start | bytes 3145732
  2.9 8.6 %copy-start.5 = (bf16[128,128]{1,0:T(8,128)(2,1)S(1)}, bf16[128,128]{1,0:T(8,128)(2,1)}, u32[]{:S(2)}) copy-start(bf16[128,128]{1,0:T(8,128)(2,1)} %sink_key_ref.1) | copy-start | bytes 98308
  4.1 12.9 %collective-permute-start.3 = (bf16[256,256]{1,0:T(8,128)(2,1)S(1)}, bf16[256,256]{1,0:T(8,128)(2,1)S(1)}, u32[]{:S(2)}, u32[]{:S(2)}) collective-permute-start(bf16[256,256]{1,0:T(8,128)(2,1)S(1)} %get-tuple-element.42), channel_id=1, source_target_pairs={{0,8},{1,9},{2,10},{3,11},{4,12},{5,13},{6,14},{7,15},{8,16},{9,17... | collective-permute-start | bytes 393224 | tf_op jit(solution)/shard_map/ppermute | solution.py:31
  4.6 12.4 %collective-permute-start.2 = (bf16[256,256]{1,0:T(8,128)(2,1)S(1)}, bf16[256,256]{1,0:T(8,128)(2,1)S(1)}, u32[]{:S(2)}, u32[]{:S(2)}) collective-permute-start(bf16[256,256]{1,0:T(8,128)(2,1)S(1)} %get-tuple-element.42), channel_id=1, source_target_pairs={{0,6},{1,7},{2,8},{3,9},{4,10},{5,11},{6,12},{7,13},{8,14},{9,15},... | collective-permute-start | bytes 393224 | tf_op jit(solution)/shard_map/ppermute | solution.py:31
  9.2 12.8 %collective-permute-start.1 = (bf16[256,256]{1,0:T(8,128)(2,1)S(1)}, bf16[256,256]{1,0:T(8,128)(2,1)S(1)}, u32[]{:S(2)}, u32[]{:S(2)}) collective-permute-start(bf16[256,256]{1,0:T(8,128)(2,1)S(1)} %get-tuple-element.42), channel_id=1, source_target_pairs={{0,4},{1,5},{2,6},{3,7},{4,8},{5,9},{6,10},{7,11},{8,12},{9,13},{1... | collective-permute-start | bytes 393224 | tf_op jit(solution)/shard_map/ppermute | solution.py:31
  9.8 12.2 %collective-permute-start = (bf16[256,256]{1,0:T(8,128)(2,1)S(1)}, bf16[256,256]{1,0:T(8,128)(2,1)S(1)}, u32[]{:S(2)}, u32[]{:S(2)}) collective-permute-start(bf16[256,256]{1,0:T(8,128)(2,1)S(1)} %get-tuple-element.42), channel_id=1, source_target_pairs={{0,2},{1,3},{2,4},{3,5},{4,6},{5,7},{6,8},{7,9},{8,10},{9,11},{10,... | collective-permute-start | bytes 393224 | tf_op jit(solution)/shard_map/ppermute | solution.py:31
  16.9 5.2 %collective-permute-start.4 = (f32[256,128]{1,0:T(8,128)S(1)}, f32[256,128]{1,0:T(8,128)S(1)}, u32[]{:S(2)}, u32[]{:S(2)}) collective-permute-start(f32[256,128]{1,0:T(8,128)S(1)} %get-tuple-element.44.refs_0_), channel_id=1, source_target_pairs={{0,8},{1,9},{2,10},{3,11},{4,12},{5,13},{6,14},{7,15},{8,0},{9,1},... | collective-permute-start | bytes 393224 | tf_op jit(solution)/shard_map/ppermute | solution.py:43
  22.6 14.8 %collective-permute-start.5 = (bf16[512,256]{1,0:T(8,128)(2,1)S(1)}, bf16[512,256]{1,0:T(8,128)(2,1)S(1)}, u32[]{:S(2)}, u32[]{:S(2)}) collective-permute-start(bf16[512,256]{1,0:T(8,128)(2,1)S(1)} %get-tuple-element.45), channel_id=1, source_target_pairs={{0,1},{1,0},{2,3},{3,2},{4,5},{5,4},{6,7},{7,6},{8,9},{9,8},{10,11... | collective-permute-start | bytes 786440 | tf_op jit(solution)/shard_map/ppermute | solution.py:43
  24.2 7.3 %collective-permute-start.8 = (f32[256,128]{1,0:T(8,128)S(1)}, f32[256,128]{1,0:T(8,128)S(1)}, u32[]{:S(2)}, u32[]{:S(2)}) collective-permute-start(f32[256,128]{1,0:T(8,128)S(1)} %get-tuple-element.46.refs_4_), channel_id=1, source_target_pairs={{0,17},{1,16},{2,19},{3,18},{4,21},{5,20},{6,23},{7,22},{8,25},{9,... | collective-permute-start | bytes 393224 | tf_op jit(solution)/shard_map/ppermute | solution.py:43
  25.7 11.8 %collective-permute-start.7 = (f32[256,128]{1,0:T(8,128)S(1)}, f32[256,128]{1,0:T(8,128)S(1)}, u32[]{:S(2)}, u32[]{:S(2)}) collective-permute-start(f32[256,128]{1,0:T(8,128)S(1)} %get-tuple-element.46.refs_4_), channel_id=1, source_target_pairs={{0,1},{1,0},{2,3},{3,2},{4,5},{5,4},{6,7},{7,6},{8,9},{9,8},{10,11... | collective-permute-start | bytes 393224 | tf_op jit(solution)/shard_map/ppermute | solution.py:43
  27.2 10.3 %collective-permute-start.6 = (f32[256,128]{1,0:T(8,128)S(1)}, f32[256,128]{1,0:T(8,128)S(1)}, u32[]{:S(2)}, u32[]{:S(2)}) collective-permute-start(f32[256,128]{1,0:T(8,128)S(1)} %get-tuple-element.46.refs_4_), channel_id=1, source_target_pairs={{0,16},{1,17},{2,18},{3,19},{4,20},{5,21},{6,22},{7,23},{8,24},{9,... | collective-permute-start | bytes 393224 | tf_op jit(solution)/shard_map/ppermute | solution.py:43
  27.7 14.6 %collective-permute-start.9 = (bf16[512,256]{1,0:T(8,128)(2,1)S(1)}, bf16[512,256]{1,0:T(8,128)(2,1)S(1)}, u32[]{:S(2)}, u32[]{:S(2)}) collective-permute-start(bf16[512,256]{1,0:T(8,128)(2,1)S(1)} %get-tuple-element.48), channel_id=1, source_target_pairs={{0,1},{1,0},{2,3},{3,2},{4,5},{5,4},{6,7},{7,6},{8,9},{9,8},{10,11... | collective-permute-start | bytes 786440 | tf_op jit(solution)/shard_map/ppermute | solution.py:43
  38.5 14.6 %collective-permute-start.11 = (bf16[256,512]{1,0:T(8,128)(2,1)S(1)}, bf16[256,512]{1,0:T(8,128)(2,1)S(1)}, u32[]{:S(2)}, u32[]{:S(2)}) collective-permute-start(bf16[256,512]{1,0:T(8,128)(2,1)S(1)} %get-tuple-element.59), channel_id=1, source_target_pairs={{0,1},{1,0},{2,3},{3,2},{4,5},{5,4},{6,7},{7,6},{8,9},{9,8},{10,11... | collective-permute-start | bytes 786440 | tf_op jit(solution)/shard_map/ppermute | solution.py:43
  43.3 13.7 %collective-permute-start.10 = (bf16[256,512]{1,0:T(8,128)(2,1)S(1)}, bf16[256,512]{1,0:T(8,128)(2,1)S(1)}, u32[]{:S(2)}, u32[]{:S(2)}) collective-permute-start(bf16[256,512]{1,0:T(8,128)(2,1)S(1)} %get-tuple-element.53), channel_id=1, source_target_pairs={{0,1},{1,0},{2,3},{3,2},{4,5},{5,4},{6,7},{7,6},{8,9},{9,8},{10,11... | collective-permute-start | bytes 786440 | tf_op jit(solution)/shard_map/ppermute | solution.py:43
  47.9 5.2 %collective-permute-start.12 = (f32[256,128]{1,0:T(8,128)S(1)}, f32[256,128]{1,0:T(8,128)S(1)}, u32[]{:S(2)}, u32[]{:S(2)}) collective-permute-start(f32[256,128]{1,0:T(8,128)S(1)} %get-tuple-element.60.refs_0_), channel_id=1, source_target_pairs={{0,2},{1,3},{2,0},{3,1},{4,6},{5,7},{6,4},{7,5},{8,10},{9,11},{10,... | collective-permute-start | bytes 393224 | tf_op jit(solution)/shard_map/ppermute | solution.py:43
  53.7 19.0 %collective-permute-start.13 = (bf16[256,256]{1,0:T(8,128)(2,1)S(1)}, bf16[256,256]{1,0:T(8,128)(2,1)S(1)}, u32[]{:S(2)}, u32[]{:S(2)}) collective-permute-start(bf16[256,256]{1,0:T(8,128)(2,1)S(1)} %get-tuple-element.61), channel_id=1, source_target_pairs={{0,30},{1,31},{2,0},{3,1},{4,2},{5,3},{6,4},{7,5},{8,6},{9,7},{10,... | collective-permute-start | bytes 393224 | tf_op jit(solution)/shard_map/ppermute | solution.py:31
  56.2 16.5 %collective-permute-start.14 = (bf16[256,256]{1,0:T(8,128)(2,1)S(1)}, bf16[256,256]{1,0:T(8,128)(2,1)S(1)}, u32[]{:S(2)}, u32[]{:S(2)}) collective-permute-start(bf16[256,256]{1,0:T(8,128)(2,1)S(1)} %get-tuple-element.62), channel_id=1, source_target_pairs={{0,28},{1,29},{2,30},{3,31},{4,0},{5,1},{6,2},{7,3},{8,4},{9,5},{1... | collective-permute-start | bytes 393224 | tf_op jit(solution)/shard_map/ppermute | solution.py:31
  57.6 15.2 %collective-permute-start.15 = (bf16[256,256]{1,0:T(8,128)(2,1)S(1)}, bf16[256,256]{1,0:T(8,128)(2,1)S(1)}, u32[]{:S(2)}, u32[]{:S(2)}) collective-permute-start(bf16[256,256]{1,0:T(8,128)(2,1)S(1)} %get-tuple-element.63), channel_id=1, source_target_pairs={{0,26},{1,27},{2,28},{3,29},{4,30},{5,31},{6,0},{7,1},{8,2},{9,3},... | collective-permute-start | bytes 393224 | tf_op jit(solution)/shard_map/ppermute | solution.py:31
  64.2 8.5 %collective-permute-start.16 = (bf16[256,256]{1,0:T(8,128)(2,1)S(1)}, bf16[256,256]{1,0:T(8,128)(2,1)S(1)}, u32[]{:S(2)}, u32[]{:S(2)}) collective-permute-start(bf16[256,256]{1,0:T(8,128)(2,1)S(1)} %get-tuple-element.54.refs_9_), channel_id=1, source_target_pairs={{0,24},{1,25},{2,26},{3,27},{4,28},{5,29},{6,30},{7,31},{8,0},{9,1... | collective-permute-start | bytes 393224 | tf_op jit(solution)/shard_map/ppermute | solution.py:31
  64.2 8.5 %collective-permute-start.17 = (bf16[256,128]{1,0:T(8,128)(2,1)S(1)}, bf16[256,128]{1,0:T(8,128)(2,1)S(1)}, u32[]{:S(2)}, u32[]{:S(2)}) collective-permute-start(bf16[256,128]{1,0:T(8,128)(2,1)S(1)} %get-tuple-element.64.refs_4_), channel_id=1, source_target_pairs={{0,4},{1,5},{2,6},{3,7},{4,0},{5,1},{6,2},{7,3},{8,12},{9,13},{10,... | collective-permute-start | bytes 196616 | tf_op jit(solution)/shard_map/ppermute | solution.py:43
  (4 other events, 18.4 us)

commit v2 on v1

--- a/solution.py
+++ b/solution.py
@@ -48,7 +48,8 @@
     for axis in AXES:
         step = 1
         while step < lax.axis_size(axis):
-            rounds.append((axis, step))
+            if axis != AXES[-1] or step > 4:
+                rounds.append((axis, step))
             step *= 2
     return rounds
 
@@ -58,13 +59,16 @@
 
 
 def sink_kernel(
-    table_ref, key_ref, value_ref, query_ref, grad_ref, out_ref, lse_in, sink_key_ref, sink_value_ref,
-    turned_ref, row_ref, dquery_ref, sink_grad_ref, own_ref,
+    window_ref, live_ref, device_ref, key_ref, value_ref, query_ref, grad_ref, out_ref, lse_in, sink_key_ref, sink_value_ref,
+    table_ref, turned_ref, row_ref, dquery_ref, sink_grad_ref, own_ref,
     *, heads, width, scale,
 ):
     rows = query_ref.shape[0]
     sinks = sink_key_ref.shape[0]
     sink_grad_ref[...] = jnp.zeros_like(sink_grad_ref)
+    for head in range(heads):
+        table_ref[head] = window_ref[head]
+    table_ref[heads] = device_ref[0]
     own_ref[:, :width] = key_ref[...]
     own_ref[:, width:] = value_ref[...]
     row_ref[:heads, :] = lse_in[...] * LOG2E
@@ -82,7 +86,7 @@
         row_ref[pl.ds(heads + head, 1), :] = delta
         probs = jnp.exp2(dot(key, query_t) * (scale * LOG2E) - row_ref[pl.ds(head, 1), :])
         at = lax.broadcasted_iota(jnp.int32, (sinks, rows), 0)
-        probs = jnp.where(at < table_ref[heads + head], probs, 0.0)
+        probs = jnp.where(at < live_ref[head], probs, 0.0)
         dscores = (probs * (dot(value, grad_t) - delta)).astype(LOW)
         sink_grad_ref[:width, :] += dot(query_t, dscores, NT) * scale
         sink_grad_ref[width:, :] += dot(grad_t, probs.astype(LOW), NT)
@@ -103,35 +107,47 @@
     return total
 
 
-def mark_kernel(window_ref, live_ref, device_ref, block_ref, table_ref, same_ref):
-    heads = window_ref.shape[0]
-    for head in range(heads):
-        table_ref[head] = window_ref[head]
-        table_ref[heads + head] = live_ref[head]
-    table_ref[2 * heads] = device_ref[0]
-
-
-def fold_kernel(device_ref, first_ref, second_ref, other_ref, *refs, rows, terms, odd_only):
-    outs = refs[terms:]
-    outs[0][...] = (first_ref[...] + other_ref[:, :rows].astype(jnp.float32)).astype(LOW)
-    other = other_ref[:, rows:].astype(jnp.float32)
-    if odd_only:
-        odd = jnp.full(other.shape, device_ref[device_ref.shape[0] - 1] & 1, jnp.int32) == 1
+def mark_kernel(block_ref, same_ref):
+    pass
+
+
+def fold_kernel(table_ref, first_ref, second_ref, other_ref, *refs, rows, near):
+    if near:
+        mine_ref, first_out, second_out, sink_out = refs
+        sinks = (mine_ref.shape[1] - 2 * rows) // 2
+        sink = None
+        for ref in (mine_ref, other_ref):
+            high, low = ref[:, 2 * rows : 2 * rows + sinks], ref[:, 2 * rows + sinks :]
+            whole = high.astype(jnp.float32) + low.astype(jnp.float32)
+            sink = whole if sink is None else sink + whole
+        sink = sink.astype(LOW)
+        sink_out[...] = sink
+        second_out[:, rows:] = sink
+    else:
+        sink_ref, first_out, second_out = refs
+        sink = sink_ref[...]
+    first_out[:, :rows] = (first_ref[...] + other_ref[:, :rows].astype(jnp.float32)).astype(LOW)
+    first_out[:, rows:] = sink
+    other = other_ref[:, rows : 2 * rows].astype(jnp.float32)
+    if not near:
+        odd = jnp.full(other.shape, table_ref[table_ref.shape[0] - 1] & 1, jnp.int32) == 1
         other = jnp.where(odd, other, 0.0)
-    outs[1][...] = (second_ref[...] + other).astype(LOW)
-    if terms:
-        outs[2][...] = sum_of(refs[:terms]).astype(LOW)
-
-
-def send_kernel(device_ref, own_ref, two_ref, four_ref, six_ref, eight_ref, *refs):
-    near_ref, far_ref, sum_ref = refs[-3:]
-    rows = own_ref.shape[0]
-    odd = jnp.full(own_ref.shape, device_ref[device_ref.shape[0] - 1] & 1, jnp.int32) == 1
+    second_out[:, :rows] = (second_ref[...] + other).astype(LOW)
+
+
+def near_kernel(two_ref, four_ref, *refs):
+    near_ref, sum_ref = refs[-2:]
+    rows = two_ref.shape[0]
     near_ref[:rows, :] = two_ref[...]
     near_ref[rows:, :] = four_ref[...]
+    sum_ref[...] = sum_of(refs[:-2])
+
+
+def far_kernel(table_ref, own_ref, six_ref, eight_ref, after_ref, far_ref):
+    rows = own_ref.shape[0]
+    odd = jnp.full(own_ref.shape, table_ref[table_ref.shape[0] - 1] & 1, jnp.int32) == 1
     far_ref[:rows, :] = six_ref[...]
     far_ref[rows:, :] = jnp.where(odd, eight_ref[...], own_ref[...])
-    sum_ref[...] = sum_of(refs[:-3])
 
 
 def local(distances, device):
@@ -151,7 +167,7 @@
 
     pairs, sink_count, back_count, joined, last = layout
     table_ref, turned_ref, row_ref = take(3)
-    device = table_ref[2 * heads]
+    device = table_ref[heads]
     distances = local([distance for pair in pairs for distance in pair], device)
     pair_refs = take(len(pairs))
     sink_refs = take(sink_count)
@@ -160,7 +176,6 @@
     take(1)
     dquery_ref = take(1)[0]
     out_refs = take(1 if joined else len(distances))
-    sink_out_refs = take(1 if sink_count else 0)
     items_ref, pair_ref, key_t_ref, sum_ref = take(4)
     low_refs = take(4)
     total_ref, total_sems = take(2) if last else (None, None)
@@ -267,7 +282,11 @@
             else:
                 out_refs[slot][strip, :] = grad.astype(out_refs[slot].dtype)
     if sink_count:
-        sink_out_refs[0][...] = sum_of(sink_refs)
+        total = sum_of(sink_refs)
+        high = total.astype(LOW)
+        sinks = total.shape[1]
+        out_refs[0][:, len(distances) * rows : len(distances) * rows + sinks] = high
+        out_refs[0][:, len(distances) * rows + sinks :] = (total - high.astype(jnp.float32)).astype(LOW)
     if last:
         for step in range(heads // UNROLL):
             total_copy(step).wait()
@@ -282,9 +301,8 @@
     count = len(distances)
     shape = jax.ShapeDtypeStruct
     outs = [shape((rows, wide) if last else (wide, rows), jnp.float32)]
-    outs += [shape((2 * width, count * rows), kind)] if joined else [shape((2 * width, rows), kind)] * count
-    if sinks:
-        outs.append(shape(sinks[0].shape, jnp.float32))
+    extra = 2 * sinks[0].shape[1] if sinks else 0
+    outs += [shape((2 * width, count * rows + extra), kind)] if joined else [shape((2 * width, rows), kind)] * count
     arrays = [turned, row_terms, *pair_arrays, *sinks, *backs, *parts, after]
     layout = (pairs, len(sinks), len(backs), joined, last)
     return pl.pallas_call(
@@ -310,15 +328,21 @@
     )(table, *arrays)
 
 
-def join_kernel(device_ref, own_ref, other_ref, *refs, backs, width):
-    key_ref, value_ref, sink_key_ref, sink_value_ref = refs[-4:]
+def join_kernel(
+    table_ref, own_ref, other_ref, sink_ref, two_ref, four_ref, six_ref, eight_ref,
+    key_ref, value_ref, sink_key_ref, sink_value_ref, *, width,
+):
     rows = own_ref.shape[1]
-    odd = jnp.full(own_ref.shape, device_ref[device_ref.shape[0] - 1] & 1, jnp.int32) == 1
+    odd = jnp.full(own_ref.shape, table_ref[table_ref.shape[0] - 1] & 1, jnp.int32) == 1
     total = own_ref[...] + jnp.where(odd, 0.0, other_ref[:, rows:].astype(jnp.float32))
-    turned = (total + sum_of(refs[:backs])).T
+    for ref in (two_ref, four_ref, six_ref, eight_ref):
+        total = total + ref[:, :rows].astype(jnp.float32)
+    turned = total.T
     key_ref[...] = turned[:, :width]
     value_ref[...] = turned[:, width:]
-    turned = sum_of(refs[backs:-4]).T
+    sums = [sink_ref[...]] + [ref[:, rows:] for ref in (two_ref, four_ref, six_ref)]
+    sums = [term.astype(jnp.float32) for term in sums]
+    turned = ((sums[0] + sums[2]) + (sums[1] + sums[3])).T
     sink_key_ref[...] = turned[:, :width]
     sink_value_ref[...] = turned[:, width:]
 
@@ -334,105 +358,111 @@
     shape = jax.ShapeDtypeStruct
     device = lax.axis_index(AXES).astype(jnp.int32).reshape(1)
     own_pair = jnp.concatenate([keys, values], axis=1)
-    table, own_pair = pl.pallas_call(
+    own_pair = pl.pallas_call(
         mark_kernel,
-        out_shape=(shape((2 * heads + 1,), jnp.int32), shape(own_pair.shape, LOW)),
-        in_specs=[SMEM] * 3 + [ANY],
-        out_specs=(SMEM, ANY),
-        input_output_aliases={3: 1},
+        out_shape=shape(own_pair.shape, LOW),
+        in_specs=[ANY],
+        out_specs=ANY,
+        input_output_aliases={0: 0},
         compiler_params=pltpu.CompilerParams(vmem_limit_bytes=1024 * 1024),
         cost_estimate=pl.CostEstimate(flops=2 * 10**10, bytes_accessed=1, transcendentals=0),
         name="mark",
-    )(window_len, sink_live, device, own_pair)
-    even = {d: rotated(own_pair, d) for d in (2, 4, 6, 8)}
-
-    turned, row_terms, dquery, sink_grad, own_held = pl.pallas_call(
+    )(own_pair)
+    even = {d: rotated(own_pair, d) for d in (8, 6, 4, 2)}
+
+    table, turned, row_terms, dquery, sink_grad, own_held = pl.pallas_call(
         functools.partial(sink_kernel, heads=heads, width=width, scale=width**-0.5),
         out_shape=(
+            shape((heads + 1,), jnp.int32),
             shape((2 * wide, rows), LOW),
             shape((2 * heads, rows), jnp.float32),
             shape((wide, rows), jnp.float32),
             shape((2 * width, sinks), jnp.float32),
             shape((rows, 2 * width), LOW),
         ),
-        in_specs=[SMEM] + [VMEM] * 8,
-        out_specs=(VMEM,) * 5,
+        in_specs=[SMEM] * 3 + [VMEM] * 8,
+        out_specs=(SMEM,) + (VMEM,) * 5,
         compiler_params=pltpu.CompilerParams(vmem_limit_bytes=VMEM_BYTES),
         cost_estimate=pl.CostEstimate(flops=10**10, bytes_accessed=10**6, transcendentals=0),
         name="sink_keys_part",
-    )(table, keys, values, queries, out_grad, outputs, lse, sink_keys, sink_values)
+    )(window_len, sink_live, device, keys, values, queries, out_grad, outputs, lse, sink_keys, sink_values)
 
     rounds = exchange_rounds()
 
-    def sink_terms(count):
-        moves = [()]
-        for _ in range(min(count, len(rounds))):
-            here = rounds.pop(0)
-            moves = moves + [move + (here,) for move in moves]
-        return [sink_grad] + [swapped(sink_grad, move) for move in moves[1:]]
-
-    near, far, sink_grad = pl.pallas_call(
-        send_kernel,
-        out_shape=(shape((2 * rows, 2 * width), LOW),) * 2 + (shape(sink_grad.shape, jnp.float32),),
-        in_specs=[SMEM] + [VMEM] * (7 if rounds else 6),
-        out_specs=(VMEM,) * 3,
+    def sink_terms():
+        return [sink_grad] + ([swapped(sink_grad, (rounds.pop(0),))] if rounds else [])
+
+    terms = sink_terms()
+    near, sink_grad = pl.pallas_call(
+        near_kernel,
+        out_shape=(shape((2 * rows, 2 * width), LOW), shape(sink_grad.shape, jnp.float32)),
+        in_specs=[VMEM] * (2 + len(terms)),
+        out_specs=(VMEM,) * 2,
         compiler_params=pltpu.CompilerParams(vmem_limit_bytes=VMEM_BYTES),
-        name="send_blocks",
-    )(table, own_held, even[2], even[4], even[6], even[8], *sink_terms(1))
+        name="near_blocks",
+    )(even[2], even[4], *terms)
     partner = ((AXES[-1], 1),)
-    near_odd, far_odd = swapped(near, partner), swapped(far, partner)
+    near_odd = swapped(near, partner)
+    while len(rounds) > 1:
+        sink_grad = sum(sink_terms())
+    terms = sink_terms()
 
     shared = (table, turned, row_terms)
     parts = [dquery]
-    sums = sink_terms(2)
     full = jnp.float32
     near_pair, far_pair = ((1, 3), (3, 5)), ((5, 7), (7, 1))
-    part, grad_2, grad_4 = block_call([(2,), (4,)], [even[2], even[4]], shared, dquery, kind=full)
+    part, grad_2, grad_4 = block_call([(2,), (4,)], [even[2], even[4]], shared, near, kind=full)
     parts.append(part)
 
-    part, odd, sink_grad = block_call([near_pair], [near_odd], shared, part, sinks=sums, joined=True)
+    far = pl.pallas_call(
+        far_kernel,
+        out_shape=shape((2 * rows, 2 * width), LOW),
+        in_specs=[SMEM] + [VMEM] * 3 + [ANY],
+        out_specs=VMEM,
+        compiler_params=pltpu.CompilerParams(vmem_limit_bytes=VMEM_BYTES),
+        name="far_blocks",
+    )(table, own_held, even[6], even[8], part)
+    far_odd = swapped(far, partner)
+
+    part, near_mine = block_call([near_pair], [near_odd], shared, far, sinks=terms, joined=True)
     parts.append(part)
-    sums = sink_terms(1)
-    near_other = swapped(odd, partner)
-
-    part, odd = block_call([far_pair], [far_odd], shared, part, joined=True)
+    near_other = swapped(near_mine, partner)
+
+    part, far_mine = block_call([far_pair], [far_odd], shared, part, joined=True)
     parts.append(part)
-    far_other = swapped(odd, partner)
+    far_other = swapped(far_mine, partner)
 
     part, grad_6, grad_8 = block_call([(6,), (8,)], [even[6], even[8]], shared, part, kind=full)
     parts.append(part)
 
-    def fold(first, second, other, terms=(), odd_only=False):
-        outs = [shape(first.shape, LOW)] * 2 + ([shape(sink_grad.shape, LOW)] if terms else [])
+    def fold(first, second, other, extra, near):
+        outs = [shape((2 * width, rows + sinks), LOW), shape((2 * width, rows + (sinks if near else 0)), LOW)]
+        outs += [shape((2 * width, sinks), LOW)] if near else []
         return pl.pallas_call(
-            functools.partial(fold_kernel, rows=rows, terms=len(terms), odd_only=odd_only),
+            functools.partial(fold_kernel, rows=rows, near=near),
             out_shape=outs,
-            in_specs=[SMEM] + [VMEM] * (3 + len(terms)),
+            in_specs=[SMEM] + [VMEM] * 4,
             out_specs=[VMEM] * len(outs),
             compiler_params=pltpu.CompilerParams(vmem_limit_bytes=VMEM_BYTES),
             name="fold",
-        )(table, first, second, other, *terms)
-
-    grad_2, grad_4, sink_grad = fold(grad_2, grad_4, near_other, sums)
-    sums = sink_terms(1)
+        )(table, first, second, other, extra)
+
+    grad_2, grad_4, sink_low = fold(grad_2, grad_4, near_other, near_mine, True)
     backs = [rotated(grad_2, -2), rotated(grad_4, -4)]
-    grad_6, grad_8 = fold(grad_6, grad_8, far_other, odd_only=True)
+    grad_6, grad_8 = fold(grad_6, grad_8, far_other, sink_low, False)
     backs += [rotated(grad_6, -6), rotated(grad_8, -8)]
     dquery, own_grad = block_call(
         [(0,)], [own_held], shared, grad_8, parts=parts, kind=full, last=True,
         groups=((2, 4), near_pair, far_pair, (6, 8)),
     )
-    while rounds:
-        sink_grad = sum(sums)
-        sums = sink_terms(1)
     key_grad, value_grad, sink_key_grad, sink_value_grad = pl.pallas_call(
-        functools.partial(join_kernel, backs=len(backs), width=width),
+        functools.partial(join_kernel, width=width),
         out_shape=(shape((rows, width), jnp.float32),) * 2 + (shape((sinks, width), jnp.float32),) * 2,
-        in_specs=[SMEM] + [VMEM] * (2 + len(backs) + len(sums)),
+        in_specs=[SMEM] + [VMEM] * 7,
         out_specs=(VMEM,) * 4,
         compiler_params=pltpu.CompilerParams(vmem_limit_bytes=VMEM_BYTES),
         name="join",
-    )(table, own_grad, far_other, *backs, *sums)
+    )(table, own_grad, far_other, sink_low, *backs)
     return (dquery, key_grad, value_grad, sink_key_grad, sink_value_grad)
 
 

time: 74.9 us -> 67.2 us (0.90)
  waiting for transfers between devices: 20.4 us -> 11.6 us
  starting transfers between devices: 31.4 us -> 33.4 us
  Pallas kernels: 19.3 us -> 18.5 us
    ppermute x10 -> x6, waiting for transfers between devices: 15.4 us -> 4.72 us  [swapped(): return lax.ppermute(block, AXES, route)]
    ppermute x8, starting transfers between devices: 17.2 us -> 22.9 us  [rotated(): lax.ppermute(block, AXES, [(i, (i + distance) % count) for i in range(cou...]
    ppermute x10 -> x6, starting transfers between devices: 14.2 us -> 10.5 us  [swapped(): return lax.ppermute(block, AXES, route)]
    ppermute x8, waiting for transfers between devices: 5.08 us -> 6.92 us  [rotated(): lax.ppermute(block, AXES, [(i, (i + distance) % count) for i in range(cou...]
    pallas_call x5 -> x6, Pallas kernels: 4.35 us -> 3.23 us  [the longest x1 1.4 us: on_device(): pl.pallas_call(functools.partial(join_kernel, width=width), out_shape=(sh...]
  transfers between devices with their start and end apart: 18 -> 14, of which waited for: 6 -> 6; matrix products, arithmetic and copies ran while one was open for 0% -> 0% of each run, Pallas kernels for 22% -> 26%
where the time goes in v2:
time: 67.2 us; the launch traced here: 66.5 us
  starting transfers between devices  33.4 us (50%)
  Pallas kernels  18.5 us (28%)
  waiting for transfers between devices  11.6 us (17%)
  local copies, waits for them, and re-layouts  1.28 us (2%)
  other arithmetic  0.89 us (1%)
  between operations  0.89 us (1%)
    ppermute x8, starting transfers between devices, rotated(): lax.ppermute(block, AXES, [(i, (i + distance) % count) for i in range(cou...  22.9 us
    ppermute x6, starting transfers between devices, swapped(): return lax.ppermute(block, AXES, route)  10.5 us
    pallas_call x5, Pallas kernels, block_call(): pl.pallas_call(functools.partial(block_kernel, layout=layout, groups=grou...  9.49 us
    ppermute x8, waiting for transfers between devices, rotated(): lax.ppermute(block, AXES, [(i, (i + distance) % count) for i in range(cou...  6.92 us
    pallas_call x1, Pallas kernels, on_device(): pl.pallas_call(functools.partial(sink_kernel, heads=heads, width=width, s...  5.74 us
    ppermute x6, waiting for transfers between devices, swapped(): return lax.ppermute(block, AXES, route)  4.72 us
    pallas_call x1, Pallas kernels, on_device(): pl.pallas_call(functools.partial(join_kernel, width=width), out_shape=(sh...  1.4 us
  transfers between devices with their start and end apart: 14, of which 6 were waited for; matrix products, arithmetic and copies ran while one was open for 0% of the time, Pallas kernels for 26%

profile of v2, /device:TPU:0, one launch (start us, length us, event | category | flops | bytes accessed | tf_op | source)
XLA Modules:
  0.0 66.5 jit_solution(17145974897812593815)
XLA Ops:
  0.6 0.9 %pad_maximum_fusion.block_ref = bf16[256,256]{1,0:T(8,128)(2,1)S(1)} fusion(bf16[256,128]{1,0:T(8,128)(2,1)} %value_ref.1, bf16[256,128]{1,0:T(8,128)(2,1)} %key_ref.1), kind=kLoop, calls=%fused_computation | loop fusion | flops 262144 | bytes 262144 | tf_op jit(solution)/shard_map/concatenate | solution.py:360
  1.6 4.1 %collective-permute-start.1 = (bf16[256,256]{1,0:T(8,128)(2,1)S(1)}, bf16[256,256]{1,0:T(8,128)(2,1)S(1)}, u32[]{:S(2)}, u32[]{:S(2)}) collective-permute-start(bf16[256,256]{1,0:T(8,128)(2,1)S(1)} %mark.1), channel_id=1, source_target_pairs={{0,4},{1,5},{2,6},{3,7},{4,8},{5,9},{6,10},{7,11},{8,12},{9,13},{1... | collective-permute-start | bytes 393224 | tf_op jit(solution)/shard_map/ppermute | solution.py:31
  5.7 1.6 %collective-permute-start = (bf16[256,256]{1,0:T(8,128)(2,1)S(1)}, bf16[256,256]{1,0:T(8,128)(2,1)S(1)}, u32[]{:S(2)}, u32[]{:S(2)}) collective-permute-start(bf16[256,256]{1,0:T(8,128)(2,1)S(1)} %mark.1), channel_id=1, source_target_pairs={{0,2},{1,3},{2,4},{3,5},{4,6},{5,7},{6,8},{7,9},{8,10},{9,11},{10,... | collective-permute-start | bytes 393224 | tf_op jit(solution)/shard_map/ppermute | solution.py:31
  7.4 1.2 %copy-done.4 = bf16[256,2048]{1,0:T(8,128)(2,1)S(1)} copy-done((bf16[256,2048]{1,0:T(8,128)(2,1)S(1)}, bf16[256,2048]{1,0:T(8,128)(2,1)}, u32[]{:S(2)}) %copy-start.4) | copy-done | bytes 1048600
  8.6 5.7 %sink_keys_part.1 = (s32[17]{0:T(128)S(1)}, bf16[4096,256]{1,0:T(8,128)(2,1)S(1)}, f32[32,256]{1,0:T(8,128)S(1)}, f32[2048,256]{1,0:T(8,128)S(1)}, f32[256,128]{1,0:T(8,128)S(1)}, /*index=5*/bf16[256,256]{1,0:T(8,128)(2,1)S(1)}) custom-call(s32[16]{0:T(128)S(1)} %copy-done.8, s32[16]{0:T(128)S(1)} %copy-done.9, s32[1]{0:T(128)} %bitcast.device_ref, ...), custom_call_target="tpu_custom_call" | custom-call | flops 10000000000 | bytes 1000000 | tf_op jit(solution)/shard_map/sink_keys_part/pallas_call | solution.py:373
  14.9 2.8 %collective-permute-start.5 = (bf16[256,256]{1,0:T(8,128)(2,1)S(1)}, bf16[256,256]{1,0:T(8,128)(2,1)S(1)}, u32[]{:S(2)}, u32[]{:S(2)}) collective-permute-start(bf16[256,256]{1,0:T(8,128)(2,1)S(1)} %mark.1), channel_id=1, source_target_pairs={{0,6},{1,7},{2,8},{3,9},{4,10},{5,11},{6,12},{7,13},{8,14},{9,15},... | collective-permute-start | bytes 393224 | tf_op jit(solution)/shard_map/ppermute | solution.py:31
  17.8 0.6 collective-permute-start.4
  18.4 1.5 %collective-permute-start.3 = (bf16[512,256]{1,0:T(8,128)(2,1)S(1)}, bf16[512,256]{1,0:T(8,128)(2,1)S(1)}, u32[]{:S(2)}, u32[]{:S(2)}) collective-permute-start(bf16[512,256]{1,0:T(8,128)(2,1)S(1)} %get-tuple-element.40.refs_5_), channel_id=1, source_target_pairs={{0,1},{1,0},{2,3},{3,2},{4,5},{5,4},{6,7},{7,6},{8,9},{9,8},{10,11... | collective-permute-start | bytes 786440 | tf_op jit(solution)/shard_map/ppermute | solution.py:43
  20.0 1.0 %blocks_2_4.1 = (f32[2048,256]{1,0:T(8,128)S(1)}, f32[256,256]{1,0:T(8,128)S(1)}, f32[256,256]{1,0:T(8,128)S(1)}) custom-call(s32[17]{0:T(128)S(1)} %get-tuple-element.34.refs_0_.table_ref, bf16[4096,256]{1,0:T(8,128)(2,1)S(1)} %get-tuple-element.35.refs_1_, f32[32,256]{1,0:T(8,128)S(1)} %get-tuple-element.36.refs_2_, ...), custom_call_target="tpu_custom_call" | custom-call | flops 2684354560 | bytes 1048576 | tf_op jit(solution)/shard_map/blocks_2_4/pallas_call | solution.py:308
  21.9 1.6 %collective-permute-start.7 = (bf16[512,256]{1,0:T(8,128)(2,1)S(1)}, bf16[512,256]{1,0:T(8,128)(2,1)S(1)}, u32[]{:S(2)}, u32[]{:S(2)}) collective-permute-start(bf16[512,256]{1,0:T(8,128)(2,1)S(1)} %far_blocks.1.refs_6_), channel_id=1, source_target_pairs={{0,1},{1,0},{2,3},{3,2},{4,5},{5,4},{6,7},{7,6},{8,9},{9,8},{10,11... | collective-permute-start | bytes 786440 | tf_op jit(solution)/shard_map/ppermute | solution.py:43
  23.9 3.7 %collective-permute-done.3.refs_3_ = bf16[512,256]{1,0:T(8,128)(2,1)S(1)} collective-permute-done((bf16[512,256]{1,0:T(8,128)(2,1)S(1)}, bf16[512,256]{1,0:T(8,128)(2,1)S(1)}, u32[]{:S(2)}, u32[]{:S(2)}) %collective-permute-start.3) | collective-permute-done | bytes 262176 | tf_op jit(solution)/shard_map/ppermute | solution.py:43
  27.6 1.0 %blocks_1_3.1 = (f32[2048,256]{1,0:T(8,128)S(1)}, bf16[256,768]{1,0:T(8,128)(2,1)S(1)}) custom-call(s32[17]{0:T(128)S(1)} %get-tuple-element.34.refs_0_.table_ref, bf16[4096,256]{1,0:T(8,128)(2,1)S(1)} %get-tuple-element.35.refs_1_, f32[32,256]{1,0:T(8,128)S(1)} %get-tuple-element.36.refs_2_, bf16[512,256]{1,0:T(8,128)(2,1)S(1)} %collective-permute-done.3.refs_3_, ...), custom_call_target="tpu_custom_call" | custom-call | flops 2684354560 | bytes 1048576 | tf_op jit(solution)/shard_map/blocks_1_3/pallas_call | solution.py:308
  28.6 1.6 %collective-permute-start.9 = (bf16[256,768]{1,0:T(8,128)(2,1)S(1)}, bf16[256,768]{1,0:T(8,128)(2,1)S(1)}, u32[]{:S(2)}, u32[]{:S(2)}) collective-permute-start(bf16[256,768]{1,0:T(8,128)(2,1)S(1)} %get-tuple-element.51.refs_0_), channel_id=1, source_target_pairs={{0,1},{1,0},{2,3},{3,2},{4,5},{5,4},{6,7},{7,6},{8,9},{9,8},{10,11... | collective-permute-start | bytes 1179656 | tf_op jit(solution)/shard_map/ppermute | solution.py:43
  30.4 1.0 %blocks_5_7.1 = (f32[2048,256]{1,0:T(8,128)S(1)}, bf16[256,512]{1,0:T(8,128)(2,1)S(1)}) custom-call(s32[17]{0:T(128)S(1)} %get-tuple-element.34.refs_0_.table_ref, bf16[4096,256]{1,0:T(8,128)(2,1)S(1)} %get-tuple-element.35.refs_1_, f32[32,256]{1,0:T(8,128)S(1)} %get-tuple-element.36.refs_2_, bf16[512,256]{1,0:T(8,128)(2,1)S(1)} %collective-permute-done.7.refs_3_, ...), custom_call_target="tpu_custom_call" | custom-call | flops 2684354560 | bytes 1048576 | tf_op jit(solution)/shard_map/blocks_5_7/pallas_call | solution.py:308
  31.4 5.1 %collective-permute-start.8 = (bf16[256,512]{1,0:T(8,128)(2,1)S(1)}, bf16[256,512]{1,0:T(8,128)(2,1)S(1)}, u32[]{:S(2)}, u32[]{:S(2)}) collective-permute-start(bf16[256,512]{1,0:T(8,128)(2,1)S(1)} %get-tuple-element.48), channel_id=1, source_target_pairs={{0,1},{1,0},{2,3},{3,2},{4,5},{5,4},{6,7},{7,6},{8,9},{9,8},{10,11... | collective-permute-start | bytes 786440 | tf_op jit(solution)/shard_map/ppermute | solution.py:43
  36.5 1.0 %blocks_6_8.1 = (f32[2048,256]{1,0:T(8,128)S(1)}, f32[256,256]{1,0:T(8,128)S(1)}, f32[256,256]{1,0:T(8,128)S(1)}) custom-call(s32[17]{0:T(128)S(1)} %get-tuple-element.34.refs_0_.table_ref, bf16[4096,256]{1,0:T(8,128)(2,1)S(1)} %get-tuple-element.35.refs_1_, f32[32,256]{1,0:T(8,128)S(1)} %get-tuple-element.36.refs_2_, ...), custom_call_target="tpu_custom_call" | custom-call | flops 2684354560 | bytes 1048576 | tf_op jit(solution)/shard_map/blocks_6_8/pallas_call | solution.py:308
  37.9 0.6 fold.2
  38.6 7.9 %collective-permute-start.10 = (bf16[256,384]{1,0:T(8,128)(2,1)S(1)}, bf16[256,384]{1,0:T(8,128)(2,1)S(1)}, u32[]{:S(2)}, u32[]{:S(2)}) collective-permute-start(bf16[256,384]{1,0:T(8,128)(2,1)S(1)} %get-tuple-element.56), channel_id=1, source_target_pairs={{0,30},{1,31},{2,0},{3,1},{4,2},{5,3},{6,4},{7,5},{8,6},{9,7},{10,... | collective-permute-start | bytes 589832 | tf_op jit(solution)/shard_map/ppermute | solution.py:31
  46.6 0.6 fold.3
  47.2 3.9 %collective-permute-start.12 = (bf16[256,384]{1,0:T(8,128)(2,1)S(1)}, bf16[256,384]{1,0:T(8,128)(2,1)S(1)}, u32[]{:S(2)}, u32[]{:S(2)}) collective-permute-start(bf16[256,384]{1,0:T(8,128)(2,1)S(1)} %get-tuple-element.58), channel_id=1, source_target_pairs={{0,26},{1,27},{2,28},{3,29},{4,30},{5,31},{6,0},{7,1},{8,2},{9,3},... | collective-permute-start | bytes 589832 | tf_op jit(solution)/shard_map/ppermute | solution.py:31
  51.0 2.1 %collective-permute-start.13 = (bf16[256,256]{1,0:T(8,128)(2,1)S(1)}, bf16[256,256]{1,0:T(8,128)(2,1)S(1)}, u32[]{:S(2)}, u32[]{:S(2)}) collective-permute-start(bf16[256,256]{1,0:T(8,128)(2,1)S(1)} %get-tuple-element.53.refs_9_), channel_id=1, source_target_pairs={{0,24},{1,25},{2,26},{3,27},{4,28},{5,29},{6,30},{7,31},{8,0},{9,1... | collective-permute-start | bytes 393224 | tf_op jit(solution)/shard_map/ppermute | solution.py:31
  53.1 5.4 %blocks_0.1 = (f32[256,2048]{1,0:T(8,128)}, f32[256,256]{1,0:T(8,128)S(1)}) custom-call(s32[17]{0:T(128)S(1)} %get-tuple-element.34.refs_0_.table_ref, bf16[4096,256]{1,0:T(8,128)(2,1)S(1)} %get-tuple-element.35.refs_1_, f32[32,256]{1,0:T(8,128)S(1)} %get-tuple-element.36.refs_2_, bf16[256,256]{1,0:T(8,128)(2,1)S(1)} %get-tuple-element.37.own_ref.refs_3_, ...), custom_call_target="tpu_custom_call" | custom-call | flops 1342177280 | bytes 1048576 | tf_op jit(solution)/shard_map/blocks_0/pallas_call | solution.py:308
  58.5 6.6 %collective-permute-done.11.four_ref = bf16[256,384]{1,0:T(8,128)(2,1)S(1)} collective-permute-done((bf16[256,384]{1,0:T(8,128)(2,1)S(1)}, bf16[256,384]{1,0:T(8,128)(2,1)S(1)}, u32[]{:S(2)}, u32[]{:S(2)}) %collective-permute-start.11) | collective-permute-done | bytes 196640 | tf_op jit(solution)/shard_map/ppermute | solution.py:31
  65.1 1.4 %join.1 = (f32[256,128]{1,0:T(8,128)}, f32[256,128]{1,0:T(8,128)}, f32[128,128]{1,0:T(8,128)}, f32[128,128]{1,0:T(8,128)}) custom-call(s32[17]{0:T(128)S(1)} %get-tuple-element.34.refs_0_.table_ref, f32[256,256]{1,0:T(8,128)S(1)} %get-tuple-element.55.own_ref, bf16[256,512]{1,0:T(8,128)(2,1)S(1)} %collective-permute-done.8.other_ref, ...), custom_call_target="tpu_custom_call" | custom-call | tf_op jit(solution)/shard_map/join/pallas_call | solution.py:458
  (37 shorter events, 2.6 us)
Async XLA Ops:
  1.5 5.8 %copy-start = (bf16[256,128]{1,0:T(8,128)(2,1)S(1)}, bf16[256,128]{1,0:T(8,128)(2,1)}, u32[]{:S(2)}) copy-start(bf16[256,128]{1,0:T(8,128)(2,1)} %key_ref.1) | copy-start | bytes 196612
  1.5 5.8 %copy-start.1 = (bf16[256,128]{1,0:T(8,128)(2,1)S(1)}, bf16[256,128]{1,0:T(8,128)(2,1)}, u32[]{:S(2)}) copy-start(bf16[256,128]{1,0:T(8,128)(2,1)} %value_ref.1) | copy-start | bytes 196612
  1.5 5.8 %copy-start.2 = (bf16[256,2048]{1,0:T(8,128)(2,1)S(1)}, bf16[256,2048]{1,0:T(8,128)(2,1)}, u32[]{:S(2)}) copy-start(bf16[256,2048]{1,0:T(8,128)(2,1)} %query_ref.1) | copy-start | bytes 3145732
  1.6 5.8 %copy-start.3 = (bf16[256,2048]{1,0:T(8,128)(2,1)S(1)}, bf16[256,2048]{1,0:T(8,128)(2,1)}, u32[]{:S(2)}) copy-start(bf16[256,2048]{1,0:T(8,128)(2,1)} %grad_ref.1) | copy-start | bytes 3145732
  1.6 5.8 %copy-start.5 = (bf16[128,128]{1,0:T(8,128)(2,1)S(1)}, bf16[128,128]{1,0:T(8,128)(2,1)}, u32[]{:S(2)}) copy-start(bf16[128,128]{1,0:T(8,128)(2,1)} %sink_key_ref.1) | copy-start | bytes 98308
  1.6 5.8 %copy-start.6 = (bf16[128,128]{1,0:T(8,128)(2,1)S(1)}, bf16[128,128]{1,0:T(8,128)(2,1)}, u32[]{:S(2)}) copy-start(bf16[128,128]{1,0:T(8,128)(2,1)} %sink_value_ref.1) | copy-start | bytes 98308
  1.6 5.8 %copy-start.7 = (f32[16,256]{1,0:T(8,128)S(1)}, f32[16,256]{1,0:T(8,128)}, u32[]{:S(2)}) copy-start(f32[16,256]{1,0:T(8,128)} %lse_in.1) | copy-start | bytes 49156
  1.6 5.8 %copy-start.8 = (s32[16]{0:T(128)S(1)}, s32[16]{0:T(128)}, u32[]{:S(2)}) copy-start(s32[16]{0:T(128)} %window_ref.1) | copy-start | bytes 196
  1.6 5.8 %copy-start.9 = (s32[16]{0:T(128)S(1)}, s32[16]{0:T(128)}, u32[]{:S(2)}) copy-start(s32[16]{0:T(128)} %live_ref.1) | copy-start | bytes 196
  1.6 16.1 %collective-permute-start.1 = (bf16[256,256]{1,0:T(8,128)(2,1)S(1)}, bf16[256,256]{1,0:T(8,128)(2,1)S(1)}, u32[]{:S(2)}, u32[]{:S(2)}) collective-permute-start(bf16[256,256]{1,0:T(8,128)(2,1)S(1)} %mark.1), channel_id=1, source_target_pairs={{0,4},{1,5},{2,6},{3,7},{4,8},{5,9},{6,10},{7,11},{8,12},{9,13},{1... | collective-permute-start | bytes 393224 | tf_op jit(solution)/shard_map/ppermute | solution.py:31
  5.7 12.0 %collective-permute-start = (bf16[256,256]{1,0:T(8,128)(2,1)S(1)}, bf16[256,256]{1,0:T(8,128)(2,1)S(1)}, u32[]{:S(2)}, u32[]{:S(2)}) collective-permute-start(bf16[256,256]{1,0:T(8,128)(2,1)S(1)} %mark.1), channel_id=1, source_target_pairs={{0,2},{1,3},{2,4},{3,5},{4,6},{5,7},{6,8},{7,9},{8,10},{9,11},{10,... | collective-permute-start | bytes 393224 | tf_op jit(solution)/shard_map/ppermute | solution.py:31
  7.4 1.2 %copy-start.4 = (bf16[256,2048]{1,0:T(8,128)(2,1)S(1)}, bf16[256,2048]{1,0:T(8,128)(2,1)}, u32[]{:S(2)}) copy-start(bf16[256,2048]{1,0:T(8,128)(2,1)} %out_ref.1) | copy-start | bytes 3145732
  14.4 3.4 %collective-permute-start.2 = (f32[256,128]{1,0:T(8,128)S(1)}, f32[256,128]{1,0:T(8,128)S(1)}, u32[]{:S(2)}, u32[]{:S(2)}) collective-permute-start(f32[256,128]{1,0:T(8,128)S(1)} %get-tuple-element.39.refs_0_), channel_id=1, source_target_pairs={{0,8},{1,9},{2,10},{3,11},{4,12},{5,13},{6,14},{7,15},{8,0},{9,1},... | collective-permute-start | bytes 393224 | tf_op jit(solution)/shard_map/ppermute | solution.py:43
  14.4 6.6 %collective-permute-start.6 = (bf16[256,256]{1,0:T(8,128)(2,1)S(1)}, bf16[256,256]{1,0:T(8,128)(2,1)S(1)}, u32[]{:S(2)}, u32[]{:S(2)}) collective-permute-start(bf16[256,256]{1,0:T(8,128)(2,1)S(1)} %mark.1), channel_id=1, source_target_pairs={{0,8},{1,9},{2,10},{3,11},{4,12},{5,13},{6,14},{7,15},{8,16},{9,17... | collective-permute-start | bytes 393224 | tf_op jit(solution)/shard_map/ppermute | solution.py:31
  14.9 6.4 %collective-permute-start.5 = (bf16[256,256]{1,0:T(8,128)(2,1)S(1)}, bf16[256,256]{1,0:T(8,128)(2,1)S(1)}, u32[]{:S(2)}, u32[]{:S(2)}) collective-permute-start(bf16[256,256]{1,0:T(8,128)(2,1)S(1)} %mark.1), channel_id=1, source_target_pairs={{0,6},{1,7},{2,8},{3,9},{4,10},{5,11},{6,12},{7,13},{8,14},{9,15},... | collective-permute-start | bytes 393224 | tf_op jit(solution)/shard_map/ppermute | solution.py:31
  17.8 6.0 %collective-permute-start.4 = (f32[256,128]{1,0:T(8,128)S(1)}, f32[256,128]{1,0:T(8,128)S(1)}, u32[]{:S(2)}, u32[]{:S(2)}) collective-permute-start(f32[256,128]{1,0:T(8,128)S(1)} %get-tuple-element.42.refs_4_), channel_id=1, source_target_pairs={{0,16},{1,17},{2,18},{3,19},{4,20},{5,21},{6,22},{7,23},{8,24},{9,... | collective-permute-start | bytes 393224 | tf_op jit(solution)/shard_map/ppermute | solution.py:43
  18.4 9.2 %collective-permute-start.3 = (bf16[512,256]{1,0:T(8,128)(2,1)S(1)}, bf16[512,256]{1,0:T(8,128)(2,1)S(1)}, u32[]{:S(2)}, u32[]{:S(2)}) collective-permute-start(bf16[512,256]{1,0:T(8,128)(2,1)S(1)} %get-tuple-element.40.refs_5_), channel_id=1, source_target_pairs={{0,1},{1,0},{2,3},{3,2},{4,5},{5,4},{6,7},{7,6},{8,9},{9,8},{10,11... | collective-permute-start | bytes 786440 | tf_op jit(solution)/shard_map/ppermute | solution.py:43
  21.9 8.6 %collective-permute-start.7 = (bf16[512,256]{1,0:T(8,128)(2,1)S(1)}, bf16[512,256]{1,0:T(8,128)(2,1)S(1)}, u32[]{:S(2)}, u32[]{:S(2)}) collective-permute-start(bf16[512,256]{1,0:T(8,128)(2,1)S(1)} %far_blocks.1.refs_6_), channel_id=1, source_target_pairs={{0,1},{1,0},{2,3},{3,2},{4,5},{5,4},{6,7},{7,6},{8,9},{9,8},{10,11... | collective-permute-start | bytes 786440 | tf_op jit(solution)/shard_map/ppermute | solution.py:43
  28.6 9.3 %collective-permute-start.9 = (bf16[256,768]{1,0:T(8,128)(2,1)S(1)}, bf16[256,768]{1,0:T(8,128)(2,1)S(1)}, u32[]{:S(2)}, u32[]{:S(2)}) collective-permute-start(bf16[256,768]{1,0:T(8,128)(2,1)S(1)} %get-tuple-element.51.refs_0_), channel_id=1, source_target_pairs={{0,1},{1,0},{2,3},{3,2},{4,5},{5,4},{6,7},{7,6},{8,9},{9,8},{10,11... | collective-permute-start | bytes 1179656 | tf_op jit(solution)/shard_map/ppermute | solution.py:43
  31.4 15.1 %collective-permute-start.8 = (bf16[256,512]{1,0:T(8,128)(2,1)S(1)}, bf16[256,512]{1,0:T(8,128)(2,1)S(1)}, u32[]{:S(2)}, u32[]{:S(2)}) collective-permute-start(bf16[256,512]{1,0:T(8,128)(2,1)S(1)} %get-tuple-element.48), channel_id=1, source_target_pairs={{0,1},{1,0},{2,3},{3,2},{4,5},{5,4},{6,7},{7,6},{8,9},{9,8},{10,11... | collective-permute-start | bytes 786440 | tf_op jit(solution)/shard_map/ppermute | solution.py:43
  38.6 19.9 %collective-permute-start.10 = (bf16[256,384]{1,0:T(8,128)(2,1)S(1)}, bf16[256,384]{1,0:T(8,128)(2,1)S(1)}, u32[]{:S(2)}, u32[]{:S(2)}) collective-permute-start(bf16[256,384]{1,0:T(8,128)(2,1)S(1)} %get-tuple-element.56), channel_id=1, source_target_pairs={{0,30},{1,31},{2,0},{3,1},{4,2},{5,3},{6,4},{7,5},{8,6},{9,7},{10,... | collective-permute-start | bytes 589832 | tf_op jit(solution)/shard_map/ppermute | solution.py:31
  46.5 18.7 %collective-permute-start.11 = (bf16[256,384]{1,0:T(8,128)(2,1)S(1)}, bf16[256,384]{1,0:T(8,128)(2,1)S(1)}, u32[]{:S(2)}, u32[]{:S(2)}) collective-permute-start(bf16[256,384]{1,0:T(8,128)(2,1)S(1)} %get-tuple-element.57), channel_id=1, source_target_pairs={{0,28},{1,29},{2,30},{3,31},{4,0},{5,1},{6,2},{7,3},{8,4},{9,5},{1... | collective-permute-start | bytes 589832 | tf_op jit(solution)/shard_map/ppermute | solution.py:31
  47.2 18.0 %collective-permute-start.12 = (bf16[256,384]{1,0:T(8,128)(2,1)S(1)}, bf16[256,384]{1,0:T(8,128)(2,1)S(1)}, u32[]{:S(2)}, u32[]{:S(2)}) collective-permute-start(bf16[256,384]{1,0:T(8,128)(2,1)S(1)} %get-tuple-element.58), channel_id=1, source_target_pairs={{0,26},{1,27},{2,28},{3,29},{4,30},{5,31},{6,0},{7,1},{8,2},{9,3},... | collective-permute-start | bytes 589832 | tf_op jit(solution)/shard_map/ppermute | solution.py:31
  51.0 7.5 %collective-permute-start.13 = (bf16[256,256]{1,0:T(8,128)(2,1)S(1)}, bf16[256,256]{1,0:T(8,128)(2,1)S(1)}, u32[]{:S(2)}, u32[]{:S(2)}) collective-permute-start(bf16[256,256]{1,0:T(8,128)(2,1)S(1)} %get-tuple-element.53.refs_9_), channel_id=1, source_target_pairs={{0,24},{1,25},{2,26},{3,27},{4,28},{5,29},{6,30},{7,31},{8,0},{9,1... | collective-permute-start | bytes 393224 | tf_op jit(solution)/shard_map/ppermute | solution.py:31

commit v3 on v2

--- a/solution.py
+++ b/solution.py
@@ -44,14 +44,11 @@
 
 
 def exchange_rounds():
-    rounds = []
-    for axis in AXES:
-        step = 1
-        while step < lax.axis_size(axis):
-            if axis != AXES[-1] or step > 4:
-                rounds.append((axis, step))
-            step *= 2
-    return rounds
+    bits = {axis: [1 << bit for bit in range(lax.axis_size(axis).bit_length() - 1)] for axis in AXES}
+    first, rest = bits[AXES[0]][:1], bits[AXES[0]][1:]
+    low, high = bits[AXES[1]][:1], bits[AXES[1]][1:]
+    order = [(AXES[0], first), (AXES[1], high), (AXES[1], low), (AXES[0], rest)]
+    return [(axis, step) for axis, steps in order for step in steps]
 
 
 def span(index, size):
@@ -111,28 +108,16 @@
     pass
 
 
-def fold_kernel(table_ref, first_ref, second_ref, other_ref, *refs, rows, near):
-    if near:
-        mine_ref, first_out, second_out, sink_out = refs
-        sinks = (mine_ref.shape[1] - 2 * rows) // 2
-        sink = None
-        for ref in (mine_ref, other_ref):
-            high, low = ref[:, 2 * rows : 2 * rows + sinks], ref[:, 2 * rows + sinks :]
-            whole = high.astype(jnp.float32) + low.astype(jnp.float32)
-            sink = whole if sink is None else sink + whole
-        sink = sink.astype(LOW)
-        sink_out[...] = sink
-        second_out[:, rows:] = sink
-    else:
-        sink_ref, first_out, second_out = refs
-        sink = sink_ref[...]
-    first_out[:, :rows] = (first_ref[...] + other_ref[:, :rows].astype(jnp.float32)).astype(LOW)
-    first_out[:, rows:] = sink
-    other = other_ref[:, rows : 2 * rows].astype(jnp.float32)
+def fold_kernel(table_ref, first_ref, second_ref, other_ref, after_ref, *refs, near):
+    first_out, second_out, sum_ref = refs[-3:]
+    rows = first_ref.shape[1]
+    first_out[...] = (first_ref[...] + other_ref[:, :rows].astype(jnp.float32)).astype(LOW)
+    other = other_ref[:, rows:].astype(jnp.float32)
     if not near:
         odd = jnp.full(other.shape, table_ref[table_ref.shape[0] - 1] & 1, jnp.int32) == 1
         other = jnp.where(odd, other, 0.0)
-    second_out[:, :rows] = (second_ref[...] + other).astype(LOW)
+    second_out[...] = (second_ref[...] + other).astype(LOW)
+    sum_ref[...] = sum_of(refs[:-3])
 
 
 def near_kernel(two_ref, four_ref, *refs):
@@ -143,11 +128,13 @@
     sum_ref[...] = sum_of(refs[:-2])
 
 
-def far_kernel(table_ref, own_ref, six_ref, eight_ref, after_ref, far_ref):
+def far_kernel(table_ref, own_ref, six_ref, eight_ref, after_ref, *refs):
+    far_ref, sum_ref = refs[-2:]
     rows = own_ref.shape[0]
     odd = jnp.full(own_ref.shape, table_ref[table_ref.shape[0] - 1] & 1, jnp.int32) == 1
     far_ref[:rows, :] = six_ref[...]
     far_ref[rows:, :] = jnp.where(odd, eight_ref[...], own_ref[...])
+    sum_ref[...] = sum_of(refs[:-2])
 
 
 def local(distances, device):
@@ -165,13 +152,11 @@
         del refs[:count]
         return taken
 
-    pairs, sink_count, back_count, joined, last = layout
+    pairs, joined, last = layout
     table_ref, turned_ref, row_ref = take(3)
     device = table_ref[heads]
     distances = local([distance for pair in pairs for distance in pair], device)
     pair_refs = take(len(pairs))
-    sink_refs = take(sink_count)
-    back_refs = take(back_count)
     part_refs = take(1 + len(groups)) if last else []
     take(1)
     dquery_ref = take(1)[0]
@@ -180,6 +165,7 @@
     low_refs = take(4)
     total_ref, total_sems = take(2) if last else (None, None)
     rows = pair_ref.shape[1]
+    unroll = UNROLL if last else 2 * UNROLL
 
     slot = 0
     for ref, members in zip(pair_refs, pairs):
@@ -206,7 +192,7 @@
         return found
 
     found = lax.fori_loop(0, heads, list_head, 0)
-    steps = lax.div(found + UNROLL - 1, UNROLL)
+    steps = lax.div(found + unroll - 1, unroll)
 
     def pad_item(index, carry):
         items_ref[0, index] = 0
@@ -215,7 +201,7 @@
         items_ref[3, index] = 0
         return carry
 
-    lax.fori_loop(found, steps * UNROLL, pad_item, 0)
+    lax.fori_loop(found, steps * unroll, pad_item, 0)
 
     def produce(index, probs_ref, dscores_ref):
         slot, head, left = items_ref[0, index], items_ref[1, index], items_ref[2, index]
@@ -255,8 +241,8 @@
         return pltpu.make_async_copy(total_ref.at[:, lanes], dquery_ref.at[:, lanes], total_sems.at[step])
 
     def some_items(step, carry):
-        for part in range(UNROLL):
-            index = step * UNROLL + part
+        for part in range(unroll):
+            index = step * unroll + part
             produce(index, *buffers[part % 2])
             consume(jnp.maximum(index - 1, 0), *buffers[(part + 1) % 2])
         if last:
@@ -267,7 +253,7 @@
 
     @pl.when(found > 0)
     def _():
-        consume(steps * UNROLL - 1, *buffers[(UNROLL - 1) % 2])
+        consume(steps * unroll - 1, *buffers[(unroll - 1) % 2])
 
     if last:
         total_copy(heads // UNROLL - 1).start()
@@ -275,24 +261,16 @@
         grads = (sum_ref[slot, :width, :] * scale, sum_ref[slot, width:, :])
         for half, grad in enumerate(grads):
             strip = slice(half * width, (half + 1) * width)
-            for ref in back_refs:
-                grad = grad + ref[strip, :].astype(jnp.float32)
             if joined:
                 out_refs[0][strip, slot * rows : (slot + 1) * rows] = grad.astype(out_refs[0].dtype)
             else:
                 out_refs[slot][strip, :] = grad.astype(out_refs[slot].dtype)
-    if sink_count:
-        total = sum_of(sink_refs)
-        high = total.astype(LOW)
-        sinks = total.shape[1]
-        out_refs[0][:, len(distances) * rows : len(distances) * rows + sinks] = high
-        out_refs[0][:, len(distances) * rows + sinks :] = (total - high.astype(jnp.float32)).astype(LOW)
     if last:
         for step in range(heads // UNROLL):
             total_copy(step).wait()
 
 
-def block_call(pairs, pair_arrays, shared, after, sinks=(), backs=(), parts=(), groups=(), last=False, kind=LOW, joined=False):
+def block_call(pairs, pair_arrays, shared, after, parts=(), groups=(), last=False, kind=LOW, joined=False):
     table, turned, row_terms = shared
     wide, rows = turned.shape[0] // 2, turned.shape[1]
     heads = row_terms.shape[0] // 2
@@ -301,10 +279,9 @@
     count = len(distances)
     shape = jax.ShapeDtypeStruct
     outs = [shape((rows, wide) if last else (wide, rows), jnp.float32)]
-    extra = 2 * sinks[0].shape[1] if sinks else 0
-    outs += [shape((2 * width, count * rows + extra), kind)] if joined else [shape((2 * width, rows), kind)] * count
-    arrays = [turned, row_terms, *pair_arrays, *sinks, *backs, *parts, after]
-    layout = (pairs, len(sinks), len(backs), joined, last)
+    outs += [shape((2 * width, count * rows), kind)] if joined else [shape((2 * width, rows), kind)] * count
+    arrays = [turned, row_terms, *pair_arrays, *parts, after]
+    layout = (pairs, joined, last)
     return pl.pallas_call(
         functools.partial(
             block_kernel, layout=layout, groups=groups, heads=heads, width=width, scale=width**-0.5
@@ -313,7 +290,7 @@
         in_specs=[SMEM] + [VMEM] * (len(arrays) - 1) + [ANY],
         out_specs=[HBM if last else VMEM] + [VMEM] * (len(outs) - 1),
         scratch_shapes=[
-            pltpu.SMEM((4, count * heads + UNROLL), jnp.int32),
+            pltpu.SMEM((4, count * heads + 2 * UNROLL), jnp.int32),
             pltpu.VMEM((count, rows, 2 * width), LOW),
             pltpu.VMEM((count, width, rows), LOW),
             pltpu.VMEM((count, 2 * width, rows), jnp.float32),
@@ -328,21 +305,15 @@
     )(table, *arrays)
 
 
-def join_kernel(
-    table_ref, own_ref, other_ref, sink_ref, two_ref, four_ref, six_ref, eight_ref,
-    key_ref, value_ref, sink_key_ref, sink_value_ref, *, width,
-):
+def join_kernel(table_ref, own_ref, other_ref, *refs, width):
+    key_ref, value_ref, sink_key_ref, sink_value_ref = refs[-4:]
     rows = own_ref.shape[1]
     odd = jnp.full(own_ref.shape, table_ref[table_ref.shape[0] - 1] & 1, jnp.int32) == 1
     total = own_ref[...] + jnp.where(odd, 0.0, other_ref[:, rows:].astype(jnp.float32))
-    for ref in (two_ref, four_ref, six_ref, eight_ref):
-        total = total + ref[:, :rows].astype(jnp.float32)
-    turned = total.T
+    turned = (total + sum_of(refs[:4])).T
     key_ref[...] = turned[:, :width]
     value_ref[...] = turned[:, width:]
-    sums = [sink_ref[...]] + [ref[:, rows:] for ref in (two_ref, four_ref, six_ref)]
-    sums = [term.astype(jnp.float32) for term in sums]
-    turned = ((sums[0] + sums[2]) + (sums[1] + sums[3])).T
+    turned = sum_of(refs[4:-4]).T
     sink_key_ref[...] = turned[:, :width]
     sink_value_ref[...] = turned[:, width:]
 
@@ -368,7 +339,7 @@
         cost_estimate=pl.CostEstimate(flops=2 * 10**10, bytes_accessed=1, transcendentals=0),
         name="mark",
     )(own_pair)
-    even = {d: rotated(own_pair, d) for d in (8, 6, 4, 2)}
+    even = {d: rotated(own_pair, d) for d in (4, 2)}
 
     table, turned, row_terms, dquery, sink_grad, own_held = pl.pallas_call(
         functools.partial(sink_kernel, heads=heads, width=width, scale=width**-0.5),
@@ -387,6 +358,7 @@
         name="sink_keys_part",
     )(window_len, sink_live, device, keys, values, queries, out_grad, outputs, lse, sink_keys, sink_values)
 
+    even.update({d: rotated(own_held, d) for d in (8, 6)})
     rounds = exchange_rounds()
 
     def sink_terms():
@@ -403,7 +375,7 @@
     )(even[2], even[4], *terms)
     partner = ((AXES[-1], 1),)
     near_odd = swapped(near, partner)
-    while len(rounds) > 1:
+    while len(rounds) > 4:
         sink_grad = sum(sink_terms())
     terms = sink_terms()
 
@@ -414,17 +386,18 @@
     part, grad_2, grad_4 = block_call([(2,), (4,)], [even[2], even[4]], shared, near, kind=full)
     parts.append(part)
 
-    far = pl.pallas_call(
+    far, sink_grad = pl.pallas_call(
         far_kernel,
-        out_shape=shape((2 * rows, 2 * width), LOW),
-        in_specs=[SMEM] + [VMEM] * 3 + [ANY],
-        out_specs=VMEM,
+        out_shape=(shape((2 * rows, 2 * width), LOW), shape(sink_grad.shape, jnp.float32)),
+        in_specs=[SMEM] + [VMEM] * 3 + [ANY] + [VMEM] * len(terms),
+        out_specs=(VMEM,) * 2,
         compiler_params=pltpu.CompilerParams(vmem_limit_bytes=VMEM_BYTES),
         name="far_blocks",
-    )(table, own_held, even[6], even[8], part)
+    )(table, own_held, even[6], even[8], part, *terms)
+    terms = sink_terms()
     far_odd = swapped(far, partner)
 
-    part, near_mine = block_call([near_pair], [near_odd], shared, far, sinks=terms, joined=True)
+    part, near_mine = block_call([near_pair], [near_odd], shared, far, joined=True)
     parts.append(part)
     near_other = swapped(near_mine, partner)
 
@@ -432,24 +405,23 @@
     parts.append(part)
     far_other = swapped(far_mine, partner)
 
-    part, grad_6, grad_8 = block_call([(6,), (8,)], [even[6], even[8]], shared, part, kind=full)
-    parts.append(part)
-
-    def fold(first, second, other, extra, near):
-        outs = [shape((2 * width, rows + sinks), LOW), shape((2 * width, rows + (sinks if near else 0)), LOW)]
-        outs += [shape((2 * width, sinks), LOW)] if near else []
+    def fold(first, second, other, after, near):
         return pl.pallas_call(
-            functools.partial(fold_kernel, rows=rows, near=near),
-            out_shape=outs,
-            in_specs=[SMEM] + [VMEM] * 4,
-            out_specs=[VMEM] * len(outs),
+            functools.partial(fold_kernel, near=near),
+            out_shape=(shape(first.shape, LOW),) * 2 + (shape(sink_grad.shape, jnp.float32),),
+            in_specs=[SMEM] + [VMEM] * 3 + [ANY] + [VMEM] * len(terms),
+            out_specs=(VMEM,) * 3,
             compiler_params=pltpu.CompilerParams(vmem_limit_bytes=VMEM_BYTES),
             name="fold",
-        )(table, first, second, other, extra)
-
-    grad_2, grad_4, sink_low = fold(grad_2, grad_4, near_other, near_mine, True)
+        )(table, first, second, other, after, *terms)
+
+    grad_2, grad_4, sink_grad = fold(grad_2, grad_4, near_other, far_mine, True)
+    terms = sink_terms()
     backs = [rotated(grad_2, -2), rotated(grad_4, -4)]
-    grad_6, grad_8 = fold(grad_6, grad_8, far_other, sink_low, False)
+    part, grad_6, grad_8 = block_call([(6,), (8,)], [even[6], even[8]], shared, grad_4, kind=full)
+    parts.append(part)
+    grad_6, grad_8, sink_grad = fold(grad_6, grad_8, far_other, part, False)
+    terms = sink_terms()
     backs += [rotated(grad_6, -6), rotated(grad_8, -8)]
     dquery, own_grad = block_call(
         [(0,)], [own_held], shared, grad_8, parts=parts, kind=full, last=True,
@@ -458,11 +430,11 @@
     key_grad, value_grad, sink_key_grad, sink_value_grad = pl.pallas_call(
         functools.partial(join_kernel, width=width),
         out_shape=(shape((rows, width), jnp.float32),) * 2 + (shape((sinks, width), jnp.float32),) * 2,
-        in_specs=[SMEM] + [VMEM] * 7,
+        in_specs=[SMEM] + [VMEM] * (6 + len(terms)),
         out_specs=(VMEM,) * 4,
         compiler_params=pltpu.CompilerParams(vmem_limit_bytes=VMEM_BYTES),
         name="join",
-    )(table, own_grad, far_other, sink_low, *backs)
+    )(table, own_grad, far_other, *backs, *terms)
     return (dquery, key_grad, value_grad, sink_key_grad, sink_value_grad)
 
 

time: 67.2 us -> 61.1 us (0.909)
  waiting for transfers between devices: 11.6 us -> 8.29 us
  starting transfers between devices: 33.4 us -> 31.1 us
    ppermute x8, starting transfers between devices: 22.9 us -> 13.5 us  [rotated(): lax.ppermute(block, AXES, [(i, (i + distance) % count) for i in range(cou...]
    ppermute x6 -> x9, starting transfers between devices: 10.5 us -> 17.7 us  [swapped(): return lax.ppermute(block, AXES, route)]
    ppermute x8, waiting for transfers between devices: 6.92 us -> 1.04 us  [rotated(): lax.ppermute(block, AXES, [(i, (i + distance) % count) for i in range(cou...]
    ppermute x6 -> x9, waiting for transfers between devices: 4.72 us -> 7.25 us  [swapped(): return lax.ppermute(block, AXES, route)]
  transfers between devices with their start and end apart: 14 -> 17, of which waited for: 6 -> 5; matrix products, arithmetic and copies ran while one was open for 0% -> 0% of each run, Pallas kernels for 26% -> 28%
where the time goes in v3:
time: 61.1 us; the launch traced here: 60.9 us
  starting transfers between devices  31.1 us (51%)
  Pallas kernels  18.4 us (30%)
  waiting for transfers between devices  8.29 us (14%)
  local copies, waits for them, and re-layouts  1.28 us (2%)
  between operations  0.92 us (2%)
  other arithmetic  0.89 us (1%)
    ppermute x9, starting transfers between devices, swapped(): return lax.ppermute(block, AXES, route)  17.7 us
    ppermute x8, starting transfers between devices, rotated(): lax.ppermute(block, AXES, [(i, (i + distance) % count) for i in range(cou...  13.5 us
    pallas_call x5, Pallas kernels, block_call(): pl.pallas_call(functools.partial(block_kernel, layout=layout, groups=grou...  9.46 us
    ppermute x9, waiting for transfers between devices, swapped(): return lax.ppermute(block, AXES, route)  7.25 us
    pallas_call x1, Pallas kernels, on_device(): pl.pallas_call(functools.partial(sink_kernel, heads=heads, width=width, s...  5.74 us
    pallas_call x1, Pallas kernels, on_device(): pl.pallas_call(functools.partial(join_kernel, width=width), out_shape=(sh...  1.4 us
    unnamed x20, local copies, waits for them, and re-layouts  1.28 us
  transfers between devices with their start and end apart: 17, of which 5 were waited for; matrix products, arithmetic and copies ran while one was open for 0% of the time, Pallas kernels for 28%

profile of v3, /device:TPU:0, one launch (start us, length us, event | category | flops | bytes accessed | tf_op | source)
XLA Modules:
  0.0 60.9 jit_solution(9238663136349288425)
XLA Ops:
  1.6 4.1 %collective-permute-start.1 = (bf16[256,256]{1,0:T(8,128)(2,1)S(1)}, bf16[256,256]{1,0:T(8,128)(2,1)S(1)}, u32[]{:S(2)}, u32[]{:S(2)}) collective-permute-start(bf16[256,256]{1,0:T(8,128)(2,1)S(1)} %mark.1), channel_id=1, source_target_pairs={{0,4},{1,5},{2,6},{3,7},{4,8},{5,9},{6,10},{7,11},{8,12},{9,13},{1... | collective-permute-start | bytes 393224 | tf_op jit(solution)/shard_map/ppermute | solution.py:31
  5.7 1.6 %collective-permute-start = (bf16[256,256]{1,0:T(8,128)(2,1)S(1)}, bf16[256,256]{1,0:T(8,128)(2,1)S(1)}, u32[]{:S(2)}, u32[]{:S(2)}) collective-permute-start(bf16[256,256]{1,0:T(8,128)(2,1)S(1)} %mark.1), channel_id=1, source_target_pairs={{0,2},{1,3},{2,4},{3,5},{4,6},{5,7},{6,8},{7,9},{8,10},{9,11},{10,... | collective-permute-start | bytes 393224 | tf_op jit(solution)/shard_map/ppermute | solution.py:31
  7.4 1.2 %copy-done.4 = bf16[256,2048]{1,0:T(8,128)(2,1)S(1)} copy-done((bf16[256,2048]{1,0:T(8,128)(2,1)S(1)}, bf16[256,2048]{1,0:T(8,128)(2,1)}, u32[]{:S(2)}) %copy-start.4) | copy-done | bytes 1048600
  8.6 5.7 %sink_keys_part.1 = (s32[17]{0:T(128)S(1)}, bf16[4096,256]{1,0:T(8,128)(2,1)S(1)}, f32[32,256]{1,0:T(8,128)S(1)}, f32[2048,256]{1,0:T(8,128)S(1)}, f32[256,128]{1,0:T(8,128)S(1)}, /*index=5*/bf16[256,256]{1,0:T(8,128)(2,1)S(1)}) custom-call(s32[16]{0:T(128)S(1)} %copy-done.8, s32[16]{0:T(128)S(1)} %copy-done.9, s32[1]{0:T(128)} %bitcast.device_ref, ...), custom_call_target="tpu_custom_call" | custom-call | flops 10000000000 | bytes 1000000 | tf_op jit(solution)/shard_map/sink_keys_part/pallas_call | solution.py:344
  14.9 2.8 %collective-permute-start.4 = (bf16[256,256]{1,0:T(8,128)(2,1)S(1)}, bf16[256,256]{1,0:T(8,128)(2,1)S(1)}, u32[]{:S(2)}, u32[]{:S(2)}) collective-permute-start(bf16[256,256]{1,0:T(8,128)(2,1)S(1)} %get-tuple-element.40.own_ref.refs_3_), channel_id=1, source_target_pairs={{0,6},{1,7},{2,8},{3,9},{4,10},{5,11},{6,12},{7,13},{8,14},{9,15},... | collective-permute-start | bytes 393224 | tf_op jit(solution)/shard_map/ppermute | solution.py:31
  17.9 1.6 %collective-permute-start.3 = (bf16[512,256]{1,0:T(8,128)(2,1)S(1)}, bf16[512,256]{1,0:T(8,128)(2,1)S(1)}, u32[]{:S(2)}, u32[]{:S(2)}) collective-permute-start(bf16[512,256]{1,0:T(8,128)(2,1)S(1)} %get-tuple-element.43.refs_5_), channel_id=1, source_target_pairs={{0,1},{1,0},{2,3},{3,2},{4,5},{5,4},{6,7},{7,6},{8,9},{9,8},{10,11... | collective-permute-start | bytes 786440 | tf_op jit(solution)/shard_map/ppermute | solution.py:43
  19.5 1.0 %blocks_2_4.1 = (f32[2048,256]{1,0:T(8,128)S(1)}, f32[256,256]{1,0:T(8,128)S(1)}, f32[256,256]{1,0:T(8,128)S(1)}) custom-call(s32[17]{0:T(128)S(1)} %get-tuple-element.37.refs_0_.table_ref, bf16[4096,256]{1,0:T(8,128)(2,1)S(1)} %get-tuple-element.38.refs_1_, f32[32,256]{1,0:T(8,128)S(1)} %get-tuple-element.39.refs_2_, ...), custom_call_target="tpu_custom_call" | custom-call | flops 2684354560 | bytes 1048576 | tf_op jit(solution)/shard_map/blocks_2_4/pallas_call | solution.py:285
  20.6 1.0 %collective-permute-done.4.six_ref.refs_3_ = bf16[256,256]{1,0:T(8,128)(2,1)S(1)} collective-permute-done((bf16[256,256]{1,0:T(8,128)(2,1)S(1)}, bf16[256,256]{1,0:T(8,128)(2,1)S(1)}, u32[]{:S(2)}, u32[]{:S(2)}) %collective-permute-start.4) | collective-permute-done | bytes 131104 | tf_op jit(solution)/shard_map/ppermute | solution.py:31
  21.6 2.9 %collective-permute-done.6.refs_1_ = f32[256,128]{1,0:T(8,128)S(1)} collective-permute-done((f32[256,128]{1,0:T(8,128)S(1)}, f32[256,128]{1,0:T(8,128)S(1)}, u32[]{:S(2)}, u32[]{:S(2)}) %collective-permute-start.6) | collective-permute-done | bytes 131104 | tf_op jit(solution)/shard_map/ppermute | solution.py:43
  25.0 1.6 %collective-permute-start.7 = (bf16[512,256]{1,0:T(8,128)(2,1)S(1)}, bf16[512,256]{1,0:T(8,128)(2,1)S(1)}, u32[]{:S(2)}, u32[]{:S(2)}) collective-permute-start(bf16[512,256]{1,0:T(8,128)(2,1)S(1)} %get-tuple-element.46.refs_4_), channel_id=1, source_target_pairs={{0,1},{1,0},{2,3},{3,2},{4,5},{5,4},{6,7},{7,6},{8,9},{9,8},{10,11... | collective-permute-start | bytes 786440 | tf_op jit(solution)/shard_map/ppermute | solution.py:43
  26.6 1.0 %blocks_1_3.1 = (f32[2048,256]{1,0:T(8,128)S(1)}, bf16[256,512]{1,0:T(8,128)(2,1)S(1)}) custom-call(s32[17]{0:T(128)S(1)} %get-tuple-element.37.refs_0_.table_ref, bf16[4096,256]{1,0:T(8,128)(2,1)S(1)} %get-tuple-element.38.refs_1_, f32[32,256]{1,0:T(8,128)S(1)} %get-tuple-element.39.refs_2_, bf16[512,256]{1,0:T(8,128)(2,1)S(1)} %collective-permute-done.3.refs_3_, ...), custom_call_target="tpu_custom_call" | custom-call | flops 2684354560 | bytes 1048576 | tf_op jit(solution)/shard_map/blocks_1_3/pallas_call | solution.py:285
  27.7 1.4 %collective-permute-start.8 = (bf16[256,512]{1,0:T(8,128)(2,1)S(1)}, bf16[256,512]{1,0:T(8,128)(2,1)S(1)}, u32[]{:S(2)}, u32[]{:S(2)}) collective-permute-start(bf16[256,512]{1,0:T(8,128)(2,1)S(1)} %get-tuple-element.51), channel_id=1, source_target_pairs={{0,1},{1,0},{2,3},{3,2},{4,5},{5,4},{6,7},{7,6},{8,9},{9,8},{10,11... | collective-permute-start | bytes 786440 | tf_op jit(solution)/shard_map/ppermute | solution.py:43
  29.1 6.0 %collective-permute-start.9 = (f32[256,128]{1,0:T(8,128)S(1)}, f32[256,128]{1,0:T(8,128)S(1)}, u32[]{:S(2)}, u32[]{:S(2)}) collective-permute-start(f32[256,128]{1,0:T(8,128)S(1)} %get-tuple-element.53.refs_0_), channel_id=1, source_target_pairs={{0,4},{1,5},{2,6},{3,7},{4,0},{5,1},{6,2},{7,3},{8,12},{9,13},{10,... | collective-permute-start | bytes 393224 | tf_op jit(solution)/shard_map/ppermute | solution.py:43
  35.1 1.0 %blocks_5_7.1 = (f32[2048,256]{1,0:T(8,128)S(1)}, bf16[256,512]{1,0:T(8,128)(2,1)S(1)}) custom-call(s32[17]{0:T(128)S(1)} %get-tuple-element.37.refs_0_.table_ref, bf16[4096,256]{1,0:T(8,128)(2,1)S(1)} %get-tuple-element.38.refs_1_, f32[32,256]{1,0:T(8,128)S(1)} %get-tuple-element.39.refs_2_, bf16[512,256]{1,0:T(8,128)(2,1)S(1)} %collective-permute-done.7.refs_3_, ...), custom_call_target="tpu_custom_call" | custom-call | flops 2684354560 | bytes 1048576 | tf_op jit(solution)/shard_map/blocks_5_7/pallas_call | solution.py:285
  36.1 4.6 %collective-permute-start.10 = (bf16[256,512]{1,0:T(8,128)(2,1)S(1)}, bf16[256,512]{1,0:T(8,128)(2,1)S(1)}, u32[]{:S(2)}, u32[]{:S(2)}) collective-permute-start(bf16[256,512]{1,0:T(8,128)(2,1)S(1)} %get-tuple-element.52.after_ref), channel_id=1, source_target_pairs={{0,1},{1,0},{2,3},{3,2},{4,5},{5,4},{6,7},{7,6},{8,9},{9,8},{10,11... | collective-permute-start | bytes 786440 | tf_op jit(solution)/shard_map/ppermute | solution.py:43
  40.7 1.4 %collective-permute-done.9.refs_1_ = f32[256,128]{1,0:T(8,128)S(1)} collective-permute-done((f32[256,128]{1,0:T(8,128)S(1)}, f32[256,128]{1,0:T(8,128)S(1)}, u32[]{:S(2)}, u32[]{:S(2)}) %collective-permute-start.9) | collective-permute-done | bytes 131104 | tf_op jit(solution)/shard_map/ppermute | solution.py:43
  42.7 2.3 %collective-permute-start.12 = (bf16[256,256]{1,0:T(8,128)(2,1)S(1)}, bf16[256,256]{1,0:T(8,128)(2,1)S(1)}, u32[]{:S(2)}, u32[]{:S(2)}) collective-permute-start(bf16[256,256]{1,0:T(8,128)(2,1)S(1)} %get-tuple-element.62), channel_id=1, source_target_pairs={{0,30},{1,31},{2,0},{3,1},{4,2},{5,3},{6,4},{7,5},{8,6},{9,7},{10,... | collective-permute-start | bytes 393224 | tf_op jit(solution)/shard_map/ppermute | solution.py:31
  45.0 1.7 %collective-permute-start.11 = (f32[256,128]{1,0:T(8,128)S(1)}, f32[256,128]{1,0:T(8,128)S(1)}, u32[]{:S(2)}, u32[]{:S(2)}) collective-permute-start(f32[256,128]{1,0:T(8,128)S(1)} %get-tuple-element.58.refs_0_), channel_id=1, source_target_pairs={{0,1},{1,0},{2,3},{3,2},{4,5},{5,4},{6,7},{7,6},{8,9},{9,8},{10,11... | collective-permute-start | bytes 393224 | tf_op jit(solution)/shard_map/ppermute | solution.py:43
  46.6 1.0 %blocks_6_8.1 = (f32[2048,256]{1,0:T(8,128)S(1)}, f32[256,256]{1,0:T(8,128)S(1)}, f32[256,256]{1,0:T(8,128)S(1)}) custom-call(s32[17]{0:T(128)S(1)} %get-tuple-element.37.refs_0_.table_ref, bf16[4096,256]{1,0:T(8,128)(2,1)S(1)} %get-tuple-element.38.refs_1_, f32[32,256]{1,0:T(8,128)S(1)} %get-tuple-element.39.refs_2_, ...), custom_call_target="tpu_custom_call" | custom-call | flops 2684354560 | bytes 1048576 | tf_op jit(solution)/shard_map/blocks_6_8/pallas_call | solution.py:285
  47.7 2.9 %collective-permute-done.11.refs_1_ = f32[256,128]{1,0:T(8,128)S(1)} collective-permute-done((f32[256,128]{1,0:T(8,128)S(1)}, f32[256,128]{1,0:T(8,128)S(1)}, u32[]{:S(2)}, u32[]{:S(2)}) %collective-permute-start.11) | collective-permute-done | bytes 131104 | tf_op jit(solution)/shard_map/ppermute | solution.py:43
  51.2 1.0 %collective-permute-start.14 = (bf16[256,256]{1,0:T(8,128)(2,1)S(1)}, bf16[256,256]{1,0:T(8,128)(2,1)S(1)}, u32[]{:S(2)}, u32[]{:S(2)}) collective-permute-start(bf16[256,256]{1,0:T(8,128)(2,1)S(1)} %get-tuple-element.63), channel_id=1, source_target_pairs={{0,26},{1,27},{2,28},{3,29},{4,30},{5,31},{6,0},{7,1},{8,2},{9,3},... | collective-permute-start | bytes 393224 | tf_op jit(solution)/shard_map/ppermute | solution.py:31
  52.2 1.2 %collective-permute-start.15 = (bf16[256,256]{1,0:T(8,128)(2,1)S(1)}, bf16[256,256]{1,0:T(8,128)(2,1)S(1)}, u32[]{:S(2)}, u32[]{:S(2)}) collective-permute-start(bf16[256,256]{1,0:T(8,128)(2,1)S(1)} %get-tuple-element.59.refs_9_), channel_id=1, source_target_pairs={{0,24},{1,25},{2,26},{3,27},{4,28},{5,29},{6,30},{7,31},{8,0},{9,1... | collective-permute-start | bytes 393224 | tf_op jit(solution)/shard_map/ppermute | solution.py:31
  54.0 5.4 %blocks_0.1 = (f32[256,2048]{1,0:T(8,128)}, f32[256,256]{1,0:T(8,128)S(1)}) custom-call(s32[17]{0:T(128)S(1)} %get-tuple-element.37.refs_0_.table_ref, bf16[4096,256]{1,0:T(8,128)(2,1)S(1)} %get-tuple-element.38.refs_1_, f32[32,256]{1,0:T(8,128)S(1)} %get-tuple-element.39.refs_2_, bf16[256,256]{1,0:T(8,128)(2,1)S(1)} %get-tuple-element.40.own_ref.refs_3_, ...), custom_call_target="tpu_custom_call" | custom-call | flops 1342177280 | bytes 1048576 | tf_op jit(solution)/shard_map/blocks_0/pallas_call | solution.py:285
  59.5 1.4 %join.1 = (f32[256,128]{1,0:T(8,128)}, f32[256,128]{1,0:T(8,128)}, f32[128,128]{1,0:T(8,128)}, f32[128,128]{1,0:T(8,128)}) custom-call(s32[17]{0:T(128)S(1)} %get-tuple-element.37.refs_0_.table_ref, f32[256,256]{1,0:T(8,128)S(1)} %get-tuple-element.61.own_ref, bf16[256,512]{1,0:T(8,128)(2,1)S(1)} %collective-permute-done.10.other_ref, ...), custom_call_target="tpu_custom_call" | custom-call | tf_op jit(solution)/shard_map/join/pallas_call | solution.py:430
  (43 shorter events, 4.2 us)
Async XLA Ops:
  1.5 5.8 %copy-start = (bf16[256,128]{1,0:T(8,128)(2,1)S(1)}, bf16[256,128]{1,0:T(8,128)(2,1)}, u32[]{:S(2)}) copy-start(bf16[256,128]{1,0:T(8,128)(2,1)} %key_ref.1) | copy-start | bytes 196612
  1.5 5.8 %copy-start.1 = (bf16[256,128]{1,0:T(8,128)(2,1)S(1)}, bf16[256,128]{1,0:T(8,128)(2,1)}, u32[]{:S(2)}) copy-start(bf16[256,128]{1,0:T(8,128)(2,1)} %value_ref.1) | copy-start | bytes 196612
  1.5 5.8 %copy-start.2 = (bf16[256,2048]{1,0:T(8,128)(2,1)S(1)}, bf16[256,2048]{1,0:T(8,128)(2,1)}, u32[]{:S(2)}) copy-start(bf16[256,2048]{1,0:T(8,128)(2,1)} %query_ref.1) | copy-start | bytes 3145732
  1.6 5.8 %copy-start.3 = (bf16[256,2048]{1,0:T(8,128)(2,1)S(1)}, bf16[256,2048]{1,0:T(8,128)(2,1)}, u32[]{:S(2)}) copy-start(bf16[256,2048]{1,0:T(8,128)(2,1)} %grad_ref.1) | copy-start | bytes 3145732
  1.6 5.8 %copy-start.5 = (bf16[128,128]{1,0:T(8,128)(2,1)S(1)}, bf16[128,128]{1,0:T(8,128)(2,1)}, u32[]{:S(2)}) copy-start(bf16[128,128]{1,0:T(8,128)(2,1)} %sink_key_ref.1) | copy-start | bytes 98308
  1.6 5.8 %copy-start.6 = (bf16[128,128]{1,0:T(8,128)(2,1)S(1)}, bf16[128,128]{1,0:T(8,128)(2,1)}, u32[]{:S(2)}) copy-start(bf16[128,128]{1,0:T(8,128)(2,1)} %sink_value_ref.1) | copy-start | bytes 98308
  1.6 5.8 %copy-start.7 = (f32[16,256]{1,0:T(8,128)S(1)}, f32[16,256]{1,0:T(8,128)}, u32[]{:S(2)}) copy-start(f32[16,256]{1,0:T(8,128)} %lse_in.1) | copy-start | bytes 49156
  1.6 16.1 %collective-permute-start.1 = (bf16[256,256]{1,0:T(8,128)(2,1)S(1)}, bf16[256,256]{1,0:T(8,128)(2,1)S(1)}, u32[]{:S(2)}, u32[]{:S(2)}) collective-permute-start(bf16[256,256]{1,0:T(8,128)(2,1)S(1)} %mark.1), channel_id=1, source_target_pairs={{0,4},{1,5},{2,6},{3,7},{4,8},{5,9},{6,10},{7,11},{8,12},{9,13},{1... | collective-permute-start | bytes 393224 | tf_op jit(solution)/shard_map/ppermute | solution.py:31
  5.7 12.0 %collective-permute-start = (bf16[256,256]{1,0:T(8,128)(2,1)S(1)}, bf16[256,256]{1,0:T(8,128)(2,1)S(1)}, u32[]{:S(2)}, u32[]{:S(2)}) collective-permute-start(bf16[256,256]{1,0:T(8,128)(2,1)S(1)} %mark.1), channel_id=1, source_target_pairs={{0,2},{1,3},{2,4},{3,5},{4,6},{5,7},{6,8},{7,9},{8,10},{9,11},{10,... | collective-permute-start | bytes 393224 | tf_op jit(solution)/shard_map/ppermute | solution.py:31
  14.4 3.4 %collective-permute-start.2 = (f32[256,128]{1,0:T(8,128)S(1)}, f32[256,128]{1,0:T(8,128)S(1)}, u32[]{:S(2)}, u32[]{:S(2)}) collective-permute-start(f32[256,128]{1,0:T(8,128)S(1)} %get-tuple-element.42.refs_0_), channel_id=1, source_target_pairs={{0,8},{1,9},{2,10},{3,11},{4,12},{5,13},{6,14},{7,15},{8,0},{9,1},... | collective-permute-start | bytes 393224 | tf_op jit(solution)/shard_map/ppermute | solution.py:43
  14.4 6.1 %collective-permute-start.5 = (bf16[256,256]{1,0:T(8,128)(2,1)S(1)}, bf16[256,256]{1,0:T(8,128)(2,1)S(1)}, u32[]{:S(2)}, u32[]{:S(2)}) collective-permute-start(bf16[256,256]{1,0:T(8,128)(2,1)S(1)} %get-tuple-element.40.own_ref.refs_3_), channel_id=1, source_target_pairs={{0,8},{1,9},{2,10},{3,11},{4,12},{5,13},{6,14},{7,15},{8,16},{9,17... | collective-permute-start | bytes 393224 | tf_op jit(solution)/shard_map/ppermute | solution.py:31
  14.9 6.6 %collective-permute-start.4 = (bf16[256,256]{1,0:T(8,128)(2,1)S(1)}, bf16[256,256]{1,0:T(8,128)(2,1)S(1)}, u32[]{:S(2)}, u32[]{:S(2)}) collective-permute-start(bf16[256,256]{1,0:T(8,128)(2,1)S(1)} %get-tuple-element.40.own_ref.refs_3_), channel_id=1, source_target_pairs={{0,6},{1,7},{2,8},{3,9},{4,10},{5,11},{6,12},{7,13},{8,14},{9,15},... | collective-permute-start | bytes 393224 | tf_op jit(solution)/shard_map/ppermute | solution.py:31
  17.8 6.6 %collective-permute-start.6 = (f32[256,128]{1,0:T(8,128)S(1)}, f32[256,128]{1,0:T(8,128)S(1)}, u32[]{:S(2)}, u32[]{:S(2)}) collective-permute-start(f32[256,128]{1,0:T(8,128)S(1)} %get-tuple-element.45.refs_0_), channel_id=1, source_target_pairs={{0,2},{1,3},{2,0},{3,1},{4,6},{5,7},{6,4},{7,5},{8,10},{9,11},{10,... | collective-permute-start | bytes 393224 | tf_op jit(solution)/shard_map/ppermute | solution.py:43
  17.9 8.7 %collective-permute-start.3 = (bf16[512,256]{1,0:T(8,128)(2,1)S(1)}, bf16[512,256]{1,0:T(8,128)(2,1)S(1)}, u32[]{:S(2)}, u32[]{:S(2)}) collective-permute-start(bf16[512,256]{1,0:T(8,128)(2,1)S(1)} %get-tuple-element.43.refs_5_), channel_id=1, source_target_pairs={{0,1},{1,0},{2,3},{3,2},{4,5},{5,4},{6,7},{7,6},{8,9},{9,8},{10,11... | collective-permute-start | bytes 786440 | tf_op jit(solution)/shard_map/ppermute | solution.py:43
  25.0 10.0 %collective-permute-start.7 = (bf16[512,256]{1,0:T(8,128)(2,1)S(1)}, bf16[512,256]{1,0:T(8,128)(2,1)S(1)}, u32[]{:S(2)}, u32[]{:S(2)}) collective-permute-start(bf16[512,256]{1,0:T(8,128)(2,1)S(1)} %get-tuple-element.46.refs_4_), channel_id=1, source_target_pairs={{0,1},{1,0},{2,3},{3,2},{4,5},{5,4},{6,7},{7,6},{8,9},{9,8},{10,11... | collective-permute-start | bytes 786440 | tf_op jit(solution)/shard_map/ppermute | solution.py:43
  27.7 14.5 %collective-permute-start.8 = (bf16[256,512]{1,0:T(8,128)(2,1)S(1)}, bf16[256,512]{1,0:T(8,128)(2,1)S(1)}, u32[]{:S(2)}, u32[]{:S(2)}) collective-permute-start(bf16[256,512]{1,0:T(8,128)(2,1)S(1)} %get-tuple-element.51), channel_id=1, source_target_pairs={{0,1},{1,0},{2,3},{3,2},{4,5},{5,4},{6,7},{7,6},{8,9},{9,8},{10,11... | collective-permute-start | bytes 786440 | tf_op jit(solution)/shard_map/ppermute | solution.py:43
  29.1 13.0 %collective-permute-start.9 = (f32[256,128]{1,0:T(8,128)S(1)}, f32[256,128]{1,0:T(8,128)S(1)}, u32[]{:S(2)}, u32[]{:S(2)}) collective-permute-start(f32[256,128]{1,0:T(8,128)S(1)} %get-tuple-element.53.refs_0_), channel_id=1, source_target_pairs={{0,4},{1,5},{2,6},{3,7},{4,0},{5,1},{6,2},{7,3},{8,12},{9,13},{10,... | collective-permute-start | bytes 393224 | tf_op jit(solution)/shard_map/ppermute | solution.py:43
  36.1 11.6 %collective-permute-start.10 = (bf16[256,512]{1,0:T(8,128)(2,1)S(1)}, bf16[256,512]{1,0:T(8,128)(2,1)S(1)}, u32[]{:S(2)}, u32[]{:S(2)}) collective-permute-start(bf16[256,512]{1,0:T(8,128)(2,1)S(1)} %get-tuple-element.52.after_ref), channel_id=1, source_target_pairs={{0,1},{1,0},{2,3},{3,2},{4,5},{5,4},{6,7},{7,6},{8,9},{9,8},{10,11... | collective-permute-start | bytes 786440 | tf_op jit(solution)/shard_map/ppermute | solution.py:43
  42.7 16.7 %collective-permute-start.12 = (bf16[256,256]{1,0:T(8,128)(2,1)S(1)}, bf16[256,256]{1,0:T(8,128)(2,1)S(1)}, u32[]{:S(2)}, u32[]{:S(2)}) collective-permute-start(bf16[256,256]{1,0:T(8,128)(2,1)S(1)} %get-tuple-element.62), channel_id=1, source_target_pairs={{0,30},{1,31},{2,0},{3,1},{4,2},{5,3},{6,4},{7,5},{8,6},{9,7},{10,... | collective-permute-start | bytes 393224 | tf_op jit(solution)/shard_map/ppermute | solution.py:31
  45.0 14.4 %collective-permute-start.13 = (bf16[256,256]{1,0:T(8,128)(2,1)S(1)}, bf16[256,256]{1,0:T(8,128)(2,1)S(1)}, u32[]{:S(2)}, u32[]{:S(2)}) collective-permute-start(bf16[256,256]{1,0:T(8,128)(2,1)S(1)} %get-tuple-element.54.refs_5_), channel_id=1, source_target_pairs={{0,28},{1,29},{2,30},{3,31},{4,0},{5,1},{6,2},{7,3},{8,4},{9,5},{1... | collective-permute-start | bytes 393224 | tf_op jit(solution)/shard_map/ppermute | solution.py:31
  45.0 5.6 %collective-permute-start.11 = (f32[256,128]{1,0:T(8,128)S(1)}, f32[256,128]{1,0:T(8,128)S(1)}, u32[]{:S(2)}, u32[]{:S(2)}) collective-permute-start(f32[256,128]{1,0:T(8,128)S(1)} %get-tuple-element.58.refs_0_), channel_id=1, source_target_pairs={{0,1},{1,0},{2,3},{3,2},{4,5},{5,4},{6,7},{7,6},{8,9},{9,8},{10,11... | collective-permute-start | bytes 393224 | tf_op jit(solution)/shard_map/ppermute | solution.py:43
  51.2 8.2 %collective-permute-start.14 = (bf16[256,256]{1,0:T(8,128)(2,1)S(1)}, bf16[256,256]{1,0:T(8,128)(2,1)S(1)}, u32[]{:S(2)}, u32[]{:S(2)}) collective-permute-start(bf16[256,256]{1,0:T(8,128)(2,1)S(1)} %get-tuple-element.63), channel_id=1, source_target_pairs={{0,26},{1,27},{2,28},{3,29},{4,30},{5,31},{6,0},{7,1},{8,2},{9,3},... | collective-permute-start | bytes 393224 | tf_op jit(solution)/shard_map/ppermute | solution.py:31
  52.2 7.2 %collective-permute-start.15 = (bf16[256,256]{1,0:T(8,128)(2,1)S(1)}, bf16[256,256]{1,0:T(8,128)(2,1)S(1)}, u32[]{:S(2)}, u32[]{:S(2)}) collective-permute-start(bf16[256,256]{1,0:T(8,128)(2,1)S(1)} %get-tuple-element.59.refs_9_), channel_id=1, source_target_pairs={{0,24},{1,25},{2,26},{3,27},{4,28},{5,29},{6,30},{7,31},{8,0},{9,1... | collective-permute-start | bytes 393224 | tf_op jit(solution)/shard_map/ppermute | solution.py:31
  53.4 6.2 %collective-permute-start.16 = (f32[256,128]{1,0:T(8,128)S(1)}, f32[256,128]{1,0:T(8,128)S(1)}, u32[]{:S(2)}, u32[]{:S(2)}) collective-permute-start(f32[256,128]{1,0:T(8,128)S(1)} %get-tuple-element.64.refs_4_), channel_id=1, source_target_pairs={{0,16},{1,17},{2,18},{3,19},{4,20},{5,21},{6,22},{7,23},{8,24},{9,... | collective-permute-start | bytes 393224 | tf_op jit(solution)/shard_map/ppermute | solution.py:43
  (3 other events, 12.7 us)

commit v4 on v3

--- a/solution.py
+++ b/solution.py
@@ -15,6 +15,7 @@
 NT = (((1,), (1,)), ((), ()))
 VMEM_BYTES = 22 * 1024 * 1024
 UNROLL = 4
+AHEAD = 2
 LOW = jnp.bfloat16
 VMEM = pl.BlockSpec(memory_space=pltpu.VMEM)
 SMEM = pl.BlockSpec(memory_space=pltpu.SMEM)
@@ -72,26 +73,31 @@
     key, value = sink_key_ref[...], sink_value_ref[...]
     key_t = key.T
 
-    def one_head(head):
-        strip = span(head, width)
-        query_t = query_ref[:, strip].T
-        grad_t = grad_ref[:, strip].T
-        turned_ref[strip, :] = query_t
-        turned_ref[span(heads + head, width), :] = grad_t
-        product = grad_t.astype(jnp.float32) * out_ref[:, strip].T.astype(jnp.float32)
-        delta = jnp.sum(product, axis=0, keepdims=True)
-        row_ref[pl.ds(heads + head, 1), :] = delta
-        probs = jnp.exp2(dot(key, query_t) * (scale * LOG2E) - row_ref[pl.ds(head, 1), :])
-        at = lax.broadcasted_iota(jnp.int32, (sinks, rows), 0)
-        probs = jnp.where(at < live_ref[head], probs, 0.0)
+    at = lax.broadcasted_iota(jnp.int32, (sinks, rows), 0)
+
+    def some_heads(step, carry):
+        heads_here = [UNROLL * step + part for part in range(UNROLL)]
+        query_t, grad_t, keep, delta = [], [], [], []
+        for head in heads_here:
+            strip = span(head, width)
+            query_t.append(query_ref[:, strip].T)
+            grad_t.append(grad_ref[:, strip].T)
+            turned_ref[strip, :] = query_t[-1]
+            turned_ref[span(heads + head, width), :] = grad_t[-1]
+            product = grad_t[-1].astype(jnp.float32) * out_ref[:, strip].T.astype(jnp.float32)
+            delta.append(jnp.sum(product, axis=0, keepdims=True))
+            row_ref[pl.ds(heads + head, 1), :] = delta[-1]
+            keep.append(at < live_ref[head])
+        lse = jnp.concatenate([lse_in[pl.ds(head, 1), :] for head in heads_here], axis=1) * LOG2E
+        query_t, grad_t, keep, delta = (jnp.concatenate(x, axis=1) for x in (query_t, grad_t, keep, delta))
+        probs = jnp.exp2(dot(key, query_t) * (scale * LOG2E) - lse)
+        probs = jnp.where(keep, probs, 0.0)
         dscores = (probs * (dot(value, grad_t) - delta)).astype(LOW)
         sink_grad_ref[:width, :] += dot(query_t, dscores, NT) * scale
         sink_grad_ref[width:, :] += dot(grad_t, probs.astype(LOW), NT)
-        dquery_ref[strip, :] = dot(key_t, dscores)
-
-    def some_heads(step, carry):
-        for part in range(UNROLL):
-            one_head(UNROLL * step + part)
+        dquery = dot(key_t, dscores)
+        for part, head in enumerate(heads_here):
+            dquery_ref[span(head, width), :] = dquery[:, part * rows : (part + 1) * rows]
         return carry
 
     lax.fori_loop(0, heads // UNROLL, some_heads, 0)
@@ -162,7 +168,7 @@
     dquery_ref = take(1)[0]
     out_refs = take(1 if joined else len(distances))
     items_ref, pair_ref, key_t_ref, sum_ref = take(4)
-    low_refs = take(4)
+    low_refs = take(2 * AHEAD + 4)
     total_ref, total_sems = take(2) if last else (None, None)
     rows = pair_ref.shape[1]
     unroll = UNROLL if last else 2 * UNROLL
@@ -234,7 +240,7 @@
         else:
             dquery_ref[strip, :] = dquery + jnp.where(items_ref[3, index] == 1, 0.0, dquery_ref[strip, :])
 
-    buffers = (low_refs[:2], low_refs[2:])
+    buffers = [low_refs[2 * at : 2 * at + 2] for at in range(AHEAD + 2)]
 
     def total_copy(step):
         lanes = span(step, UNROLL * width)
@@ -243,8 +249,8 @@
     def some_items(step, carry):
         for part in range(unroll):
             index = step * unroll + part
-            produce(index, *buffers[part % 2])
-            consume(jnp.maximum(index - 1, 0), *buffers[(part + 1) % 2])
+            produce(index, *buffers[part % len(buffers)])
+            consume(jnp.maximum(index - AHEAD, 0), *buffers[(part - AHEAD) % len(buffers)])
         if last:
             pl.when(step > 0)(lambda: total_copy(step - 1).start())
         return carry
@@ -253,7 +259,8 @@
 
     @pl.when(found > 0)
     def _():
-        consume(steps * unroll - 1, *buffers[(unroll - 1) % 2])
+        for at in range(unroll - AHEAD, unroll):
+            consume((steps - 1) * unroll + at, *buffers[at % len(buffers)])
 
     if last:
         total_copy(heads // UNROLL - 1).start()
@@ -295,7 +302,7 @@
             pltpu.VMEM((count, width, rows), LOW),
             pltpu.VMEM((count, 2 * width, rows), jnp.float32),
         ]
-        + [pltpu.VMEM((rows, rows), LOW)] * 4
+        + [pltpu.VMEM((rows, rows), LOW)] * (2 * AHEAD + 4)
         + ([pltpu.VMEM((rows, wide), jnp.float32), pltpu.SemaphoreType.DMA((heads // UNROLL,))] if last else []),
         compiler_params=pltpu.CompilerParams(vmem_limit_bytes=VMEM_BYTES),
         cost_estimate=pl.CostEstimate(

time: 61.1 us -> 59.9 us (0.980)
  waiting for transfers between devices: 8.29 us -> 10.5 us
  starting transfers between devices: 31.1 us -> 29.4 us
  Pallas kernels: 18.4 us -> 17.1 us
    ppermute x9, waiting for transfers between devices: 7.25 us -> 9.54 us  [swapped(): return lax.ppermute(block, AXES, route)]
    pallas_call x1, Pallas kernels: 5.74 us -> 3.98 us  [on_device(): pl.pallas_call(functools.partial(sink_kernel, heads=heads, width=width, s...]
    ppermute x9, starting transfers between devices: 17.7 us -> 16.2 us  [swapped(): return lax.ppermute(block, AXES, route)]
  transfers between devices with their start and end apart: 17 -> 17, of which waited for: 5 -> 5; matrix products, arithmetic and copies ran while one was open for 0% -> 0% of each run, Pallas kernels for 28% -> 26%
where the time goes in v4:
time: 59.9 us; the launch traced here: 60 us
  starting transfers between devices  29.4 us (49%)
  Pallas kernels  17.1 us (29%)
  waiting for transfers between devices  10.5 us (18%)
  local copies, waits for them, and re-layouts  1.28 us (2%)
  between operations  0.92 us (2%)
  other arithmetic  0.89 us (1%)
    ppermute x9, starting transfers between devices, swapped(): return lax.ppermute(block, AXES, route)  16.2 us
    ppermute x8, starting transfers between devices, rotated(): lax.ppermute(block, AXES, [(i, (i + distance) % count) for i in range(cou...  13.2 us
    pallas_call x5, Pallas kernels, block_call(): pl.pallas_call(functools.partial(block_kernel, layout=layout, groups=grou...  9.86 us
    ppermute x9, waiting for transfers between devices, swapped(): return lax.ppermute(block, AXES, route)  9.54 us
    pallas_call x1, Pallas kernels, on_device(): pl.pallas_call(functools.partial(sink_kernel, heads=heads, width=width, s...  3.98 us
    pallas_call x1, Pallas kernels, on_device(): pl.pallas_call(functools.partial(join_kernel, width=width), out_shape=(sh...  1.4 us
    unnamed x20, local copies, waits for them, and re-layouts  1.28 us
    pallas_call x2, Pallas kernels, fold(): pl.pallas_call(functools.partial(fold_kernel, near=near), out_shape=(shap...  1.2 us
  transfers between devices with their start and end apart: 17, of which 5 were waited for; matrix products, arithmetic and copies ran while one was open for 0% of the time, Pallas kernels for 26%

profile of v4, /device:TPU:0, one launch (start us, length us, event | category | flops | bytes accessed | tf_op | source)
XLA Modules:
  0.0 60.0 jit_solution(6559895491655244515)
XLA Ops:
  0.6 0.9 %pad_maximum_fusion.block_ref = bf16[256,256]{1,0:T(8,128)(2,1)S(1)} fusion(bf16[256,128]{1,0:T(8,128)(2,1)} %value_ref.1, bf16[256,128]{1,0:T(8,128)(2,1)} %key_ref.1), kind=kLoop, calls=%fused_computation | loop fusion | flops 262144 | bytes 262144 | tf_op jit(solution)/shard_map/concatenate | solution.py:338
  1.6 4.1 %collective-permute-start.1 = (bf16[256,256]{1,0:T(8,128)(2,1)S(1)}, bf16[256,256]{1,0:T(8,128)(2,1)S(1)}, u32[]{:S(2)}, u32[]{:S(2)}) collective-permute-start(bf16[256,256]{1,0:T(8,128)(2,1)S(1)} %mark.1), channel_id=1, source_target_pairs={{0,4},{1,5},{2,6},{3,7},{4,8},{5,9},{6,10},{7,11},{8,12},{9,13},{1... | collective-permute-start | bytes 393224 | tf_op jit(solution)/shard_map/ppermute | solution.py:32
  5.7 1.6 %collective-permute-start = (bf16[256,256]{1,0:T(8,128)(2,1)S(1)}, bf16[256,256]{1,0:T(8,128)(2,1)S(1)}, u32[]{:S(2)}, u32[]{:S(2)}) collective-permute-start(bf16[256,256]{1,0:T(8,128)(2,1)S(1)} %mark.1), channel_id=1, source_target_pairs={{0,2},{1,3},{2,4},{3,5},{4,6},{5,7},{6,8},{7,9},{8,10},{9,11},{10,... | collective-permute-start | bytes 393224 | tf_op jit(solution)/shard_map/ppermute | solution.py:32
  7.4 1.2 %copy-done.4 = bf16[256,2048]{1,0:T(8,128)(2,1)S(1)} copy-done((bf16[256,2048]{1,0:T(8,128)(2,1)S(1)}, bf16[256,2048]{1,0:T(8,128)(2,1)}, u32[]{:S(2)}) %copy-start.4) | copy-done | bytes 1048600
  8.6 4.0 %sink_keys_part.1 = (s32[17]{0:T(128)S(1)}, bf16[4096,256]{1,0:T(8,128)(2,1)S(1)}, f32[32,256]{1,0:T(8,128)S(1)}, f32[2048,256]{1,0:T(8,128)S(1)}, f32[256,128]{1,0:T(8,128)S(1)}, /*index=5*/bf16[256,256]{1,0:T(8,128)(2,1)S(1)}) custom-call(s32[16]{0:T(128)S(1)} %copy-done.8, s32[16]{0:T(128)S(1)} %copy-done.9, s32[1]{0:T(128)} %bitcast.device_ref, ...), custom_call_target="tpu_custom_call" | custom-call | flops 10000000000 | bytes 1000000 | tf_op jit(solution)/shard_map/sink_keys_part/pallas_call | solution.py:351
  13.2 2.8 %collective-permute-start.4 = (bf16[256,256]{1,0:T(8,128)(2,1)S(1)}, bf16[256,256]{1,0:T(8,128)(2,1)S(1)}, u32[]{:S(2)}, u32[]{:S(2)}) collective-permute-start(bf16[256,256]{1,0:T(8,128)(2,1)S(1)} %get-tuple-element.40.own_ref.refs_3_), channel_id=1, source_target_pairs={{0,6},{1,7},{2,8},{3,9},{4,10},{5,11},{6,12},{7,13},{8,14},{9,15},... | collective-permute-start | bytes 393224 | tf_op jit(solution)/shard_map/ppermute | solution.py:32
  16.2 1.7 %collective-permute-start.3 = (bf16[512,256]{1,0:T(8,128)(2,1)S(1)}, bf16[512,256]{1,0:T(8,128)(2,1)S(1)}, u32[]{:S(2)}, u32[]{:S(2)}) collective-permute-start(bf16[512,256]{1,0:T(8,128)(2,1)S(1)} %get-tuple-element.43.refs_5_), channel_id=1, source_target_pairs={{0,1},{1,0},{2,3},{3,2},{4,5},{5,4},{6,7},{7,6},{8,9},{9,8},{10,11... | collective-permute-start | bytes 786440 | tf_op jit(solution)/shard_map/ppermute | solution.py:44
  17.8 1.1 %blocks_2_4.1 = (f32[2048,256]{1,0:T(8,128)S(1)}, f32[256,256]{1,0:T(8,128)S(1)}, f32[256,256]{1,0:T(8,128)S(1)}) custom-call(s32[17]{0:T(128)S(1)} %get-tuple-element.37.refs_0_.table_ref, bf16[4096,256]{1,0:T(8,128)(2,1)S(1)} %get-tuple-element.38.refs_1_, f32[32,256]{1,0:T(8,128)S(1)} %get-tuple-element.39.refs_2_, ...), custom_call_target="tpu_custom_call" | custom-call | flops 2684354560 | bytes 1048576 | tf_op jit(solution)/shard_map/blocks_2_4/pallas_call | solution.py:292
  18.9 0.9 %collective-permute-done.4.six_ref.refs_3_ = bf16[256,256]{1,0:T(8,128)(2,1)S(1)} collective-permute-done((bf16[256,256]{1,0:T(8,128)(2,1)S(1)}, bf16[256,256]{1,0:T(8,128)(2,1)S(1)}, u32[]{:S(2)}, u32[]{:S(2)}) %collective-permute-start.4) | collective-permute-done | bytes 131104 | tf_op jit(solution)/shard_map/ppermute | solution.py:32
  19.8 2.9 %collective-permute-done.6.refs_1_ = f32[256,128]{1,0:T(8,128)S(1)} collective-permute-done((f32[256,128]{1,0:T(8,128)S(1)}, f32[256,128]{1,0:T(8,128)S(1)}, u32[]{:S(2)}, u32[]{:S(2)}) %collective-permute-start.6) | collective-permute-done | bytes 131104 | tf_op jit(solution)/shard_map/ppermute | solution.py:44
  23.3 1.6 %collective-permute-start.7 = (bf16[512,256]{1,0:T(8,128)(2,1)S(1)}, bf16[512,256]{1,0:T(8,128)(2,1)S(1)}, u32[]{:S(2)}, u32[]{:S(2)}) collective-permute-start(bf16[512,256]{1,0:T(8,128)(2,1)S(1)} %get-tuple-element.46.refs_4_), channel_id=1, source_target_pairs={{0,1},{1,0},{2,3},{3,2},{4,5},{5,4},{6,7},{7,6},{8,9},{9,8},{10,11... | collective-permute-start | bytes 786440 | tf_op jit(solution)/shard_map/ppermute | solution.py:44
  24.9 1.0 %blocks_1_3.1 = (f32[2048,256]{1,0:T(8,128)S(1)}, bf16[256,512]{1,0:T(8,128)(2,1)S(1)}) custom-call(s32[17]{0:T(128)S(1)} %get-tuple-element.37.refs_0_.table_ref, bf16[4096,256]{1,0:T(8,128)(2,1)S(1)} %get-tuple-element.38.refs_1_, f32[32,256]{1,0:T(8,128)S(1)} %get-tuple-element.39.refs_2_, bf16[512,256]{1,0:T(8,128)(2,1)S(1)} %collective-permute-done.3.refs_3_, ...), custom_call_target="tpu_custom_call" | custom-call | flops 2684354560 | bytes 1048576 | tf_op jit(solution)/shard_map/blocks_1_3/pallas_call | solution.py:292
  25.9 1.4 %collective-permute-start.8 = (bf16[256,512]{1,0:T(8,128)(2,1)S(1)}, bf16[256,512]{1,0:T(8,128)(2,1)S(1)}, u32[]{:S(2)}, u32[]{:S(2)}) collective-permute-start(bf16[256,512]{1,0:T(8,128)(2,1)S(1)} %get-tuple-element.51), channel_id=1, source_target_pairs={{0,1},{1,0},{2,3},{3,2},{4,5},{5,4},{6,7},{7,6},{8,9},{9,8},{10,11... | collective-permute-start | bytes 786440 | tf_op jit(solution)/shard_map/ppermute | solution.py:44
  27.4 7.1 %collective-permute-start.9 = (f32[256,128]{1,0:T(8,128)S(1)}, f32[256,128]{1,0:T(8,128)S(1)}, u32[]{:S(2)}, u32[]{:S(2)}) collective-permute-start(f32[256,128]{1,0:T(8,128)S(1)} %get-tuple-element.53.refs_0_), channel_id=1, source_target_pairs={{0,4},{1,5},{2,6},{3,7},{4,0},{5,1},{6,2},{7,3},{8,12},{9,13},{10,... | collective-permute-start | bytes 393224 | tf_op jit(solution)/shard_map/ppermute | solution.py:44
  34.5 1.0 %blocks_5_7.1 = (f32[2048,256]{1,0:T(8,128)S(1)}, bf16[256,512]{1,0:T(8,128)(2,1)S(1)}) custom-call(s32[17]{0:T(128)S(1)} %get-tuple-element.37.refs_0_.table_ref, bf16[4096,256]{1,0:T(8,128)(2,1)S(1)} %get-tuple-element.38.refs_1_, f32[32,256]{1,0:T(8,128)S(1)} %get-tuple-element.39.refs_2_, bf16[512,256]{1,0:T(8,128)(2,1)S(1)} %collective-permute-done.7.refs_3_, ...), custom_call_target="tpu_custom_call" | custom-call | flops 2684354560 | bytes 1048576 | tf_op jit(solution)/shard_map/blocks_5_7/pallas_call | solution.py:292
  35.5 3.2 %collective-permute-start.10 = (bf16[256,512]{1,0:T(8,128)(2,1)S(1)}, bf16[256,512]{1,0:T(8,128)(2,1)S(1)}, u32[]{:S(2)}, u32[]{:S(2)}) collective-permute-start(bf16[256,512]{1,0:T(8,128)(2,1)S(1)} %get-tuple-element.52.after_ref), channel_id=1, source_target_pairs={{0,1},{1,0},{2,3},{3,2},{4,5},{5,4},{6,7},{7,6},{8,9},{9,8},{10,11... | collective-permute-start | bytes 786440 | tf_op jit(solution)/shard_map/ppermute | solution.py:44
  38.8 2.8 %collective-permute-done.9.refs_1_ = f32[256,128]{1,0:T(8,128)S(1)} collective-permute-done((f32[256,128]{1,0:T(8,128)S(1)}, f32[256,128]{1,0:T(8,128)S(1)}, u32[]{:S(2)}, u32[]{:S(2)}) %collective-permute-start.9) | collective-permute-done | bytes 131104 | tf_op jit(solution)/shard_map/ppermute | solution.py:44
  42.1 2.3 %collective-permute-start.12 = (bf16[256,256]{1,0:T(8,128)(2,1)S(1)}, bf16[256,256]{1,0:T(8,128)(2,1)S(1)}, u32[]{:S(2)}, u32[]{:S(2)}) collective-permute-start(bf16[256,256]{1,0:T(8,128)(2,1)S(1)} %get-tuple-element.62), channel_id=1, source_target_pairs={{0,30},{1,31},{2,0},{3,1},{4,2},{5,3},{6,4},{7,5},{8,6},{9,7},{10,... | collective-permute-start | bytes 393224 | tf_op jit(solution)/shard_map/ppermute | solution.py:32
  44.9 1.1 %blocks_6_8.1 = (f32[2048,256]{1,0:T(8,128)S(1)}, f32[256,256]{1,0:T(8,128)S(1)}, f32[256,256]{1,0:T(8,128)S(1)}) custom-call(s32[17]{0:T(128)S(1)} %get-tuple-element.37.refs_0_.table_ref, bf16[4096,256]{1,0:T(8,128)(2,1)S(1)} %get-tuple-element.38.refs_1_, f32[32,256]{1,0:T(8,128)S(1)} %get-tuple-element.39.refs_2_, ...), custom_call_target="tpu_custom_call" | custom-call | flops 2684354560 | bytes 1048576 | tf_op jit(solution)/shard_map/blocks_6_8/pallas_call | solution.py:292
  46.0 3.8 %collective-permute-done.11.refs_1_ = f32[256,128]{1,0:T(8,128)S(1)} collective-permute-done((f32[256,128]{1,0:T(8,128)S(1)}, f32[256,128]{1,0:T(8,128)S(1)}, u32[]{:S(2)}, u32[]{:S(2)}) %collective-permute-start.11) | collective-permute-done | bytes 131104 | tf_op jit(solution)/shard_map/ppermute | solution.py:44
  50.4 1.1 %collective-permute-start.14 = (bf16[256,256]{1,0:T(8,128)(2,1)S(1)}, bf16[256,256]{1,0:T(8,128)(2,1)S(1)}, u32[]{:S(2)}, u32[]{:S(2)}) collective-permute-start(bf16[256,256]{1,0:T(8,128)(2,1)S(1)} %get-tuple-element.63), channel_id=1, source_target_pairs={{0,26},{1,27},{2,28},{3,29},{4,30},{5,31},{6,0},{7,1},{8,2},{9,3},... | collective-permute-start | bytes 393224 | tf_op jit(solution)/shard_map/ppermute | solution.py:32
  51.5 0.8 %collective-permute-start.15 = (bf16[256,256]{1,0:T(8,128)(2,1)S(1)}, bf16[256,256]{1,0:T(8,128)(2,1)S(1)}, u32[]{:S(2)}, u32[]{:S(2)}) collective-permute-start(bf16[256,256]{1,0:T(8,128)(2,1)S(1)} %get-tuple-element.59.refs_9_), channel_id=1, source_target_pairs={{0,24},{1,25},{2,26},{3,27},{4,28},{5,29},{6,30},{7,31},{8,0},{9,1... | collective-permute-start | bytes 393224 | tf_op jit(solution)/shard_map/ppermute | solution.py:32
  52.9 5.6 %blocks_0.1 = (f32[256,2048]{1,0:T(8,128)}, f32[256,256]{1,0:T(8,128)S(1)}) custom-call(s32[17]{0:T(128)S(1)} %get-tuple-element.37.refs_0_.table_ref, bf16[4096,256]{1,0:T(8,128)(2,1)S(1)} %get-tuple-element.38.refs_1_, f32[32,256]{1,0:T(8,128)S(1)} %get-tuple-element.39.refs_2_, bf16[256,256]{1,0:T(8,128)(2,1)S(1)} %get-tuple-element.40.own_ref.refs_3_, ...), custom_call_target="tpu_custom_call" | custom-call | flops 1342177280 | bytes 1048576 | tf_op jit(solution)/shard_map/blocks_0/pallas_call | solution.py:292
  58.6 1.4 %join.1 = (f32[256,128]{1,0:T(8,128)}, f32[256,128]{1,0:T(8,128)}, f32[128,128]{1,0:T(8,128)}, f32[128,128]{1,0:T(8,128)}) custom-call(s32[17]{0:T(128)S(1)} %get-tuple-element.37.refs_0_.table_ref, f32[256,256]{1,0:T(8,128)S(1)} %get-tuple-element.61.own_ref, bf16[256,512]{1,0:T(8,128)(2,1)S(1)} %collective-permute-done.10.other_ref, ...), custom_call_target="tpu_custom_call" | custom-call | tf_op jit(solution)/shard_map/join/pallas_call | solution.py:437
  (43 shorter events, 3.7 us)
Async XLA Ops:
  1.5 5.8 %copy-start = (bf16[256,128]{1,0:T(8,128)(2,1)S(1)}, bf16[256,128]{1,0:T(8,128)(2,1)}, u32[]{:S(2)}) copy-start(bf16[256,128]{1,0:T(8,128)(2,1)} %key_ref.1) | copy-start | bytes 196612
  1.5 5.8 %copy-start.1 = (bf16[256,128]{1,0:T(8,128)(2,1)S(1)}, bf16[256,128]{1,0:T(8,128)(2,1)}, u32[]{:S(2)}) copy-start(bf16[256,128]{1,0:T(8,128)(2,1)} %value_ref.1) | copy-start | bytes 196612
  1.5 5.8 %copy-start.2 = (bf16[256,2048]{1,0:T(8,128)(2,1)S(1)}, bf16[256,2048]{1,0:T(8,128)(2,1)}, u32[]{:S(2)}) copy-start(bf16[256,2048]{1,0:T(8,128)(2,1)} %query_ref.1) | copy-start | bytes 3145732
  1.6 5.8 %copy-start.3 = (bf16[256,2048]{1,0:T(8,128)(2,1)S(1)}, bf16[256,2048]{1,0:T(8,128)(2,1)}, u32[]{:S(2)}) copy-start(bf16[256,2048]{1,0:T(8,128)(2,1)} %grad_ref.1) | copy-start | bytes 3145732
  1.6 5.8 %copy-start.5 = (bf16[128,128]{1,0:T(8,128)(2,1)S(1)}, bf16[128,128]{1,0:T(8,128)(2,1)}, u32[]{:S(2)}) copy-start(bf16[128,128]{1,0:T(8,128)(2,1)} %sink_key_ref.1) | copy-start | bytes 98308
  1.6 5.8 %copy-start.6 = (bf16[128,128]{1,0:T(8,128)(2,1)S(1)}, bf16[128,128]{1,0:T(8,128)(2,1)}, u32[]{:S(2)}) copy-start(bf16[128,128]{1,0:T(8,128)(2,1)} %sink_value_ref.1) | copy-start | bytes 98308
  1.6 5.8 %copy-start.7 = (f32[16,256]{1,0:T(8,128)S(1)}, f32[16,256]{1,0:T(8,128)}, u32[]{:S(2)}) copy-start(f32[16,256]{1,0:T(8,128)} %lse_in.1) | copy-start | bytes 49156
  1.6 14.4 %collective-permute-start.1 = (bf16[256,256]{1,0:T(8,128)(2,1)S(1)}, bf16[256,256]{1,0:T(8,128)(2,1)S(1)}, u32[]{:S(2)}, u32[]{:S(2)}) collective-permute-start(bf16[256,256]{1,0:T(8,128)(2,1)S(1)} %mark.1), channel_id=1, source_target_pairs={{0,4},{1,5},{2,6},{3,7},{4,8},{5,9},{6,10},{7,11},{8,12},{9,13},{1... | collective-permute-start | bytes 393224 | tf_op jit(solution)/shard_map/ppermute | solution.py:32
  5.7 10.3 %collective-permute-start = (bf16[256,256]{1,0:T(8,128)(2,1)S(1)}, bf16[256,256]{1,0:T(8,128)(2,1)S(1)}, u32[]{:S(2)}, u32[]{:S(2)}) collective-permute-start(bf16[256,256]{1,0:T(8,128)(2,1)S(1)} %mark.1), channel_id=1, source_target_pairs={{0,2},{1,3},{2,4},{3,5},{4,6},{5,7},{6,8},{7,9},{8,10},{9,11},{10,... | collective-permute-start | bytes 393224 | tf_op jit(solution)/shard_map/ppermute | solution.py:32
  12.6 3.4 %collective-permute-start.2 = (f32[256,128]{1,0:T(8,128)S(1)}, f32[256,128]{1,0:T(8,128)S(1)}, u32[]{:S(2)}, u32[]{:S(2)}) collective-permute-start(f32[256,128]{1,0:T(8,128)S(1)} %get-tuple-element.42.refs_0_), channel_id=1, source_target_pairs={{0,8},{1,9},{2,10},{3,11},{4,12},{5,13},{6,14},{7,15},{8,0},{9,1},... | collective-permute-start | bytes 393224 | tf_op jit(solution)/shard_map/ppermute | solution.py:44
  12.7 6.2 %collective-permute-start.5 = (bf16[256,256]{1,0:T(8,128)(2,1)S(1)}, bf16[256,256]{1,0:T(8,128)(2,1)S(1)}, u32[]{:S(2)}, u32[]{:S(2)}) collective-permute-start(bf16[256,256]{1,0:T(8,128)(2,1)S(1)} %get-tuple-element.40.own_ref.refs_3_), channel_id=1, source_target_pairs={{0,8},{1,9},{2,10},{3,11},{4,12},{5,13},{6,14},{7,15},{8,16},{9,17... | collective-permute-start | bytes 393224 | tf_op jit(solution)/shard_map/ppermute | solution.py:32
  13.2 6.6 %collective-permute-start.4 = (bf16[256,256]{1,0:T(8,128)(2,1)S(1)}, bf16[256,256]{1,0:T(8,128)(2,1)S(1)}, u32[]{:S(2)}, u32[]{:S(2)}) collective-permute-start(bf16[256,256]{1,0:T(8,128)(2,1)S(1)} %get-tuple-element.40.own_ref.refs_3_), channel_id=1, source_target_pairs={{0,6},{1,7},{2,8},{3,9},{4,10},{5,11},{6,12},{7,13},{8,14},{9,15},... | collective-permute-start | bytes 393224 | tf_op jit(solution)/shard_map/ppermute | solution.py:32
  16.1 6.6 %collective-permute-start.6 = (f32[256,128]{1,0:T(8,128)S(1)}, f32[256,128]{1,0:T(8,128)S(1)}, u32[]{:S(2)}, u32[]{:S(2)}) collective-permute-start(f32[256,128]{1,0:T(8,128)S(1)} %get-tuple-element.45.refs_0_), channel_id=1, source_target_pairs={{0,2},{1,3},{2,0},{3,1},{4,6},{5,7},{6,4},{7,5},{8,10},{9,11},{10,... | collective-permute-start | bytes 393224 | tf_op jit(solution)/shard_map/ppermute | solution.py:44
  16.2 8.7 %collective-permute-start.3 = (bf16[512,256]{1,0:T(8,128)(2,1)S(1)}, bf16[512,256]{1,0:T(8,128)(2,1)S(1)}, u32[]{:S(2)}, u32[]{:S(2)}) collective-permute-start(bf16[512,256]{1,0:T(8,128)(2,1)S(1)} %get-tuple-element.43.refs_5_), channel_id=1, source_target_pairs={{0,1},{1,0},{2,3},{3,2},{4,5},{5,4},{6,7},{7,6},{8,9},{9,8},{10,11... | collective-permute-start | bytes 786440 | tf_op jit(solution)/shard_map/ppermute | solution.py:44
  23.3 11.2 %collective-permute-start.7 = (bf16[512,256]{1,0:T(8,128)(2,1)S(1)}, bf16[512,256]{1,0:T(8,128)(2,1)S(1)}, u32[]{:S(2)}, u32[]{:S(2)}) collective-permute-start(bf16[512,256]{1,0:T(8,128)(2,1)S(1)} %get-tuple-element.46.refs_4_), channel_id=1, source_target_pairs={{0,1},{1,0},{2,3},{3,2},{4,5},{5,4},{6,7},{7,6},{8,9},{9,8},{10,11... | collective-permute-start | bytes 786440 | tf_op jit(solution)/shard_map/ppermute | solution.py:44
  25.9 15.6 %collective-permute-start.8 = (bf16[256,512]{1,0:T(8,128)(2,1)S(1)}, bf16[256,512]{1,0:T(8,128)(2,1)S(1)}, u32[]{:S(2)}, u32[]{:S(2)}) collective-permute-start(bf16[256,512]{1,0:T(8,128)(2,1)S(1)} %get-tuple-element.51), channel_id=1, source_target_pairs={{0,1},{1,0},{2,3},{3,2},{4,5},{5,4},{6,7},{7,6},{8,9},{9,8},{10,11... | collective-permute-start | bytes 786440 | tf_op jit(solution)/shard_map/ppermute | solution.py:44
  27.4 14.1 %collective-permute-start.9 = (f32[256,128]{1,0:T(8,128)S(1)}, f32[256,128]{1,0:T(8,128)S(1)}, u32[]{:S(2)}, u32[]{:S(2)}) collective-permute-start(f32[256,128]{1,0:T(8,128)S(1)} %get-tuple-element.53.refs_0_), channel_id=1, source_target_pairs={{0,4},{1,5},{2,6},{3,7},{4,0},{5,1},{6,2},{7,3},{8,12},{9,13},{10,... | collective-permute-start | bytes 393224 | tf_op jit(solution)/shard_map/ppermute | solution.py:44
  35.5 10.5 %collective-permute-start.10 = (bf16[256,512]{1,0:T(8,128)(2,1)S(1)}, bf16[256,512]{1,0:T(8,128)(2,1)S(1)}, u32[]{:S(2)}, u32[]{:S(2)}) collective-permute-start(bf16[256,512]{1,0:T(8,128)(2,1)S(1)} %get-tuple-element.52.after_ref), channel_id=1, source_target_pairs={{0,1},{1,0},{2,3},{3,2},{4,5},{5,4},{6,7},{7,6},{8,9},{9,8},{10,11... | collective-permute-start | bytes 786440 | tf_op jit(solution)/shard_map/ppermute | solution.py:44
  42.1 16.4 %collective-permute-start.12 = (bf16[256,256]{1,0:T(8,128)(2,1)S(1)}, bf16[256,256]{1,0:T(8,128)(2,1)S(1)}, u32[]{:S(2)}, u32[]{:S(2)}) collective-permute-start(bf16[256,256]{1,0:T(8,128)(2,1)S(1)} %get-tuple-element.62), channel_id=1, source_target_pairs={{0,30},{1,31},{2,0},{3,1},{4,2},{5,3},{6,4},{7,5},{8,6},{9,7},{10,... | collective-permute-start | bytes 393224 | tf_op jit(solution)/shard_map/ppermute | solution.py:32
  44.4 14.0 %collective-permute-start.13 = (bf16[256,256]{1,0:T(8,128)(2,1)S(1)}, bf16[256,256]{1,0:T(8,128)(2,1)S(1)}, u32[]{:S(2)}, u32[]{:S(2)}) collective-permute-start(bf16[256,256]{1,0:T(8,128)(2,1)S(1)} %get-tuple-element.54.refs_5_), channel_id=1, source_target_pairs={{0,28},{1,29},{2,30},{3,31},{4,0},{5,1},{6,2},{7,3},{8,4},{9,5},{1... | collective-permute-start | bytes 393224 | tf_op jit(solution)/shard_map/ppermute | solution.py:32
  44.5 5.4 %collective-permute-start.11 = (f32[256,128]{1,0:T(8,128)S(1)}, f32[256,128]{1,0:T(8,128)S(1)}, u32[]{:S(2)}, u32[]{:S(2)}) collective-permute-start(f32[256,128]{1,0:T(8,128)S(1)} %get-tuple-element.58.refs_0_), channel_id=1, source_target_pairs={{0,1},{1,0},{2,3},{3,2},{4,5},{5,4},{6,7},{7,6},{8,9},{9,8},{10,11... | collective-permute-start | bytes 393224 | tf_op jit(solution)/shard_map/ppermute | solution.py:44
  50.4 8.1 %collective-permute-start.14 = (bf16[256,256]{1,0:T(8,128)(2,1)S(1)}, bf16[256,256]{1,0:T(8,128)(2,1)S(1)}, u32[]{:S(2)}, u32[]{:S(2)}) collective-permute-start(bf16[256,256]{1,0:T(8,128)(2,1)S(1)} %get-tuple-element.63), channel_id=1, source_target_pairs={{0,26},{1,27},{2,28},{3,29},{4,30},{5,31},{6,0},{7,1},{8,2},{9,3},... | collective-permute-start | bytes 393224 | tf_op jit(solution)/shard_map/ppermute | solution.py:32
  51.5 7.0 %collective-permute-start.15 = (bf16[256,256]{1,0:T(8,128)(2,1)S(1)}, bf16[256,256]{1,0:T(8,128)(2,1)S(1)}, u32[]{:S(2)}, u32[]{:S(2)}) collective-permute-start(bf16[256,256]{1,0:T(8,128)(2,1)S(1)} %get-tuple-element.59.refs_9_), channel_id=1, source_target_pairs={{0,24},{1,25},{2,26},{3,27},{4,28},{5,29},{6,30},{7,31},{8,0},{9,1... | collective-permute-start | bytes 393224 | tf_op jit(solution)/shard_map/ppermute | solution.py:32
  52.3 6.3 %collective-permute-start.16 = (f32[256,128]{1,0:T(8,128)S(1)}, f32[256,128]{1,0:T(8,128)S(1)}, u32[]{:S(2)}, u32[]{:S(2)}) collective-permute-start(f32[256,128]{1,0:T(8,128)S(1)} %get-tuple-element.64.refs_4_), channel_id=1, source_target_pairs={{0,16},{1,17},{2,18},{3,19},{4,20},{5,21},{6,22},{7,23},{8,24},{9,... | collective-permute-start | bytes 393224 | tf_op jit(solution)/shard_map/ppermute | solution.py:44
  (3 other events, 12.7 us)

commit v5 on v4

--- a/solution.py
+++ b/solution.py
@@ -48,7 +48,7 @@
     bits = {axis: [1 << bit for bit in range(lax.axis_size(axis).bit_length() - 1)] for axis in AXES}
     first, rest = bits[AXES[0]][:1], bits[AXES[0]][1:]
     low, high = bits[AXES[1]][:1], bits[AXES[1]][1:]
-    order = [(AXES[0], first), (AXES[1], high), (AXES[1], low), (AXES[0], rest)]
+    order = [(AXES[0], first), (AXES[1], high), (AXES[0], rest), (AXES[1], low)]
     return [(axis, step) for axis, steps in order for step in steps]
 
 
@@ -123,7 +123,7 @@
         odd = jnp.full(other.shape, table_ref[table_ref.shape[0] - 1] & 1, jnp.int32) == 1
         other = jnp.where(odd, other, 0.0)
     second_out[...] = (second_ref[...] + other).astype(LOW)
-    sum_ref[...] = sum_of(refs[:-3])
+    sum_ref[...] = sum_of(refs[:-3]).astype(sum_ref.dtype)
 
 
 def near_kernel(two_ref, four_ref, *refs):
@@ -164,6 +164,7 @@
     distances = local([distance for pair in pairs for distance in pair], device)
     pair_refs = take(len(pairs))
     part_refs = take(1 + len(groups)) if last else []
+    other_refs = take(1) if last else []
     take(1)
     dquery_ref = take(1)[0]
     out_refs = take(1 if joined else len(distances))
@@ -171,7 +172,7 @@
     low_refs = take(2 * AHEAD + 4)
     total_ref, total_sems = take(2) if last else (None, None)
     rows = pair_ref.shape[1]
-    unroll = UNROLL if last else 2 * UNROLL
+    unroll = 2 * UNROLL
 
     slot = 0
     for ref, members in zip(pair_refs, pairs):
@@ -181,7 +182,7 @@
             key_t_ref[slot] = block[:, :width].T
             slot += 1
     sum_ref[...] = jnp.zeros_like(sum_ref)
-    for ref in low_refs:
+    for ref in low_refs[4:]:
         ref[...] = jnp.zeros_like(ref)
 
     def needed(head, distance):
@@ -197,8 +198,9 @@
             found = found + needed(head, distance).astype(jnp.int32)
         return found
 
-    found = lax.fori_loop(0, heads, list_head, 0)
-    steps = lax.div(found + unroll - 1, unroll)
+    found = lax.fori_loop(0, heads, list_head, 0, unroll=UNROLL)
+    padded = lax.div(found + UNROLL - 1, UNROLL) * UNROLL
+    steps = lax.div(padded, unroll)
 
     def pad_item(index, carry):
         items_ref[0, index] = 0
@@ -207,7 +209,7 @@
         items_ref[3, index] = 0
         return carry
 
-    lax.fori_loop(found, steps * unroll, pad_item, 0)
+    lax.fori_loop(found, padded, pad_item, 0)
 
     def produce(index, probs_ref, dscores_ref):
         slot, head, left = items_ref[0, index], items_ref[1, index], items_ref[2, index]
@@ -246,21 +248,27 @@
         lanes = span(step, UNROLL * width)
         return pltpu.make_async_copy(total_ref.at[:, lanes], dquery_ref.at[:, lanes], total_sems.at[step])
 
-    def some_items(step, carry):
-        for part in range(unroll):
+    def some_items(step, carry, count=unroll):
+        for part in range(count):
             index = step * unroll + part
             produce(index, *buffers[part % len(buffers)])
             consume(jnp.maximum(index - AHEAD, 0), *buffers[(part - AHEAD) % len(buffers)])
         if last:
-            pl.when(step > 0)(lambda: total_copy(step - 1).start())
+            total_copy(2 * step).start()
+            pl.when(step > 0)(lambda: total_copy(2 * step - 1).start())
         return carry
 
     lax.fori_loop(0, steps, some_items, 0)
+    if not last:
+
+        @pl.when(padded > steps * unroll)
+        def _():
+            some_items(steps, 0, UNROLL)
 
     @pl.when(found > 0)
     def _():
-        for at in range(unroll - AHEAD, unroll):
-            consume((steps - 1) * unroll + at, *buffers[at % len(buffers)])
+        for at in range(UNROLL - AHEAD, UNROLL):
+            consume(padded - UNROLL + at, *buffers[at % len(buffers)])
 
     if last:
         total_copy(heads // UNROLL - 1).start()
@@ -268,6 +276,9 @@
         grads = (sum_ref[slot, :width, :] * scale, sum_ref[slot, width:, :])
         for half, grad in enumerate(grads):
             strip = slice(half * width, (half + 1) * width)
+            for ref in other_refs:
+                other = ref[strip, rows:].astype(jnp.float32)
+                grad = grad + jnp.where(jnp.full(other.shape, device & 1, jnp.int32) == 1, 0.0, other)
             if joined:
                 out_refs[0][strip, slot * rows : (slot + 1) * rows] = grad.astype(out_refs[0].dtype)
             else:
@@ -277,7 +288,7 @@
             total_copy(step).wait()
 
 
-def block_call(pairs, pair_arrays, shared, after, parts=(), groups=(), last=False, kind=LOW, joined=False):
+def block_call(pairs, pair_arrays, shared, after, parts=(), others=(), groups=(), last=False, kind=LOW, joined=False):
     table, turned, row_terms = shared
     wide, rows = turned.shape[0] // 2, turned.shape[1]
     heads = row_terms.shape[0] // 2
@@ -287,7 +298,7 @@
     shape = jax.ShapeDtypeStruct
     outs = [shape((rows, wide) if last else (wide, rows), jnp.float32)]
     outs += [shape((2 * width, count * rows), kind)] if joined else [shape((2 * width, rows), kind)] * count
-    arrays = [turned, row_terms, *pair_arrays, *parts, after]
+    arrays = [turned, row_terms, *pair_arrays, *parts, *others, after]
     layout = (pairs, joined, last)
     return pl.pallas_call(
         functools.partial(
@@ -312,15 +323,12 @@
     )(table, *arrays)
 
 
-def join_kernel(table_ref, own_ref, other_ref, *refs, width):
+def join_kernel(*refs, width):
     key_ref, value_ref, sink_key_ref, sink_value_ref = refs[-4:]
-    rows = own_ref.shape[1]
-    odd = jnp.full(own_ref.shape, table_ref[table_ref.shape[0] - 1] & 1, jnp.int32) == 1
-    total = own_ref[...] + jnp.where(odd, 0.0, other_ref[:, rows:].astype(jnp.float32))
-    turned = (total + sum_of(refs[:4])).T
+    turned = sum_of(refs[:5]).T
     key_ref[...] = turned[:, :width]
     value_ref[...] = turned[:, width:]
-    turned = sum_of(refs[4:-4]).T
+    turned = sum_of(refs[5:-4]).T
     sink_key_ref[...] = turned[:, :width]
     sink_value_ref[...] = turned[:, width:]
 
@@ -415,7 +423,7 @@
     def fold(first, second, other, after, near):
         return pl.pallas_call(
             functools.partial(fold_kernel, near=near),
-            out_shape=(shape(first.shape, LOW),) * 2 + (shape(sink_grad.shape, jnp.float32),),
+            out_shape=(shape(first.shape, LOW),) * 2 + (shape(sink_grad.shape, full if near else LOW),),
             in_specs=[SMEM] + [VMEM] * 3 + [ANY] + [VMEM] * len(terms),
             out_specs=(VMEM,) * 3,
             compiler_params=pltpu.CompilerParams(vmem_limit_bytes=VMEM_BYTES),
@@ -431,17 +439,17 @@
     terms = sink_terms()
     backs += [rotated(grad_6, -6), rotated(grad_8, -8)]
     dquery, own_grad = block_call(
-        [(0,)], [own_held], shared, grad_8, parts=parts, kind=full, last=True,
+        [(0,)], [own_held], shared, grad_8, parts=parts, others=(far_other,), kind=full, last=True,
         groups=((2, 4), near_pair, far_pair, (6, 8)),
     )
     key_grad, value_grad, sink_key_grad, sink_value_grad = pl.pallas_call(
         functools.partial(join_kernel, width=width),
         out_shape=(shape((rows, width), jnp.float32),) * 2 + (shape((sinks, width), jnp.float32),) * 2,
-        in_specs=[SMEM] + [VMEM] * (6 + len(terms)),
+        in_specs=[VMEM] * (5 + len(terms)),
         out_specs=(VMEM,) * 4,
         compiler_params=pltpu.CompilerParams(vmem_limit_bytes=VMEM_BYTES),
         name="join",
-    )(table, own_grad, far_other, *backs, *terms)
+    )(own_grad, *backs, *terms)
     return (dquery, key_grad, value_grad, sink_key_grad, sink_value_grad)
 
 

time: 59.9 us -> 58.9 us (0.983)
  Pallas kernels: 17.1 us -> 15.7 us
  starting transfers between devices: 29.4 us -> 30 us
    ppermute x9, starting transfers between devices: 16.2 us -> 17.1 us  [swapped(): return lax.ppermute(block, AXES, route)]
    pallas_call x5, Pallas kernels: 9.86 us -> 9 us  [block_call(): pl.pallas_call(functools.partial(block_kernel, layout=layout, groups=grou...]
    ppermute x9, waiting for transfers between devices: 9.54 us -> 8.9 us  [swapped(): return lax.ppermute(block, AXES, route)]
  transfers between devices with their start and end apart: 17 -> 17, of which waited for: 5 -> 5; matrix products, arithmetic and copies ran while one was open for 0% -> 0% of each run, Pallas kernels for 26% -> 25%
where the time goes in v5:
time: 58.9 us; the launch traced here: 58.7 us
  starting transfers between devices  30 us (51%)
  Pallas kernels  15.7 us (27%)
  waiting for transfers between devices  9.99 us (17%)
  local copies, waits for them, and re-layouts  1.28 us (2%)
  between operations  0.92 us (2%)
  other arithmetic  0.89 us (2%)
    ppermute x9, starting transfers between devices, swapped(): return lax.ppermute(block, AXES, route)  17.1 us
    ppermute x8, starting transfers between devices, rotated(): lax.ppermute(block, AXES, [(i, (i + distance) % count) for i in range(cou...  12.8 us
    pallas_call x5, Pallas kernels, block_call(): pl.pallas_call(functools.partial(block_kernel, layout=layout, groups=grou...  9 us
    ppermute x9, waiting for transfers between devices, swapped(): return lax.ppermute(block, AXES, route)  8.9 us
    pallas_call x1, Pallas kernels, on_device(): pl.pallas_call(functools.partial(sink_kernel, heads=heads, width=width, s...  3.99 us
    unnamed x20, local copies, waits for them, and re-layouts  1.28 us
    pallas_call x2, Pallas kernels, fold(): pl.pallas_call(functools.partial(fold_kernel, near=near), out_shape=(shap...  1.2 us
  transfers between devices with their start and end apart: 17, of which 5 were waited for; matrix products, arithmetic and copies ran while one was open for 0% of the time, Pallas kernels for 25%

profile of v5, /device:TPU:0, one launch (start us, length us, event | category | flops | bytes accessed | tf_op | source)
XLA Modules:
  0.0 58.7 jit_solution(10395004274930638802)
XLA Ops:
  0.6 0.9 %pad_maximum_fusion.block_ref = bf16[256,256]{1,0:T(8,128)(2,1)S(1)} fusion(bf16[256,128]{1,0:T(8,128)(2,1)} %value_ref.1, bf16[256,128]{1,0:T(8,128)(2,1)} %key_ref.1), kind=kLoop, calls=%fused_computation | loop fusion | flops 262144 | bytes 262144 | tf_op jit(solution)/shard_map/concatenate | solution.py:346
  1.6 4.1 %collective-permute-start.1 = (bf16[256,256]{1,0:T(8,128)(2,1)S(1)}, bf16[256,256]{1,0:T(8,128)(2,1)S(1)}, u32[]{:S(2)}, u32[]{:S(2)}) collective-permute-start(bf16[256,256]{1,0:T(8,128)(2,1)S(1)} %mark.1), channel_id=1, source_target_pairs={{0,4},{1,5},{2,6},{3,7},{4,8},{5,9},{6,10},{7,11},{8,12},{9,13},{1... | collective-permute-start | bytes 393224 | tf_op jit(solution)/shard_map/ppermute | solution.py:32
  5.7 1.6 %collective-permute-start = (bf16[256,256]{1,0:T(8,128)(2,1)S(1)}, bf16[256,256]{1,0:T(8,128)(2,1)S(1)}, u32[]{:S(2)}, u32[]{:S(2)}) collective-permute-start(bf16[256,256]{1,0:T(8,128)(2,1)S(1)} %mark.1), channel_id=1, source_target_pairs={{0,2},{1,3},{2,4},{3,5},{4,6},{5,7},{6,8},{7,9},{8,10},{9,11},{10,... | collective-permute-start | bytes 393224 | tf_op jit(solution)/shard_map/ppermute | solution.py:32
  7.4 1.2 %copy-done.4 = bf16[256,2048]{1,0:T(8,128)(2,1)S(1)} copy-done((bf16[256,2048]{1,0:T(8,128)(2,1)S(1)}, bf16[256,2048]{1,0:T(8,128)(2,1)}, u32[]{:S(2)}) %copy-start.4) | copy-done | bytes 1048600
  8.6 4.0 %sink_keys_part.1 = (s32[17]{0:T(128)S(1)}, bf16[4096,256]{1,0:T(8,128)(2,1)S(1)}, f32[32,256]{1,0:T(8,128)S(1)}, f32[2048,256]{1,0:T(8,128)S(1)}, f32[256,128]{1,0:T(8,128)S(1)}, /*index=5*/bf16[256,256]{1,0:T(8,128)(2,1)S(1)}) custom-call(s32[16]{0:T(128)S(1)} %copy-done.8, s32[16]{0:T(128)S(1)} %copy-done.9, s32[1]{0:T(128)} %bitcast.device_ref, ...), custom_call_target="tpu_custom_call" | custom-call | flops 10000000000 | bytes 1000000 | tf_op jit(solution)/shard_map/sink_keys_part/pallas_call | solution.py:359
  13.2 2.8 %collective-permute-start.4 = (bf16[256,256]{1,0:T(8,128)(2,1)S(1)}, bf16[256,256]{1,0:T(8,128)(2,1)S(1)}, u32[]{:S(2)}, u32[]{:S(2)}) collective-permute-start(bf16[256,256]{1,0:T(8,128)(2,1)S(1)} %get-tuple-element.40.own_ref.refs_3_), channel_id=1, source_target_pairs={{0,6},{1,7},{2,8},{3,9},{4,10},{5,11},{6,12},{7,13},{8,14},{9,15},... | collective-permute-start | bytes 393224 | tf_op jit(solution)/shard_map/ppermute | solution.py:32
  16.2 1.6 %collective-permute-start.3 = (bf16[512,256]{1,0:T(8,128)(2,1)S(1)}, bf16[512,256]{1,0:T(8,128)(2,1)S(1)}, u32[]{:S(2)}, u32[]{:S(2)}) collective-permute-start(bf16[512,256]{1,0:T(8,128)(2,1)S(1)} %get-tuple-element.43.refs_5_), channel_id=1, source_target_pairs={{0,1},{1,0},{2,3},{3,2},{4,5},{5,4},{6,7},{7,6},{8,9},{9,8},{10,11... | collective-permute-start | bytes 786440 | tf_op jit(solution)/shard_map/ppermute | solution.py:44
  17.8 0.9 %blocks_2_4.1 = (f32[2048,256]{1,0:T(8,128)S(1)}, f32[256,256]{1,0:T(8,128)S(1)}, f32[256,256]{1,0:T(8,128)S(1)}) custom-call(s32[17]{0:T(128)S(1)} %get-tuple-element.37.refs_0_.table_ref, bf16[4096,256]{1,0:T(8,128)(2,1)S(1)} %get-tuple-element.38.refs_1_, f32[32,256]{1,0:T(8,128)S(1)} %get-tuple-element.39.refs_2_, ...), custom_call_target="tpu_custom_call" | custom-call | flops 2684354560 | bytes 1048576 | tf_op jit(solution)/shard_map/blocks_2_4/pallas_call | solution.py:303
  18.8 1.1 %collective-permute-done.4.six_ref.refs_3_ = bf16[256,256]{1,0:T(8,128)(2,1)S(1)} collective-permute-done((bf16[256,256]{1,0:T(8,128)(2,1)S(1)}, bf16[256,256]{1,0:T(8,128)(2,1)S(1)}, u32[]{:S(2)}, u32[]{:S(2)}) %collective-permute-start.4) | collective-permute-done | bytes 131104 | tf_op jit(solution)/shard_map/ppermute | solution.py:32
  19.8 2.9 %collective-permute-done.6.refs_1_ = f32[256,128]{1,0:T(8,128)S(1)} collective-permute-done((f32[256,128]{1,0:T(8,128)S(1)}, f32[256,128]{1,0:T(8,128)S(1)}, u32[]{:S(2)}, u32[]{:S(2)}) %collective-permute-start.6) | collective-permute-done | bytes 131104 | tf_op jit(solution)/shard_map/ppermute | solution.py:44
  23.3 1.6 %collective-permute-start.7 = (bf16[512,256]{1,0:T(8,128)(2,1)S(1)}, bf16[512,256]{1,0:T(8,128)(2,1)S(1)}, u32[]{:S(2)}, u32[]{:S(2)}) collective-permute-start(bf16[512,256]{1,0:T(8,128)(2,1)S(1)} %get-tuple-element.46.refs_4_), channel_id=1, source_target_pairs={{0,1},{1,0},{2,3},{3,2},{4,5},{5,4},{6,7},{7,6},{8,9},{9,8},{10,11... | collective-permute-start | bytes 786440 | tf_op jit(solution)/shard_map/ppermute | solution.py:44
  24.9 0.9 %blocks_1_3.1 = (f32[2048,256]{1,0:T(8,128)S(1)}, bf16[256,512]{1,0:T(8,128)(2,1)S(1)}) custom-call(s32[17]{0:T(128)S(1)} %get-tuple-element.37.refs_0_.table_ref, bf16[4096,256]{1,0:T(8,128)(2,1)S(1)} %get-tuple-element.38.refs_1_, f32[32,256]{1,0:T(8,128)S(1)} %get-tuple-element.39.refs_2_, bf16[512,256]{1,0:T(8,128)(2,1)S(1)} %collective-permute-done.3.refs_3_, ...), custom_call_target="tpu_custom_call" | custom-call | flops 2684354560 | bytes 1048576 | tf_op jit(solution)/shard_map/blocks_1_3/pallas_call | solution.py:303
  25.8 1.4 %collective-permute-start.8 = (bf16[256,512]{1,0:T(8,128)(2,1)S(1)}, bf16[256,512]{1,0:T(8,128)(2,1)S(1)}, u32[]{:S(2)}, u32[]{:S(2)}) collective-permute-start(bf16[256,512]{1,0:T(8,128)(2,1)S(1)} %get-tuple-element.51), channel_id=1, source_target_pairs={{0,1},{1,0},{2,3},{3,2},{4,5},{5,4},{6,7},{7,6},{8,9},{9,8},{10,11... | collective-permute-start | bytes 786440 | tf_op jit(solution)/shard_map/ppermute | solution.py:44
  27.2 5.7 %collective-permute-start.9 = (f32[256,128]{1,0:T(8,128)S(1)}, f32[256,128]{1,0:T(8,128)S(1)}, u32[]{:S(2)}, u32[]{:S(2)}) collective-permute-start(f32[256,128]{1,0:T(8,128)S(1)} %get-tuple-element.53.refs_0_), channel_id=1, source_target_pairs={{0,4},{1,5},{2,6},{3,7},{4,0},{5,1},{6,2},{7,3},{8,12},{9,13},{10,... | collective-permute-start | bytes 393224 | tf_op jit(solution)/shard_map/ppermute | solution.py:44
  32.9 0.9 %blocks_5_7.1 = (f32[2048,256]{1,0:T(8,128)S(1)}, bf16[256,512]{1,0:T(8,128)(2,1)S(1)}) custom-call(s32[17]{0:T(128)S(1)} %get-tuple-element.37.refs_0_.table_ref, bf16[4096,256]{1,0:T(8,128)(2,1)S(1)} %get-tuple-element.38.refs_1_, f32[32,256]{1,0:T(8,128)S(1)} %get-tuple-element.39.refs_2_, bf16[512,256]{1,0:T(8,128)(2,1)S(1)} %collective-permute-done.7.refs_3_, ...), custom_call_target="tpu_custom_call" | custom-call | flops 2684354560 | bytes 1048576 | tf_op jit(solution)/shard_map/blocks_5_7/pallas_call | solution.py:303
  33.9 4.5 %collective-permute-start.10 = (bf16[256,512]{1,0:T(8,128)(2,1)S(1)}, bf16[256,512]{1,0:T(8,128)(2,1)S(1)}, u32[]{:S(2)}, u32[]{:S(2)}) collective-permute-start(bf16[256,512]{1,0:T(8,128)(2,1)S(1)} %get-tuple-element.52.after_ref), channel_id=1, source_target_pairs={{0,1},{1,0},{2,3},{3,2},{4,5},{5,4},{6,7},{7,6},{8,9},{9,8},{10,11... | collective-permute-start | bytes 786440 | tf_op jit(solution)/shard_map/ppermute | solution.py:44
  38.3 1.7 %collective-permute-done.9.refs_1_ = f32[256,128]{1,0:T(8,128)S(1)} collective-permute-done((f32[256,128]{1,0:T(8,128)S(1)}, f32[256,128]{1,0:T(8,128)S(1)}, u32[]{:S(2)}, u32[]{:S(2)}) %collective-permute-start.9) | collective-permute-done | bytes 131104 | tf_op jit(solution)/shard_map/ppermute | solution.py:44
  40.7 2.4 %collective-permute-start.12 = (bf16[256,256]{1,0:T(8,128)(2,1)S(1)}, bf16[256,256]{1,0:T(8,128)(2,1)S(1)}, u32[]{:S(2)}, u32[]{:S(2)}) collective-permute-start(bf16[256,256]{1,0:T(8,128)(2,1)S(1)} %get-tuple-element.62), channel_id=1, source_target_pairs={{0,30},{1,31},{2,0},{3,1},{4,2},{5,3},{6,4},{7,5},{8,6},{9,7},{10,... | collective-permute-start | bytes 393224 | tf_op jit(solution)/shard_map/ppermute | solution.py:32
  43.6 0.9 %blocks_6_8.1 = (f32[2048,256]{1,0:T(8,128)S(1)}, f32[256,256]{1,0:T(8,128)S(1)}, f32[256,256]{1,0:T(8,128)S(1)}) custom-call(s32[17]{0:T(128)S(1)} %get-tuple-element.37.refs_0_.table_ref, bf16[4096,256]{1,0:T(8,128)(2,1)S(1)} %get-tuple-element.38.refs_1_, f32[32,256]{1,0:T(8,128)S(1)} %get-tuple-element.39.refs_2_, ...), custom_call_target="tpu_custom_call" | custom-call | flops 2684354560 | bytes 1048576 | tf_op jit(solution)/shard_map/blocks_6_8/pallas_call | solution.py:303
  44.5 0.9 %collective-permute-done.10.other_ref.refs_9_ = bf16[256,512]{1,0:T(8,128)(2,1)S(1)} collective-permute-done((bf16[256,512]{1,0:T(8,128)(2,1)S(1)}, bf16[256,512]{1,0:T(8,128)(2,1)S(1)}, u32[]{:S(2)}, u32[]{:S(2)}) %collective-permute-start.10) | collective-permute-done | bytes 262176 | tf_op jit(solution)/shard_map/ppermute | solution.py:44
  45.4 3.4 %collective-permute-done.11.refs_1_ = f32[256,128]{1,0:T(8,128)S(1)} collective-permute-done((f32[256,128]{1,0:T(8,128)S(1)}, f32[256,128]{1,0:T(8,128)S(1)}, u32[]{:S(2)}, u32[]{:S(2)}) %collective-permute-start.11) | collective-permute-done | bytes 131104 | tf_op jit(solution)/shard_map/ppermute | solution.py:44
  50.8 1.7 %collective-permute-start.16 = (bf16[256,128]{1,0:T(8,128)(2,1)S(1)}, bf16[256,128]{1,0:T(8,128)(2,1)S(1)}, u32[]{:S(2)}, u32[]{:S(2)}) collective-permute-start(bf16[256,128]{1,0:T(8,128)(2,1)S(1)} %get-tuple-element.64.refs_5_), channel_id=1, source_target_pairs={{0,1},{1,0},{2,3},{3,2},{4,5},{5,4},{6,7},{7,6},{8,9},{9,8},{10,11... | collective-permute-start | bytes 196616 | tf_op jit(solution)/shard_map/ppermute | solution.py:44
  52.5 5.3 %blocks_0.1 = (f32[256,2048]{1,0:T(8,128)}, f32[256,256]{1,0:T(8,128)S(1)}) custom-call(s32[17]{0:T(128)S(1)} %get-tuple-element.37.refs_0_.table_ref, bf16[4096,256]{1,0:T(8,128)(2,1)S(1)} %get-tuple-element.38.refs_1_, f32[32,256]{1,0:T(8,128)S(1)} %get-tuple-element.39.refs_2_, bf16[256,256]{1,0:T(8,128)(2,1)S(1)} %get-tuple-element.40.own_ref.refs_3_, ...), custom_call_target="tpu_custom_call" | custom-call | flops 1342177280 | bytes 1048576 | tf_op jit(solution)/shard_map/blocks_0/pallas_call | solution.py:303
  57.8 0.9 %join.1 = (f32[256,128]{1,0:T(8,128)}, f32[256,128]{1,0:T(8,128)}, f32[128,128]{1,0:T(8,128)}, f32[128,128]{1,0:T(8,128)}) custom-call(f32[256,256]{1,0:T(8,128)S(1)} %get-tuple-element.61.refs_0_, bf16[256,256]{1,0:T(8,128)(2,1)S(1)} %collective-permute-done.12.refs_1_, bf16[256,256]{1,0:T(8,128)(2,1)S(1)} %collective-permute-done.13.refs_2_, ...), custom_call_target="tpu_custom_call" | custom-call | tf_op jit(solution)/shard_map/join/pallas_call | solution.py:445
  (43 shorter events, 4.4 us)
Async XLA Ops:
  1.5 5.8 %copy-start = (bf16[256,128]{1,0:T(8,128)(2,1)S(1)}, bf16[256,128]{1,0:T(8,128)(2,1)}, u32[]{:S(2)}) copy-start(bf16[256,128]{1,0:T(8,128)(2,1)} %key_ref.1) | copy-start | bytes 196612
  1.5 5.8 %copy-start.1 = (bf16[256,128]{1,0:T(8,128)(2,1)S(1)}, bf16[256,128]{1,0:T(8,128)(2,1)}, u32[]{:S(2)}) copy-start(bf16[256,128]{1,0:T(8,128)(2,1)} %value_ref.1) | copy-start | bytes 196612
  1.5 5.8 %copy-start.2 = (bf16[256,2048]{1,0:T(8,128)(2,1)S(1)}, bf16[256,2048]{1,0:T(8,128)(2,1)}, u32[]{:S(2)}) copy-start(bf16[256,2048]{1,0:T(8,128)(2,1)} %query_ref.1) | copy-start | bytes 3145732
  1.6 5.8 %copy-start.3 = (bf16[256,2048]{1,0:T(8,128)(2,1)S(1)}, bf16[256,2048]{1,0:T(8,128)(2,1)}, u32[]{:S(2)}) copy-start(bf16[256,2048]{1,0:T(8,128)(2,1)} %grad_ref.1) | copy-start | bytes 3145732
  1.6 5.8 %copy-start.5 = (bf16[128,128]{1,0:T(8,128)(2,1)S(1)}, bf16[128,128]{1,0:T(8,128)(2,1)}, u32[]{:S(2)}) copy-start(bf16[128,128]{1,0:T(8,128)(2,1)} %sink_key_ref.1) | copy-start | bytes 98308
  1.6 5.8 %copy-start.6 = (bf16[128,128]{1,0:T(8,128)(2,1)S(1)}, bf16[128,128]{1,0:T(8,128)(2,1)}, u32[]{:S(2)}) copy-start(bf16[128,128]{1,0:T(8,128)(2,1)} %sink_value_ref.1) | copy-start | bytes 98308
  1.6 5.8 %copy-start.7 = (f32[16,256]{1,0:T(8,128)S(1)}, f32[16,256]{1,0:T(8,128)}, u32[]{:S(2)}) copy-start(f32[16,256]{1,0:T(8,128)} %lse_in.1) | copy-start | bytes 49156
  1.6 14.4 %collective-permute-start.1 = (bf16[256,256]{1,0:T(8,128)(2,1)S(1)}, bf16[256,256]{1,0:T(8,128)(2,1)S(1)}, u32[]{:S(2)}, u32[]{:S(2)}) collective-permute-start(bf16[256,256]{1,0:T(8,128)(2,1)S(1)} %mark.1), channel_id=1, source_target_pairs={{0,4},{1,5},{2,6},{3,7},{4,8},{5,9},{6,10},{7,11},{8,12},{9,13},{1... | collective-permute-start | bytes 393224 | tf_op jit(solution)/shard_map/ppermute | solution.py:32
  5.7 10.3 %collective-permute-start = (bf16[256,256]{1,0:T(8,128)(2,1)S(1)}, bf16[256,256]{1,0:T(8,128)(2,1)S(1)}, u32[]{:S(2)}, u32[]{:S(2)}) collective-permute-start(bf16[256,256]{1,0:T(8,128)(2,1)S(1)} %mark.1), channel_id=1, source_target_pairs={{0,2},{1,3},{2,4},{3,5},{4,6},{5,7},{6,8},{7,9},{8,10},{9,11},{10,... | collective-permute-start | bytes 393224 | tf_op jit(solution)/shard_map/ppermute | solution.py:32
  12.6 3.4 %collective-permute-start.2 = (f32[256,128]{1,0:T(8,128)S(1)}, f32[256,128]{1,0:T(8,128)S(1)}, u32[]{:S(2)}, u32[]{:S(2)}) collective-permute-start(f32[256,128]{1,0:T(8,128)S(1)} %get-tuple-element.42.refs_0_), channel_id=1, source_target_pairs={{0,8},{1,9},{2,10},{3,11},{4,12},{5,13},{6,14},{7,15},{8,0},{9,1},... | collective-permute-start | bytes 393224 | tf_op jit(solution)/shard_map/ppermute | solution.py:44
  12.7 6.1 %collective-permute-start.5 = (bf16[256,256]{1,0:T(8,128)(2,1)S(1)}, bf16[256,256]{1,0:T(8,128)(2,1)S(1)}, u32[]{:S(2)}, u32[]{:S(2)}) collective-permute-start(bf16[256,256]{1,0:T(8,128)(2,1)S(1)} %get-tuple-element.40.own_ref.refs_3_), channel_id=1, source_target_pairs={{0,8},{1,9},{2,10},{3,11},{4,12},{5,13},{6,14},{7,15},{8,16},{9,17... | collective-permute-start | bytes 393224 | tf_op jit(solution)/shard_map/ppermute | solution.py:32
  13.2 6.6 %collective-permute-start.4 = (bf16[256,256]{1,0:T(8,128)(2,1)S(1)}, bf16[256,256]{1,0:T(8,128)(2,1)S(1)}, u32[]{:S(2)}, u32[]{:S(2)}) collective-permute-start(bf16[256,256]{1,0:T(8,128)(2,1)S(1)} %get-tuple-element.40.own_ref.refs_3_), channel_id=1, source_target_pairs={{0,6},{1,7},{2,8},{3,9},{4,10},{5,11},{6,12},{7,13},{8,14},{9,15},... | collective-permute-start | bytes 393224 | tf_op jit(solution)/shard_map/ppermute | solution.py:32
  16.1 6.6 %collective-permute-start.6 = (f32[256,128]{1,0:T(8,128)S(1)}, f32[256,128]{1,0:T(8,128)S(1)}, u32[]{:S(2)}, u32[]{:S(2)}) collective-permute-start(f32[256,128]{1,0:T(8,128)S(1)} %get-tuple-element.45.refs_0_), channel_id=1, source_target_pairs={{0,2},{1,3},{2,0},{3,1},{4,6},{5,7},{6,4},{7,5},{8,10},{9,11},{10,... | collective-permute-start | bytes 393224 | tf_op jit(solution)/shard_map/ppermute | solution.py:44
  16.2 8.7 %collective-permute-start.3 = (bf16[512,256]{1,0:T(8,128)(2,1)S(1)}, bf16[512,256]{1,0:T(8,128)(2,1)S(1)}, u32[]{:S(2)}, u32[]{:S(2)}) collective-permute-start(bf16[512,256]{1,0:T(8,128)(2,1)S(1)} %get-tuple-element.43.refs_5_), channel_id=1, source_target_pairs={{0,1},{1,0},{2,3},{3,2},{4,5},{5,4},{6,7},{7,6},{8,9},{9,8},{10,11... | collective-permute-start | bytes 786440 | tf_op jit(solution)/shard_map/ppermute | solution.py:44
  23.3 9.6 %collective-permute-start.7 = (bf16[512,256]{1,0:T(8,128)(2,1)S(1)}, bf16[512,256]{1,0:T(8,128)(2,1)S(1)}, u32[]{:S(2)}, u32[]{:S(2)}) collective-permute-start(bf16[512,256]{1,0:T(8,128)(2,1)S(1)} %get-tuple-element.46.refs_4_), channel_id=1, source_target_pairs={{0,1},{1,0},{2,3},{3,2},{4,5},{5,4},{6,7},{7,6},{8,9},{9,8},{10,11... | collective-permute-start | bytes 786440 | tf_op jit(solution)/shard_map/ppermute | solution.py:44
  25.8 14.2 %collective-permute-start.8 = (bf16[256,512]{1,0:T(8,128)(2,1)S(1)}, bf16[256,512]{1,0:T(8,128)(2,1)S(1)}, u32[]{:S(2)}, u32[]{:S(2)}) collective-permute-start(bf16[256,512]{1,0:T(8,128)(2,1)S(1)} %get-tuple-element.51), channel_id=1, source_target_pairs={{0,1},{1,0},{2,3},{3,2},{4,5},{5,4},{6,7},{7,6},{8,9},{9,8},{10,11... | collective-permute-start | bytes 786440 | tf_op jit(solution)/shard_map/ppermute | solution.py:44
  27.2 12.8 %collective-permute-start.9 = (f32[256,128]{1,0:T(8,128)S(1)}, f32[256,128]{1,0:T(8,128)S(1)}, u32[]{:S(2)}, u32[]{:S(2)}) collective-permute-start(f32[256,128]{1,0:T(8,128)S(1)} %get-tuple-element.53.refs_0_), channel_id=1, source_target_pairs={{0,4},{1,5},{2,6},{3,7},{4,0},{5,1},{6,2},{7,3},{8,12},{9,13},{10,... | collective-permute-start | bytes 393224 | tf_op jit(solution)/shard_map/ppermute | solution.py:44
  33.9 11.5 %collective-permute-start.10 = (bf16[256,512]{1,0:T(8,128)(2,1)S(1)}, bf16[256,512]{1,0:T(8,128)(2,1)S(1)}, u32[]{:S(2)}, u32[]{:S(2)}) collective-permute-start(bf16[256,512]{1,0:T(8,128)(2,1)S(1)} %get-tuple-element.52.after_ref), channel_id=1, source_target_pairs={{0,1},{1,0},{2,3},{3,2},{4,5},{5,4},{6,7},{7,6},{8,9},{9,8},{10,11... | collective-permute-start | bytes 786440 | tf_op jit(solution)/shard_map/ppermute | solution.py:44
  40.7 17.1 %collective-permute-start.12 = (bf16[256,256]{1,0:T(8,128)(2,1)S(1)}, bf16[256,256]{1,0:T(8,128)(2,1)S(1)}, u32[]{:S(2)}, u32[]{:S(2)}) collective-permute-start(bf16[256,256]{1,0:T(8,128)(2,1)S(1)} %get-tuple-element.62), channel_id=1, source_target_pairs={{0,30},{1,31},{2,0},{3,1},{4,2},{5,3},{6,4},{7,5},{8,6},{9,7},{10,... | collective-permute-start | bytes 393224 | tf_op jit(solution)/shard_map/ppermute | solution.py:32
  43.1 14.7 %collective-permute-start.13 = (bf16[256,256]{1,0:T(8,128)(2,1)S(1)}, bf16[256,256]{1,0:T(8,128)(2,1)S(1)}, u32[]{:S(2)}, u32[]{:S(2)}) collective-permute-start(bf16[256,256]{1,0:T(8,128)(2,1)S(1)} %get-tuple-element.54.refs_5_), channel_id=1, source_target_pairs={{0,28},{1,29},{2,30},{3,31},{4,0},{5,1},{6,2},{7,3},{8,4},{9,5},{1... | collective-permute-start | bytes 393224 | tf_op jit(solution)/shard_map/ppermute | solution.py:32
  43.1 5.7 %collective-permute-start.11 = (f32[256,128]{1,0:T(8,128)S(1)}, f32[256,128]{1,0:T(8,128)S(1)}, u32[]{:S(2)}, u32[]{:S(2)}) collective-permute-start(f32[256,128]{1,0:T(8,128)S(1)} %get-tuple-element.58.refs_0_), channel_id=1, source_target_pairs={{0,16},{1,17},{2,18},{3,19},{4,20},{5,21},{6,22},{7,23},{8,24},{9,... | collective-permute-start | bytes 393224 | tf_op jit(solution)/shard_map/ppermute | solution.py:44
  49.4 8.4 %collective-permute-start.14 = (bf16[256,256]{1,0:T(8,128)(2,1)S(1)}, bf16[256,256]{1,0:T(8,128)(2,1)S(1)}, u32[]{:S(2)}, u32[]{:S(2)}) collective-permute-start(bf16[256,256]{1,0:T(8,128)(2,1)S(1)} %get-tuple-element.63), channel_id=1, source_target_pairs={{0,26},{1,27},{2,28},{3,29},{4,30},{5,31},{6,0},{7,1},{8,2},{9,3},... | collective-permute-start | bytes 393224 | tf_op jit(solution)/shard_map/ppermute | solution.py:32
  50.1 7.8 %collective-permute-start.15 = (bf16[256,256]{1,0:T(8,128)(2,1)S(1)}, bf16[256,256]{1,0:T(8,128)(2,1)S(1)}, u32[]{:S(2)}, u32[]{:S(2)}) collective-permute-start(bf16[256,256]{1,0:T(8,128)(2,1)S(1)} %get-tuple-element.59.refs_10_), channel_id=1, source_target_pairs={{0,24},{1,25},{2,26},{3,27},{4,28},{5,29},{6,30},{7,31},{8,0},{9,1... | collective-permute-start | bytes 393224 | tf_op jit(solution)/shard_map/ppermute | solution.py:32
  50.8 7.0 %collective-permute-start.16 = (bf16[256,128]{1,0:T(8,128)(2,1)S(1)}, bf16[256,128]{1,0:T(8,128)(2,1)S(1)}, u32[]{:S(2)}, u32[]{:S(2)}) collective-permute-start(bf16[256,128]{1,0:T(8,128)(2,1)S(1)} %get-tuple-element.64.refs_5_), channel_id=1, source_target_pairs={{0,1},{1,0},{2,3},{3,2},{4,5},{5,4},{6,7},{7,6},{8,9},{9,8},{10,11... | collective-permute-start | bytes 196616 | tf_op jit(solution)/shard_map/ppermute | solution.py:44
  (3 other events, 12.7 us)

commit v6 on v5

--- a/solution.py
+++ b/solution.py
@@ -423,7 +423,7 @@
     def fold(first, second, other, after, near):
         return pl.pallas_call(
             functools.partial(fold_kernel, near=near),
-            out_shape=(shape(first.shape, LOW),) * 2 + (shape(sink_grad.shape, full if near else LOW),),
+            out_shape=(shape(first.shape, LOW),) * 2 + (shape(sink_grad.shape, LOW),),
             in_specs=[SMEM] + [VMEM] * 3 + [ANY] + [VMEM] * len(terms),
             out_specs=(VMEM,) * 3,
             compiler_params=pltpu.CompilerParams(vmem_limit_bytes=VMEM_BYTES),

time: 58.9 us -> 57.2 us (0.971)
  waiting for transfers between devices: 9.99 us -> 8.01 us
  starting transfers between devices: 30 us -> 30.6 us
    ppermute x9, waiting for transfers between devices: 8.9 us -> 6.29 us  [swapped(): return lax.ppermute(block, AXES, route)]
    ppermute x8, waiting for transfers between devices: 1.09 us -> 1.72 us  [rotated(): lax.ppermute(block, AXES, [(i, (i + distance) % count) for i in range(cou...]
  transfers between devices with their start and end apart: 17 -> 17, of which waited for: 5 -> 5; matrix products, arithmetic and copies ran while one was open for 0% -> 0% of each run, Pallas kernels for 25% -> 26%
where the time goes in v6:
time: 57.2 us; the launch traced here: 57.3 us
  starting transfers between devices  30.6 us (53%)
  Pallas kernels  15.7 us (27%)
  waiting for transfers between devices  8.01 us (14%)
  local copies, waits for them, and re-layouts  1.28 us (2%)
  other arithmetic  0.89 us (2%)
  between operations  0.88 us (2%)
    ppermute x9, starting transfers between devices, swapped(): return lax.ppermute(block, AXES, route)  17.2 us
    ppermute x8, starting transfers between devices, rotated(): lax.ppermute(block, AXES, [(i, (i + distance) % count) for i in range(cou...  13.3 us
    pallas_call x5, Pallas kernels, block_call(): pl.pallas_call(functools.partial(block_kernel, layout=layout, groups=grou...  9 us
    ppermute x9, waiting for transfers between devices, swapped(): return lax.ppermute(block, AXES, route)  6.29 us
    pallas_call x1, Pallas kernels, on_device(): pl.pallas_call(functools.partial(sink_kernel, heads=heads, width=width, s...  3.99 us
    ppermute x8, waiting for transfers between devices, rotated(): lax.ppermute(block, AXES, [(i, (i + distance) % count) for i in range(cou...  1.72 us
    unnamed x20, local copies, waits for them, and re-layouts  1.28 us
    pallas_call x2, Pallas kernels, fold(): pl.pallas_call(functools.partial(fold_kernel, near=near), out_shape=(shap...  1.2 us
  transfers between devices with their start and end apart: 17, of which 5 were waited for; matrix products, arithmetic and copies ran while one was open for 0% of the time, Pallas kernels for 26%

profile of v6, /device:TPU:0, one launch (start us, length us, event | category | flops | bytes accessed | tf_op | source)
XLA Modules:
  0.0 57.3 jit_solution(15803513245534311931)
XLA Ops:
  0.6 0.9 %pad_maximum_fusion.block_ref = bf16[256,256]{1,0:T(8,128)(2,1)S(1)} fusion(bf16[256,128]{1,0:T(8,128)(2,1)} %value_ref.1, bf16[256,128]{1,0:T(8,128)(2,1)} %key_ref.1), kind=kLoop, calls=%fused_computation | loop fusion | flops 262144 | bytes 262144 | tf_op jit(solution)/shard_map/concatenate | solution.py:346
  1.6 4.1 %collective-permute-start.1 = (bf16[256,256]{1,0:T(8,128)(2,1)S(1)}, bf16[256,256]{1,0:T(8,128)(2,1)S(1)}, u32[]{:S(2)}, u32[]{:S(2)}) collective-permute-start(bf16[256,256]{1,0:T(8,128)(2,1)S(1)} %mark.1), channel_id=1, source_target_pairs={{0,4},{1,5},{2,6},{3,7},{4,8},{5,9},{6,10},{7,11},{8,12},{9,13},{1... | collective-permute-start | bytes 393224 | tf_op jit(solution)/shard_map/ppermute | solution.py:32
  5.7 1.6 %collective-permute-start = (bf16[256,256]{1,0:T(8,128)(2,1)S(1)}, bf16[256,256]{1,0:T(8,128)(2,1)S(1)}, u32[]{:S(2)}, u32[]{:S(2)}) collective-permute-start(bf16[256,256]{1,0:T(8,128)(2,1)S(1)} %mark.1), channel_id=1, source_target_pairs={{0,2},{1,3},{2,4},{3,5},{4,6},{5,7},{6,8},{7,9},{8,10},{9,11},{10,... | collective-permute-start | bytes 393224 | tf_op jit(solution)/shard_map/ppermute | solution.py:32
  7.4 1.2 %copy-done.4 = bf16[256,2048]{1,0:T(8,128)(2,1)S(1)} copy-done((bf16[256,2048]{1,0:T(8,128)(2,1)S(1)}, bf16[256,2048]{1,0:T(8,128)(2,1)}, u32[]{:S(2)}) %copy-start.4) | copy-done | bytes 1048600
  8.6 4.0 %sink_keys_part.1 = (s32[17]{0:T(128)S(1)}, bf16[4096,256]{1,0:T(8,128)(2,1)S(1)}, f32[32,256]{1,0:T(8,128)S(1)}, f32[2048,256]{1,0:T(8,128)S(1)}, f32[256,128]{1,0:T(8,128)S(1)}, /*index=5*/bf16[256,256]{1,0:T(8,128)(2,1)S(1)}) custom-call(s32[16]{0:T(128)S(1)} %copy-done.8, s32[16]{0:T(128)S(1)} %copy-done.9, s32[1]{0:T(128)} %bitcast.device_ref, ...), custom_call_target="tpu_custom_call" | custom-call | flops 10000000000 | bytes 1000000 | tf_op jit(solution)/shard_map/sink_keys_part/pallas_call | solution.py:359
  13.2 2.8 %collective-permute-start.4 = (bf16[256,256]{1,0:T(8,128)(2,1)S(1)}, bf16[256,256]{1,0:T(8,128)(2,1)S(1)}, u32[]{:S(2)}, u32[]{:S(2)}) collective-permute-start(bf16[256,256]{1,0:T(8,128)(2,1)S(1)} %get-tuple-element.40.own_ref.refs_3_), channel_id=1, source_target_pairs={{0,6},{1,7},{2,8},{3,9},{4,10},{5,11},{6,12},{7,13},{8,14},{9,15},... | collective-permute-start | bytes 393224 | tf_op jit(solution)/shard_map/ppermute | solution.py:32
  16.1 1.6 %collective-permute-start.3 = (bf16[512,256]{1,0:T(8,128)(2,1)S(1)}, bf16[512,256]{1,0:T(8,128)(2,1)S(1)}, u32[]{:S(2)}, u32[]{:S(2)}) collective-permute-start(bf16[512,256]{1,0:T(8,128)(2,1)S(1)} %get-tuple-element.43.refs_5_), channel_id=1, source_target_pairs={{0,1},{1,0},{2,3},{3,2},{4,5},{5,4},{6,7},{7,6},{8,9},{9,8},{10,11... | collective-permute-start | bytes 786440 | tf_op jit(solution)/shard_map/ppermute | solution.py:44
  17.7 0.9 %blocks_2_4.1 = (f32[2048,256]{1,0:T(8,128)S(1)}, f32[256,256]{1,0:T(8,128)S(1)}, f32[256,256]{1,0:T(8,128)S(1)}) custom-call(s32[17]{0:T(128)S(1)} %get-tuple-element.37.refs_0_.table_ref, bf16[4096,256]{1,0:T(8,128)(2,1)S(1)} %get-tuple-element.38.refs_1_, f32[32,256]{1,0:T(8,128)S(1)} %get-tuple-element.39.refs_2_, ...), custom_call_target="tpu_custom_call" | custom-call | flops 2684354560 | bytes 1048576 | tf_op jit(solution)/shard_map/blocks_2_4/pallas_call | solution.py:303
  18.7 1.1 %collective-permute-done.4.six_ref.refs_3_ = bf16[256,256]{1,0:T(8,128)(2,1)S(1)} collective-permute-done((bf16[256,256]{1,0:T(8,128)(2,1)S(1)}, bf16[256,256]{1,0:T(8,128)(2,1)S(1)}, u32[]{:S(2)}, u32[]{:S(2)}) %collective-permute-start.4) | collective-permute-done | bytes 131104 | tf_op jit(solution)/shard_map/ppermute | solution.py:32
  19.8 3.3 %collective-permute-done.6.refs_1_ = f32[256,128]{1,0:T(8,128)S(1)} collective-permute-done((f32[256,128]{1,0:T(8,128)S(1)}, f32[256,128]{1,0:T(8,128)S(1)}, u32[]{:S(2)}, u32[]{:S(2)}) %collective-permute-start.6) | collective-permute-done | bytes 131104 | tf_op jit(solution)/shard_map/ppermute | solution.py:44
  23.7 1.2 %collective-permute-start.7 = (bf16[512,256]{1,0:T(8,128)(2,1)S(1)}, bf16[512,256]{1,0:T(8,128)(2,1)S(1)}, u32[]{:S(2)}, u32[]{:S(2)}) collective-permute-start(bf16[512,256]{1,0:T(8,128)(2,1)S(1)} %get-tuple-element.46.refs_4_), channel_id=1, source_target_pairs={{0,1},{1,0},{2,3},{3,2},{4,5},{5,4},{6,7},{7,6},{8,9},{9,8},{10,11... | collective-permute-start | bytes 786440 | tf_op jit(solution)/shard_map/ppermute | solution.py:44
  24.9 0.9 %blocks_1_3.1 = (f32[2048,256]{1,0:T(8,128)S(1)}, bf16[256,512]{1,0:T(8,128)(2,1)S(1)}) custom-call(s32[17]{0:T(128)S(1)} %get-tuple-element.37.refs_0_.table_ref, bf16[4096,256]{1,0:T(8,128)(2,1)S(1)} %get-tuple-element.38.refs_1_, f32[32,256]{1,0:T(8,128)S(1)} %get-tuple-element.39.refs_2_, bf16[512,256]{1,0:T(8,128)(2,1)S(1)} %collective-permute-done.3.refs_3_, ...), custom_call_target="tpu_custom_call" | custom-call | flops 2684354560 | bytes 1048576 | tf_op jit(solution)/shard_map/blocks_1_3/pallas_call | solution.py:303
  25.8 1.4 %collective-permute-start.8 = (bf16[256,512]{1,0:T(8,128)(2,1)S(1)}, bf16[256,512]{1,0:T(8,128)(2,1)S(1)}, u32[]{:S(2)}, u32[]{:S(2)}) collective-permute-start(bf16[256,512]{1,0:T(8,128)(2,1)S(1)} %get-tuple-element.51), channel_id=1, source_target_pairs={{0,1},{1,0},{2,3},{3,2},{4,5},{5,4},{6,7},{7,6},{8,9},{9,8},{10,11... | collective-permute-start | bytes 786440 | tf_op jit(solution)/shard_map/ppermute | solution.py:44
  27.2 6.4 %collective-permute-start.9 = (f32[256,128]{1,0:T(8,128)S(1)}, f32[256,128]{1,0:T(8,128)S(1)}, u32[]{:S(2)}, u32[]{:S(2)}) collective-permute-start(f32[256,128]{1,0:T(8,128)S(1)} %get-tuple-element.53.refs_0_), channel_id=1, source_target_pairs={{0,4},{1,5},{2,6},{3,7},{4,0},{5,1},{6,2},{7,3},{8,12},{9,13},{10,... | collective-permute-start | bytes 393224 | tf_op jit(solution)/shard_map/ppermute | solution.py:44
  33.5 0.9 %blocks_5_7.1 = (f32[2048,256]{1,0:T(8,128)S(1)}, bf16[256,512]{1,0:T(8,128)(2,1)S(1)}) custom-call(s32[17]{0:T(128)S(1)} %get-tuple-element.37.refs_0_.table_ref, bf16[4096,256]{1,0:T(8,128)(2,1)S(1)} %get-tuple-element.38.refs_1_, f32[32,256]{1,0:T(8,128)S(1)} %get-tuple-element.39.refs_2_, bf16[512,256]{1,0:T(8,128)(2,1)S(1)} %collective-permute-done.7.refs_3_, ...), custom_call_target="tpu_custom_call" | custom-call | flops 2684354560 | bytes 1048576 | tf_op jit(solution)/shard_map/blocks_5_7/pallas_call | solution.py:303
  34.4 3.8 %collective-permute-start.10 = (bf16[256,512]{1,0:T(8,128)(2,1)S(1)}, bf16[256,512]{1,0:T(8,128)(2,1)S(1)}, u32[]{:S(2)}, u32[]{:S(2)}) collective-permute-start(bf16[256,512]{1,0:T(8,128)(2,1)S(1)} %get-tuple-element.52.after_ref), channel_id=1, source_target_pairs={{0,1},{1,0},{2,3},{3,2},{4,5},{5,4},{6,7},{7,6},{8,9},{9,8},{10,11... | collective-permute-start | bytes 786440 | tf_op jit(solution)/shard_map/ppermute | solution.py:44
  38.3 2.3 %collective-permute-done.9.refs_1_ = f32[256,128]{1,0:T(8,128)S(1)} collective-permute-done((f32[256,128]{1,0:T(8,128)S(1)}, f32[256,128]{1,0:T(8,128)S(1)}, u32[]{:S(2)}, u32[]{:S(2)}) %collective-permute-start.9) | collective-permute-done | bytes 131104 | tf_op jit(solution)/shard_map/ppermute | solution.py:44
  41.2 1.6 %collective-permute-start.11 = (bf16[256,128]{1,0:T(8,128)(2,1)S(1)}, bf16[256,128]{1,0:T(8,128)(2,1)S(1)}, u32[]{:S(2)}, u32[]{:S(2)}) collective-permute-start(bf16[256,128]{1,0:T(8,128)(2,1)S(1)} %get-tuple-element.58.refs_0_), channel_id=1, source_target_pairs={{0,16},{1,17},{2,18},{3,19},{4,20},{5,21},{6,22},{7,23},{8,24},{9,... | collective-permute-start | bytes 196616 | tf_op jit(solution)/shard_map/ppermute | solution.py:44
  42.7 1.1 %collective-permute-start.12 = (bf16[256,256]{1,0:T(8,128)(2,1)S(1)}, bf16[256,256]{1,0:T(8,128)(2,1)S(1)}, u32[]{:S(2)}, u32[]{:S(2)}) collective-permute-start(bf16[256,256]{1,0:T(8,128)(2,1)S(1)} %get-tuple-element.62), channel_id=1, source_target_pairs={{0,30},{1,31},{2,0},{3,1},{4,2},{5,3},{6,4},{7,5},{8,6},{9,7},{10,... | collective-permute-start | bytes 393224 | tf_op jit(solution)/shard_map/ppermute | solution.py:32
  43.9 0.9 %blocks_6_8.1 = (f32[2048,256]{1,0:T(8,128)S(1)}, f32[256,256]{1,0:T(8,128)S(1)}, f32[256,256]{1,0:T(8,128)S(1)}) custom-call(s32[17]{0:T(128)S(1)} %get-tuple-element.37.refs_0_.table_ref, bf16[4096,256]{1,0:T(8,128)(2,1)S(1)} %get-tuple-element.38.refs_1_, f32[32,256]{1,0:T(8,128)S(1)} %get-tuple-element.39.refs_2_, ...), custom_call_target="tpu_custom_call" | custom-call | flops 2684354560 | bytes 1048576 | tf_op jit(solution)/shard_map/blocks_6_8/pallas_call | solution.py:303
  46.1 2.8 %collective-permute-start.14 = (bf16[256,256]{1,0:T(8,128)(2,1)S(1)}, bf16[256,256]{1,0:T(8,128)(2,1)S(1)}, u32[]{:S(2)}, u32[]{:S(2)}) collective-permute-start(bf16[256,256]{1,0:T(8,128)(2,1)S(1)} %get-tuple-element.63), channel_id=1, source_target_pairs={{0,26},{1,27},{2,28},{3,29},{4,30},{5,31},{6,0},{7,1},{8,2},{9,3},... | collective-permute-start | bytes 393224 | tf_op jit(solution)/shard_map/ppermute | solution.py:32
  49.3 1.2 %collective-permute-start.16 = (bf16[256,128]{1,0:T(8,128)(2,1)S(1)}, bf16[256,128]{1,0:T(8,128)(2,1)S(1)}, u32[]{:S(2)}, u32[]{:S(2)}) collective-permute-start(bf16[256,128]{1,0:T(8,128)(2,1)S(1)} %get-tuple-element.64.refs_5_), channel_id=1, source_target_pairs={{0,1},{1,0},{2,3},{3,2},{4,5},{5,4},{6,7},{7,6},{8,9},{9,8},{10,11... | collective-permute-start | bytes 196616 | tf_op jit(solution)/shard_map/ppermute | solution.py:44
  50.6 5.3 %blocks_0.1 = (f32[256,2048]{1,0:T(8,128)}, f32[256,256]{1,0:T(8,128)S(1)}) custom-call(s32[17]{0:T(128)S(1)} %get-tuple-element.37.refs_0_.table_ref, bf16[4096,256]{1,0:T(8,128)(2,1)S(1)} %get-tuple-element.38.refs_1_, f32[32,256]{1,0:T(8,128)S(1)} %get-tuple-element.39.refs_2_, bf16[256,256]{1,0:T(8,128)(2,1)S(1)} %get-tuple-element.40.own_ref.refs_3_, ...), custom_call_target="tpu_custom_call" | custom-call | flops 1342177280 | bytes 1048576 | tf_op jit(solution)/shard_map/blocks_0/pallas_call | solution.py:303
  56.4 0.9 %join.1 = (f32[256,128]{1,0:T(8,128)}, f32[256,128]{1,0:T(8,128)}, f32[128,128]{1,0:T(8,128)}, f32[128,128]{1,0:T(8,128)}) custom-call(f32[256,256]{1,0:T(8,128)S(1)} %get-tuple-element.61.refs_0_, bf16[256,256]{1,0:T(8,128)(2,1)S(1)} %collective-permute-done.12.refs_1_, bf16[256,256]{1,0:T(8,128)(2,1)S(1)} %collective-permute-done.13.refs_2_, ...), custom_call_target="tpu_custom_call" | custom-call | tf_op jit(solution)/shard_map/join/pallas_call | solution.py:445
  (43 shorter events, 4.1 us)
Async XLA Ops:
  1.5 5.8 %copy-start = (bf16[256,128]{1,0:T(8,128)(2,1)S(1)}, bf16[256,128]{1,0:T(8,128)(2,1)}, u32[]{:S(2)}) copy-start(bf16[256,128]{1,0:T(8,128)(2,1)} %key_ref.1) | copy-start | bytes 196612
  1.5 5.8 %copy-start.1 = (bf16[256,128]{1,0:T(8,128)(2,1)S(1)}, bf16[256,128]{1,0:T(8,128)(2,1)}, u32[]{:S(2)}) copy-start(bf16[256,128]{1,0:T(8,128)(2,1)} %value_ref.1) | copy-start | bytes 196612
  1.5 5.8 %copy-start.2 = (bf16[256,2048]{1,0:T(8,128)(2,1)S(1)}, bf16[256,2048]{1,0:T(8,128)(2,1)}, u32[]{:S(2)}) copy-start(bf16[256,2048]{1,0:T(8,128)(2,1)} %query_ref.1) | copy-start | bytes 3145732
  1.6 5.8 %copy-start.3 = (bf16[256,2048]{1,0:T(8,128)(2,1)S(1)}, bf16[256,2048]{1,0:T(8,128)(2,1)}, u32[]{:S(2)}) copy-start(bf16[256,2048]{1,0:T(8,128)(2,1)} %grad_ref.1) | copy-start | bytes 3145732
  1.6 5.8 %copy-start.5 = (bf16[128,128]{1,0:T(8,128)(2,1)S(1)}, bf16[128,128]{1,0:T(8,128)(2,1)}, u32[]{:S(2)}) copy-start(bf16[128,128]{1,0:T(8,128)(2,1)} %sink_key_ref.1) | copy-start | bytes 98308
  1.6 5.8 %copy-start.6 = (bf16[128,128]{1,0:T(8,128)(2,1)S(1)}, bf16[128,128]{1,0:T(8,128)(2,1)}, u32[]{:S(2)}) copy-start(bf16[128,128]{1,0:T(8,128)(2,1)} %sink_value_ref.1) | copy-start | bytes 98308
  1.6 5.8 %copy-start.7 = (f32[16,256]{1,0:T(8,128)S(1)}, f32[16,256]{1,0:T(8,128)}, u32[]{:S(2)}) copy-start(f32[16,256]{1,0:T(8,128)} %lse_in.1) | copy-start | bytes 49156
  1.6 14.4 %collective-permute-start.1 = (bf16[256,256]{1,0:T(8,128)(2,1)S(1)}, bf16[256,256]{1,0:T(8,128)(2,1)S(1)}, u32[]{:S(2)}, u32[]{:S(2)}) collective-permute-start(bf16[256,256]{1,0:T(8,128)(2,1)S(1)} %mark.1), channel_id=1, source_target_pairs={{0,4},{1,5},{2,6},{3,7},{4,8},{5,9},{6,10},{7,11},{8,12},{9,13},{1... | collective-permute-start | bytes 393224 | tf_op jit(solution)/shard_map/ppermute | solution.py:32
  5.7 10.3 %collective-permute-start = (bf16[256,256]{1,0:T(8,128)(2,1)S(1)}, bf16[256,256]{1,0:T(8,128)(2,1)S(1)}, u32[]{:S(2)}, u32[]{:S(2)}) collective-permute-start(bf16[256,256]{1,0:T(8,128)(2,1)S(1)} %mark.1), channel_id=1, source_target_pairs={{0,2},{1,3},{2,4},{3,5},{4,6},{5,7},{6,8},{7,9},{8,10},{9,11},{10,... | collective-permute-start | bytes 393224 | tf_op jit(solution)/shard_map/ppermute | solution.py:32
  12.6 3.4 %collective-permute-start.2 = (f32[256,128]{1,0:T(8,128)S(1)}, f32[256,128]{1,0:T(8,128)S(1)}, u32[]{:S(2)}, u32[]{:S(2)}) collective-permute-start(f32[256,128]{1,0:T(8,128)S(1)} %get-tuple-element.42.refs_0_), channel_id=1, source_target_pairs={{0,8},{1,9},{2,10},{3,11},{4,12},{5,13},{6,14},{7,15},{8,0},{9,1},... | collective-permute-start | bytes 393224 | tf_op jit(solution)/shard_map/ppermute | solution.py:44
  12.7 6.0 %collective-permute-start.5 = (bf16[256,256]{1,0:T(8,128)(2,1)S(1)}, bf16[256,256]{1,0:T(8,128)(2,1)S(1)}, u32[]{:S(2)}, u32[]{:S(2)}) collective-permute-start(bf16[256,256]{1,0:T(8,128)(2,1)S(1)} %get-tuple-element.40.own_ref.refs_3_), channel_id=1, source_target_pairs={{0,8},{1,9},{2,10},{3,11},{4,12},{5,13},{6,14},{7,15},{8,16},{9,17... | collective-permute-start | bytes 393224 | tf_op jit(solution)/shard_map/ppermute | solution.py:32
  13.2 6.6 %collective-permute-start.4 = (bf16[256,256]{1,0:T(8,128)(2,1)S(1)}, bf16[256,256]{1,0:T(8,128)(2,1)S(1)}, u32[]{:S(2)}, u32[]{:S(2)}) collective-permute-start(bf16[256,256]{1,0:T(8,128)(2,1)S(1)} %get-tuple-element.40.own_ref.refs_3_), channel_id=1, source_target_pairs={{0,6},{1,7},{2,8},{3,9},{4,10},{5,11},{6,12},{7,13},{8,14},{9,15},... | collective-permute-start | bytes 393224 | tf_op jit(solution)/shard_map/ppermute | solution.py:32
  16.1 8.8 %collective-permute-start.3 = (bf16[512,256]{1,0:T(8,128)(2,1)S(1)}, bf16[512,256]{1,0:T(8,128)(2,1)S(1)}, u32[]{:S(2)}, u32[]{:S(2)}) collective-permute-start(bf16[512,256]{1,0:T(8,128)(2,1)S(1)} %get-tuple-element.43.refs_5_), channel_id=1, source_target_pairs={{0,1},{1,0},{2,3},{3,2},{4,5},{5,4},{6,7},{7,6},{8,9},{9,8},{10,11... | collective-permute-start | bytes 786440 | tf_op jit(solution)/shard_map/ppermute | solution.py:44
  17.7 5.4 %collective-permute-start.6 = (f32[256,128]{1,0:T(8,128)S(1)}, f32[256,128]{1,0:T(8,128)S(1)}, u32[]{:S(2)}, u32[]{:S(2)}) collective-permute-start(f32[256,128]{1,0:T(8,128)S(1)} %get-tuple-element.45.refs_0_), channel_id=1, source_target_pairs={{0,2},{1,3},{2,0},{3,1},{4,6},{5,7},{6,4},{7,5},{8,10},{9,11},{10,... | collective-permute-start | bytes 393224 | tf_op jit(solution)/shard_map/ppermute | solution.py:44
  23.7 9.9 %collective-permute-start.7 = (bf16[512,256]{1,0:T(8,128)(2,1)S(1)}, bf16[512,256]{1,0:T(8,128)(2,1)S(1)}, u32[]{:S(2)}, u32[]{:S(2)}) collective-permute-start(bf16[512,256]{1,0:T(8,128)(2,1)S(1)} %get-tuple-element.46.refs_4_), channel_id=1, source_target_pairs={{0,1},{1,0},{2,3},{3,2},{4,5},{5,4},{6,7},{7,6},{8,9},{9,8},{10,11... | collective-permute-start | bytes 786440 | tf_op jit(solution)/shard_map/ppermute | solution.py:44
  25.8 14.8 %collective-permute-start.8 = (bf16[256,512]{1,0:T(8,128)(2,1)S(1)}, bf16[256,512]{1,0:T(8,128)(2,1)S(1)}, u32[]{:S(2)}, u32[]{:S(2)}) collective-permute-start(bf16[256,512]{1,0:T(8,128)(2,1)S(1)} %get-tuple-element.51), channel_id=1, source_target_pairs={{0,1},{1,0},{2,3},{3,2},{4,5},{5,4},{6,7},{7,6},{8,9},{9,8},{10,11... | collective-permute-start | bytes 786440 | tf_op jit(solution)/shard_map/ppermute | solution.py:44
  27.2 13.4 %collective-permute-start.9 = (f32[256,128]{1,0:T(8,128)S(1)}, f32[256,128]{1,0:T(8,128)S(1)}, u32[]{:S(2)}, u32[]{:S(2)}) collective-permute-start(f32[256,128]{1,0:T(8,128)S(1)} %get-tuple-element.53.refs_0_), channel_id=1, source_target_pairs={{0,4},{1,5},{2,6},{3,7},{4,0},{5,1},{6,2},{7,3},{8,12},{9,13},{10,... | collective-permute-start | bytes 393224 | tf_op jit(solution)/shard_map/ppermute | solution.py:44
  34.4 11.1 %collective-permute-start.10 = (bf16[256,512]{1,0:T(8,128)(2,1)S(1)}, bf16[256,512]{1,0:T(8,128)(2,1)S(1)}, u32[]{:S(2)}, u32[]{:S(2)}) collective-permute-start(bf16[256,512]{1,0:T(8,128)(2,1)S(1)} %get-tuple-element.52.after_ref), channel_id=1, source_target_pairs={{0,1},{1,0},{2,3},{3,2},{4,5},{5,4},{6,7},{7,6},{8,9},{9,8},{10,11... | collective-permute-start | bytes 786440 | tf_op jit(solution)/shard_map/ppermute | solution.py:44
  41.2 4.3 %collective-permute-start.11 = (bf16[256,128]{1,0:T(8,128)(2,1)S(1)}, bf16[256,128]{1,0:T(8,128)(2,1)S(1)}, u32[]{:S(2)}, u32[]{:S(2)}) collective-permute-start(bf16[256,128]{1,0:T(8,128)(2,1)S(1)} %get-tuple-element.58.refs_0_), channel_id=1, source_target_pairs={{0,16},{1,17},{2,18},{3,19},{4,20},{5,21},{6,22},{7,23},{8,24},{9,... | collective-permute-start | bytes 196616 | tf_op jit(solution)/shard_map/ppermute | solution.py:44
  42.7 13.1 %collective-permute-start.12 = (bf16[256,256]{1,0:T(8,128)(2,1)S(1)}, bf16[256,256]{1,0:T(8,128)(2,1)S(1)}, u32[]{:S(2)}, u32[]{:S(2)}) collective-permute-start(bf16[256,256]{1,0:T(8,128)(2,1)S(1)} %get-tuple-element.62), channel_id=1, source_target_pairs={{0,30},{1,31},{2,0},{3,1},{4,2},{5,3},{6,4},{7,5},{8,6},{9,7},{10,... | collective-permute-start | bytes 393224 | tf_op jit(solution)/shard_map/ppermute | solution.py:32
  43.9 12.6 %collective-permute-start.13 = (bf16[256,256]{1,0:T(8,128)(2,1)S(1)}, bf16[256,256]{1,0:T(8,128)(2,1)S(1)}, u32[]{:S(2)}, u32[]{:S(2)}) collective-permute-start(bf16[256,256]{1,0:T(8,128)(2,1)S(1)} %get-tuple-element.54.refs_5_), channel_id=1, source_target_pairs={{0,28},{1,29},{2,30},{3,31},{4,0},{5,1},{6,2},{7,3},{8,4},{9,5},{1... | collective-permute-start | bytes 393224 | tf_op jit(solution)/shard_map/ppermute | solution.py:32
  46.1 10.3 %collective-permute-start.14 = (bf16[256,256]{1,0:T(8,128)(2,1)S(1)}, bf16[256,256]{1,0:T(8,128)(2,1)S(1)}, u32[]{:S(2)}, u32[]{:S(2)}) collective-permute-start(bf16[256,256]{1,0:T(8,128)(2,1)S(1)} %get-tuple-element.63), channel_id=1, source_target_pairs={{0,26},{1,27},{2,28},{3,29},{4,30},{5,31},{6,0},{7,1},{8,2},{9,3},... | collective-permute-start | bytes 393224 | tf_op jit(solution)/shard_map/ppermute | solution.py:32
  49.0 7.5 %collective-permute-start.15 = (bf16[256,256]{1,0:T(8,128)(2,1)S(1)}, bf16[256,256]{1,0:T(8,128)(2,1)S(1)}, u32[]{:S(2)}, u32[]{:S(2)}) collective-permute-start(bf16[256,256]{1,0:T(8,128)(2,1)S(1)} %get-tuple-element.59.refs_10_), channel_id=1, source_target_pairs={{0,24},{1,25},{2,26},{3,27},{4,28},{5,29},{6,30},{7,31},{8,0},{9,1... | collective-permute-start | bytes 393224 | tf_op jit(solution)/shard_map/ppermute | solution.py:32
  49.3 7.1 %collective-permute-start.16 = (bf16[256,128]{1,0:T(8,128)(2,1)S(1)}, bf16[256,128]{1,0:T(8,128)(2,1)S(1)}, u32[]{:S(2)}, u32[]{:S(2)}) collective-permute-start(bf16[256,128]{1,0:T(8,128)(2,1)S(1)} %get-tuple-element.64.refs_5_), channel_id=1, source_target_pairs={{0,1},{1,0},{2,3},{3,2},{4,5},{5,4},{6,7},{7,6},{8,9},{9,8},{10,11... | collective-permute-start | bytes 196616 | tf_op jit(solution)/shard_map/ppermute | solution.py:44
  (3 other events, 12.7 us)

commit v7 on v6

--- a/solution.py
+++ b/solution.py
@@ -75,8 +75,10 @@
 
     at = lax.broadcasted_iota(jnp.int32, (sinks, rows), 0)
 
+    group = 2 * UNROLL
+
     def some_heads(step, carry):
-        heads_here = [UNROLL * step + part for part in range(UNROLL)]
+        heads_here = [group * step + part for part in range(group)]
         query_t, grad_t, keep, delta = [], [], [], []
         for head in heads_here:
             strip = span(head, width)
@@ -100,7 +102,7 @@
             dquery_ref[span(head, width), :] = dquery[:, part * rows : (part + 1) * rows]
         return carry
 
-    lax.fori_loop(0, heads // UNROLL, some_heads, 0)
+    lax.fori_loop(0, heads // group, some_heads, 0)
 
 
 def sum_of(refs):

time: 57.2 us -> 57.2 us (level)
  waiting for transfers between devices: 8.01 us -> 6.4 us
  starting transfers between devices: 30.6 us -> 31.6 us
    ppermute x9, waiting for transfers between devices: 6.29 us -> 5.34 us  [swapped(): return lax.ppermute(block, AXES, route)]
    ppermute x8, waiting for transfers between devices: 1.72 us -> 1.06 us  [rotated(): lax.ppermute(block, AXES, [(i, (i + distance) % count) for i in range(cou...]
    ppermute x9, starting transfers between devices: 17.2 us -> 17.8 us  [swapped(): return lax.ppermute(block, AXES, route)]
  transfers between devices with their start and end apart: 17 -> 17, of which waited for: 5 -> 4; matrix products, arithmetic and copies ran while one was open for 0% -> 0% of each run, Pallas kernels for 26% -> 26%
where the time goes in v7:
time: 57.2 us; the launch traced here: 56.8 us
  starting transfers between devices  31.6 us (55%)
  Pallas kernels  15.7 us (27%)
  waiting for transfers between devices  6.4 us (11%)
  local copies, waits for them, and re-layouts  1.28 us (2%)
  between operations  0.91 us (2%)
  other arithmetic  0.89 us (2%)
    ppermute x9, starting transfers between devices, swapped(): return lax.ppermute(block, AXES, route)  17.8 us
    ppermute x8, starting transfers between devices, rotated(): lax.ppermute(block, AXES, [(i, (i + distance) % count) for i in range(cou...  13.8 us
    pallas_call x5, Pallas kernels, block_call(): pl.pallas_call(functools.partial(block_kernel, layout=layout, groups=grou...  9.18 us
    ppermute x9, waiting for transfers between devices, swapped(): return lax.ppermute(block, AXES, route)  5.34 us
    pallas_call x1, Pallas kernels, on_device(): pl.pallas_call(functools.partial(sink_kernel, heads=heads, width=width, s...  3.88 us
    unnamed x20, local copies, waits for them, and re-layouts  1.28 us
    pallas_call x2, Pallas kernels, fold(): pl.pallas_call(functools.partial(fold_kernel, near=near), out_shape=(shap...  1.2 us
  transfers between devices with their start and end apart: 17, of which 4 were waited for; matrix products, arithmetic and copies ran while one was open for 0% of the time, Pallas kernels for 26%

profile of v7, /device:TPU:0, one launch (start us, length us, event | category | flops | bytes accessed | tf_op | source)
XLA Modules:
  0.0 56.8 jit_solution(6350281060733111786)
XLA Ops:
  0.6 0.9 %pad_maximum_fusion.block_ref = bf16[256,256]{1,0:T(8,128)(2,1)S(1)} fusion(bf16[256,128]{1,0:T(8,128)(2,1)} %value_ref.1, bf16[256,128]{1,0:T(8,128)(2,1)} %key_ref.1), kind=kLoop, calls=%fused_computation | loop fusion | flops 262144 | bytes 262144 | tf_op jit(solution)/shard_map/concatenate | solution.py:348
  1.6 4.1 %collective-permute-start.1 = (bf16[256,256]{1,0:T(8,128)(2,1)S(1)}, bf16[256,256]{1,0:T(8,128)(2,1)S(1)}, u32[]{:S(2)}, u32[]{:S(2)}) collective-permute-start(bf16[256,256]{1,0:T(8,128)(2,1)S(1)} %mark.1), channel_id=1, source_target_pairs={{0,4},{1,5},{2,6},{3,7},{4,8},{5,9},{6,10},{7,11},{8,12},{9,13},{1... | collective-permute-start | bytes 393224 | tf_op jit(solution)/shard_map/ppermute | solution.py:32
  5.7 1.6 %collective-permute-start = (bf16[256,256]{1,0:T(8,128)(2,1)S(1)}, bf16[256,256]{1,0:T(8,128)(2,1)S(1)}, u32[]{:S(2)}, u32[]{:S(2)}) collective-permute-start(bf16[256,256]{1,0:T(8,128)(2,1)S(1)} %mark.1), channel_id=1, source_target_pairs={{0,2},{1,3},{2,4},{3,5},{4,6},{5,7},{6,8},{7,9},{8,10},{9,11},{10,... | collective-permute-start | bytes 393224 | tf_op jit(solution)/shard_map/ppermute | solution.py:32
  7.4 1.2 %copy-done.4 = bf16[256,2048]{1,0:T(8,128)(2,1)S(1)} copy-done((bf16[256,2048]{1,0:T(8,128)(2,1)S(1)}, bf16[256,2048]{1,0:T(8,128)(2,1)}, u32[]{:S(2)}) %copy-start.4) | copy-done | bytes 1048600
  8.6 3.9 %sink_keys_part.1 = (s32[17]{0:T(128)S(1)}, bf16[4096,256]{1,0:T(8,128)(2,1)S(1)}, f32[32,256]{1,0:T(8,128)S(1)}, f32[2048,256]{1,0:T(8,128)S(1)}, f32[256,128]{1,0:T(8,128)S(1)}, /*index=5*/bf16[256,256]{1,0:T(8,128)(2,1)S(1)}) custom-call(s32[16]{0:T(128)S(1)} %copy-done.8, s32[16]{0:T(128)S(1)} %copy-done.9, s32[1]{0:T(128)} %bitcast.device_ref, ...), custom_call_target="tpu_custom_call" | custom-call | flops 10000000000 | bytes 1000000 | tf_op jit(solution)/shard_map/sink_keys_part/pallas_call | solution.py:361
  13.1 2.8 %collective-permute-start.4 = (bf16[256,256]{1,0:T(8,128)(2,1)S(1)}, bf16[256,256]{1,0:T(8,128)(2,1)S(1)}, u32[]{:S(2)}, u32[]{:S(2)}) collective-permute-start(bf16[256,256]{1,0:T(8,128)(2,1)S(1)} %get-tuple-element.40.own_ref.refs_3_), channel_id=1, source_target_pairs={{0,6},{1,7},{2,8},{3,9},{4,10},{5,11},{6,12},{7,13},{8,14},{9,15},... | collective-permute-start | bytes 393224 | tf_op jit(solution)/shard_map/ppermute | solution.py:32
  16.0 1.7 %collective-permute-start.3 = (bf16[512,256]{1,0:T(8,128)(2,1)S(1)}, bf16[512,256]{1,0:T(8,128)(2,1)S(1)}, u32[]{:S(2)}, u32[]{:S(2)}) collective-permute-start(bf16[512,256]{1,0:T(8,128)(2,1)S(1)} %get-tuple-element.43.refs_5_), channel_id=1, source_target_pairs={{0,1},{1,0},{2,3},{3,2},{4,5},{5,4},{6,7},{7,6},{8,9},{9,8},{10,11... | collective-permute-start | bytes 786440 | tf_op jit(solution)/shard_map/ppermute | solution.py:44
  17.7 0.9 %blocks_2_4.1 = (f32[2048,256]{1,0:T(8,128)S(1)}, f32[256,256]{1,0:T(8,128)S(1)}, f32[256,256]{1,0:T(8,128)S(1)}) custom-call(s32[17]{0:T(128)S(1)} %get-tuple-element.37.refs_0_.table_ref, bf16[4096,256]{1,0:T(8,128)(2,1)S(1)} %get-tuple-element.38.refs_1_, f32[32,256]{1,0:T(8,128)S(1)} %get-tuple-element.39.refs_2_, ...), custom_call_target="tpu_custom_call" | custom-call | flops 2684354560 | bytes 1048576 | tf_op jit(solution)/shard_map/blocks_2_4/pallas_call | solution.py:305
  18.7 1.0 %collective-permute-done.4.six_ref.refs_3_ = bf16[256,256]{1,0:T(8,128)(2,1)S(1)} collective-permute-done((bf16[256,256]{1,0:T(8,128)(2,1)S(1)}, bf16[256,256]{1,0:T(8,128)(2,1)S(1)}, u32[]{:S(2)}, u32[]{:S(2)}) %collective-permute-start.4) | collective-permute-done | bytes 131104 | tf_op jit(solution)/shard_map/ppermute | solution.py:32
  19.7 3.3 %collective-permute-done.6.refs_1_ = f32[256,128]{1,0:T(8,128)S(1)} collective-permute-done((f32[256,128]{1,0:T(8,128)S(1)}, f32[256,128]{1,0:T(8,128)S(1)}, u32[]{:S(2)}, u32[]{:S(2)}) %collective-permute-start.6) | collective-permute-done | bytes 131104 | tf_op jit(solution)/shard_map/ppermute | solution.py:44
  23.6 1.2 %collective-permute-start.7 = (bf16[512,256]{1,0:T(8,128)(2,1)S(1)}, bf16[512,256]{1,0:T(8,128)(2,1)S(1)}, u32[]{:S(2)}, u32[]{:S(2)}) collective-permute-start(bf16[512,256]{1,0:T(8,128)(2,1)S(1)} %get-tuple-element.46.refs_4_), channel_id=1, source_target_pairs={{0,1},{1,0},{2,3},{3,2},{4,5},{5,4},{6,7},{7,6},{8,9},{9,8},{10,11... | collective-permute-start | bytes 786440 | tf_op jit(solution)/shard_map/ppermute | solution.py:44
  24.8 0.9 %blocks_1_3.1 = (f32[2048,256]{1,0:T(8,128)S(1)}, bf16[256,512]{1,0:T(8,128)(2,1)S(1)}) custom-call(s32[17]{0:T(128)S(1)} %get-tuple-element.37.refs_0_.table_ref, bf16[4096,256]{1,0:T(8,128)(2,1)S(1)} %get-tuple-element.38.refs_1_, f32[32,256]{1,0:T(8,128)S(1)} %get-tuple-element.39.refs_2_, bf16[512,256]{1,0:T(8,128)(2,1)S(1)} %collective-permute-done.3.refs_3_, ...), custom_call_target="tpu_custom_call" | custom-call | flops 2684354560 | bytes 1048576 | tf_op jit(solution)/shard_map/blocks_1_3/pallas_call | solution.py:305
  25.7 1.4 %collective-permute-start.8 = (bf16[256,512]{1,0:T(8,128)(2,1)S(1)}, bf16[256,512]{1,0:T(8,128)(2,1)S(1)}, u32[]{:S(2)}, u32[]{:S(2)}) collective-permute-start(bf16[256,512]{1,0:T(8,128)(2,1)S(1)} %get-tuple-element.51), channel_id=1, source_target_pairs={{0,1},{1,0},{2,3},{3,2},{4,5},{5,4},{6,7},{7,6},{8,9},{9,8},{10,11... | collective-permute-start | bytes 786440 | tf_op jit(solution)/shard_map/ppermute | solution.py:44
  27.1 5.8 %collective-permute-start.9 = (f32[256,128]{1,0:T(8,128)S(1)}, f32[256,128]{1,0:T(8,128)S(1)}, u32[]{:S(2)}, u32[]{:S(2)}) collective-permute-start(f32[256,128]{1,0:T(8,128)S(1)} %get-tuple-element.53.refs_0_), channel_id=1, source_target_pairs={{0,4},{1,5},{2,6},{3,7},{4,0},{5,1},{6,2},{7,3},{8,12},{9,13},{10,... | collective-permute-start | bytes 393224 | tf_op jit(solution)/shard_map/ppermute | solution.py:44
  32.9 0.9 %blocks_5_7.1 = (f32[2048,256]{1,0:T(8,128)S(1)}, bf16[256,512]{1,0:T(8,128)(2,1)S(1)}) custom-call(s32[17]{0:T(128)S(1)} %get-tuple-element.37.refs_0_.table_ref, bf16[4096,256]{1,0:T(8,128)(2,1)S(1)} %get-tuple-element.38.refs_1_, f32[32,256]{1,0:T(8,128)S(1)} %get-tuple-element.39.refs_2_, bf16[512,256]{1,0:T(8,128)(2,1)S(1)} %collective-permute-done.7.refs_3_, ...), custom_call_target="tpu_custom_call" | custom-call | flops 2684354560 | bytes 1048576 | tf_op jit(solution)/shard_map/blocks_5_7/pallas_call | solution.py:305
  33.8 4.5 %collective-permute-start.10 = (bf16[256,512]{1,0:T(8,128)(2,1)S(1)}, bf16[256,512]{1,0:T(8,128)(2,1)S(1)}, u32[]{:S(2)}, u32[]{:S(2)}) collective-permute-start(bf16[256,512]{1,0:T(8,128)(2,1)S(1)} %get-tuple-element.52.after_ref), channel_id=1, source_target_pairs={{0,1},{1,0},{2,3},{3,2},{4,5},{5,4},{6,7},{7,6},{8,9},{9,8},{10,11... | collective-permute-start | bytes 786440 | tf_op jit(solution)/shard_map/ppermute | solution.py:44
  38.2 1.6 %collective-permute-done.9.refs_1_ = f32[256,128]{1,0:T(8,128)S(1)} collective-permute-done((f32[256,128]{1,0:T(8,128)S(1)}, f32[256,128]{1,0:T(8,128)S(1)}, u32[]{:S(2)}, u32[]{:S(2)}) %collective-permute-start.9) | collective-permute-done | bytes 131104 | tf_op jit(solution)/shard_map/ppermute | solution.py:44
  40.5 1.6 %collective-permute-start.11 = (bf16[256,128]{1,0:T(8,128)(2,1)S(1)}, bf16[256,128]{1,0:T(8,128)(2,1)S(1)}, u32[]{:S(2)}, u32[]{:S(2)}) collective-permute-start(bf16[256,128]{1,0:T(8,128)(2,1)S(1)} %get-tuple-element.58.refs_0_), channel_id=1, source_target_pairs={{0,16},{1,17},{2,18},{3,19},{4,20},{5,21},{6,22},{7,23},{8,24},{9,... | collective-permute-start | bytes 196616 | tf_op jit(solution)/shard_map/ppermute | solution.py:44
  42.0 1.2 %collective-permute-start.12 = (bf16[256,256]{1,0:T(8,128)(2,1)S(1)}, bf16[256,256]{1,0:T(8,128)(2,1)S(1)}, u32[]{:S(2)}, u32[]{:S(2)}) collective-permute-start(bf16[256,256]{1,0:T(8,128)(2,1)S(1)} %get-tuple-element.62), channel_id=1, source_target_pairs={{0,30},{1,31},{2,0},{3,1},{4,2},{5,3},{6,4},{7,5},{8,6},{9,7},{10,... | collective-permute-start | bytes 393224 | tf_op jit(solution)/shard_map/ppermute | solution.py:32
  43.2 1.1 %blocks_6_8.1 = (f32[2048,256]{1,0:T(8,128)S(1)}, f32[256,256]{1,0:T(8,128)S(1)}, f32[256,256]{1,0:T(8,128)S(1)}) custom-call(s32[17]{0:T(128)S(1)} %get-tuple-element.37.refs_0_.table_ref, bf16[4096,256]{1,0:T(8,128)(2,1)S(1)} %get-tuple-element.38.refs_1_, f32[32,256]{1,0:T(8,128)S(1)} %get-tuple-element.39.refs_2_, ...), custom_call_target="tpu_custom_call" | custom-call | flops 2684354560 | bytes 1048576 | tf_op jit(solution)/shard_map/blocks_6_8/pallas_call | solution.py:305
  45.4 3.1 %collective-permute-start.14 = (bf16[256,256]{1,0:T(8,128)(2,1)S(1)}, bf16[256,256]{1,0:T(8,128)(2,1)S(1)}, u32[]{:S(2)}, u32[]{:S(2)}) collective-permute-start(bf16[256,256]{1,0:T(8,128)(2,1)S(1)} %get-tuple-element.63), channel_id=1, source_target_pairs={{0,26},{1,27},{2,28},{3,29},{4,30},{5,31},{6,0},{7,1},{8,2},{9,3},... | collective-permute-start | bytes 393224 | tf_op jit(solution)/shard_map/ppermute | solution.py:32
  49.0 1.6 %collective-permute-start.16 = (bf16[256,128]{1,0:T(8,128)(2,1)S(1)}, bf16[256,128]{1,0:T(8,128)(2,1)S(1)}, u32[]{:S(2)}, u32[]{:S(2)}) collective-permute-start(bf16[256,128]{1,0:T(8,128)(2,1)S(1)} %get-tuple-element.64.refs_5_), channel_id=1, source_target_pairs={{0,1},{1,0},{2,3},{3,2},{4,5},{5,4},{6,7},{7,6},{8,9},{9,8},{10,11... | collective-permute-start | bytes 196616 | tf_op jit(solution)/shard_map/ppermute | solution.py:44
  50.6 5.3 %blocks_0.1 = (f32[256,2048]{1,0:T(8,128)}, f32[256,256]{1,0:T(8,128)S(1)}) custom-call(s32[17]{0:T(128)S(1)} %get-tuple-element.37.refs_0_.table_ref, bf16[4096,256]{1,0:T(8,128)(2,1)S(1)} %get-tuple-element.38.refs_1_, f32[32,256]{1,0:T(8,128)S(1)} %get-tuple-element.39.refs_2_, bf16[256,256]{1,0:T(8,128)(2,1)S(1)} %get-tuple-element.40.own_ref.refs_3_, ...), custom_call_target="tpu_custom_call" | custom-call | flops 1342177280 | bytes 1048576 | tf_op jit(solution)/shard_map/blocks_0/pallas_call | solution.py:305
  56.0 0.9 %join.1 = (f32[256,128]{1,0:T(8,128)}, f32[256,128]{1,0:T(8,128)}, f32[128,128]{1,0:T(8,128)}, f32[128,128]{1,0:T(8,128)}) custom-call(f32[256,256]{1,0:T(8,128)S(1)} %get-tuple-element.61.refs_0_, bf16[256,256]{1,0:T(8,128)(2,1)S(1)} %collective-permute-done.12.refs_1_, bf16[256,256]{1,0:T(8,128)(2,1)S(1)} %collective-permute-done.13.refs_2_, ...), custom_call_target="tpu_custom_call" | custom-call | tf_op jit(solution)/shard_map/join/pallas_call | solution.py:447
  (43 shorter events, 3.4 us)
Async XLA Ops:
  1.5 5.8 %copy-start = (bf16[256,128]{1,0:T(8,128)(2,1)S(1)}, bf16[256,128]{1,0:T(8,128)(2,1)}, u32[]{:S(2)}) copy-start(bf16[256,128]{1,0:T(8,128)(2,1)} %key_ref.1) | copy-start | bytes 196612
  1.5 5.8 %copy-start.1 = (bf16[256,128]{1,0:T(8,128)(2,1)S(1)}, bf16[256,128]{1,0:T(8,128)(2,1)}, u32[]{:S(2)}) copy-start(bf16[256,128]{1,0:T(8,128)(2,1)} %value_ref.1) | copy-start | bytes 196612
  1.5 5.8 %copy-start.2 = (bf16[256,2048]{1,0:T(8,128)(2,1)S(1)}, bf16[256,2048]{1,0:T(8,128)(2,1)}, u32[]{:S(2)}) copy-start(bf16[256,2048]{1,0:T(8,128)(2,1)} %query_ref.1) | copy-start | bytes 3145732
  1.6 5.8 %copy-start.3 = (bf16[256,2048]{1,0:T(8,128)(2,1)S(1)}, bf16[256,2048]{1,0:T(8,128)(2,1)}, u32[]{:S(2)}) copy-start(bf16[256,2048]{1,0:T(8,128)(2,1)} %grad_ref.1) | copy-start | bytes 3145732
  1.6 5.8 %copy-start.5 = (bf16[128,128]{1,0:T(8,128)(2,1)S(1)}, bf16[128,128]{1,0:T(8,128)(2,1)}, u32[]{:S(2)}) copy-start(bf16[128,128]{1,0:T(8,128)(2,1)} %sink_key_ref.1) | copy-start | bytes 98308
  1.6 5.8 %copy-start.6 = (bf16[128,128]{1,0:T(8,128)(2,1)S(1)}, bf16[128,128]{1,0:T(8,128)(2,1)}, u32[]{:S(2)}) copy-start(bf16[128,128]{1,0:T(8,128)(2,1)} %sink_value_ref.1) | copy-start | bytes 98308
  1.6 5.8 %copy-start.7 = (f32[16,256]{1,0:T(8,128)S(1)}, f32[16,256]{1,0:T(8,128)}, u32[]{:S(2)}) copy-start(f32[16,256]{1,0:T(8,128)} %lse_in.1) | copy-start | bytes 49156
  1.6 14.3 %collective-permute-start.1 = (bf16[256,256]{1,0:T(8,128)(2,1)S(1)}, bf16[256,256]{1,0:T(8,128)(2,1)S(1)}, u32[]{:S(2)}, u32[]{:S(2)}) collective-permute-start(bf16[256,256]{1,0:T(8,128)(2,1)S(1)} %mark.1), channel_id=1, source_target_pairs={{0,4},{1,5},{2,6},{3,7},{4,8},{5,9},{6,10},{7,11},{8,12},{9,13},{1... | collective-permute-start | bytes 393224 | tf_op jit(solution)/shard_map/ppermute | solution.py:32
  5.7 10.2 %collective-permute-start = (bf16[256,256]{1,0:T(8,128)(2,1)S(1)}, bf16[256,256]{1,0:T(8,128)(2,1)S(1)}, u32[]{:S(2)}, u32[]{:S(2)}) collective-permute-start(bf16[256,256]{1,0:T(8,128)(2,1)S(1)} %mark.1), channel_id=1, source_target_pairs={{0,2},{1,3},{2,4},{3,5},{4,6},{5,7},{6,8},{7,9},{8,10},{9,11},{10,... | collective-permute-start | bytes 393224 | tf_op jit(solution)/shard_map/ppermute | solution.py:32
  12.5 3.4 %collective-permute-start.2 = (f32[256,128]{1,0:T(8,128)S(1)}, f32[256,128]{1,0:T(8,128)S(1)}, u32[]{:S(2)}, u32[]{:S(2)}) collective-permute-start(f32[256,128]{1,0:T(8,128)S(1)} %get-tuple-element.42.refs_0_), channel_id=1, source_target_pairs={{0,8},{1,9},{2,10},{3,11},{4,12},{5,13},{6,14},{7,15},{8,0},{9,1},... | collective-permute-start | bytes 393224 | tf_op jit(solution)/shard_map/ppermute | solution.py:44
  12.6 6.1 %collective-permute-start.5 = (bf16[256,256]{1,0:T(8,128)(2,1)S(1)}, bf16[256,256]{1,0:T(8,128)(2,1)S(1)}, u32[]{:S(2)}, u32[]{:S(2)}) collective-permute-start(bf16[256,256]{1,0:T(8,128)(2,1)S(1)} %get-tuple-element.40.own_ref.refs_3_), channel_id=1, source_target_pairs={{0,8},{1,9},{2,10},{3,11},{4,12},{5,13},{6,14},{7,15},{8,16},{9,17... | collective-permute-start | bytes 393224 | tf_op jit(solution)/shard_map/ppermute | solution.py:32
  13.1 6.6 %collective-permute-start.4 = (bf16[256,256]{1,0:T(8,128)(2,1)S(1)}, bf16[256,256]{1,0:T(8,128)(2,1)S(1)}, u32[]{:S(2)}, u32[]{:S(2)}) collective-permute-start(bf16[256,256]{1,0:T(8,128)(2,1)S(1)} %get-tuple-element.40.own_ref.refs_3_), channel_id=1, source_target_pairs={{0,6},{1,7},{2,8},{3,9},{4,10},{5,11},{6,12},{7,13},{8,14},{9,15},... | collective-permute-start | bytes 393224 | tf_op jit(solution)/shard_map/ppermute | solution.py:32
  16.0 8.8 %collective-permute-start.3 = (bf16[512,256]{1,0:T(8,128)(2,1)S(1)}, bf16[512,256]{1,0:T(8,128)(2,1)S(1)}, u32[]{:S(2)}, u32[]{:S(2)}) collective-permute-start(bf16[512,256]{1,0:T(8,128)(2,1)S(1)} %get-tuple-element.43.refs_5_), channel_id=1, source_target_pairs={{0,1},{1,0},{2,3},{3,2},{4,5},{5,4},{6,7},{7,6},{8,9},{9,8},{10,11... | collective-permute-start | bytes 786440 | tf_op jit(solution)/shard_map/ppermute | solution.py:44
  17.7 5.3 %collective-permute-start.6 = (f32[256,128]{1,0:T(8,128)S(1)}, f32[256,128]{1,0:T(8,128)S(1)}, u32[]{:S(2)}, u32[]{:S(2)}) collective-permute-start(f32[256,128]{1,0:T(8,128)S(1)} %get-tuple-element.45.refs_0_), channel_id=1, source_target_pairs={{0,2},{1,3},{2,0},{3,1},{4,6},{5,7},{6,4},{7,5},{8,10},{9,11},{10,... | collective-permute-start | bytes 393224 | tf_op jit(solution)/shard_map/ppermute | solution.py:44
  23.6 9.3 %collective-permute-start.7 = (bf16[512,256]{1,0:T(8,128)(2,1)S(1)}, bf16[512,256]{1,0:T(8,128)(2,1)S(1)}, u32[]{:S(2)}, u32[]{:S(2)}) collective-permute-start(bf16[512,256]{1,0:T(8,128)(2,1)S(1)} %get-tuple-element.46.refs_4_), channel_id=1, source_target_pairs={{0,1},{1,0},{2,3},{3,2},{4,5},{5,4},{6,7},{7,6},{8,9},{9,8},{10,11... | collective-permute-start | bytes 786440 | tf_op jit(solution)/shard_map/ppermute | solution.py:44
  25.7 14.2 %collective-permute-start.8 = (bf16[256,512]{1,0:T(8,128)(2,1)S(1)}, bf16[256,512]{1,0:T(8,128)(2,1)S(1)}, u32[]{:S(2)}, u32[]{:S(2)}) collective-permute-start(bf16[256,512]{1,0:T(8,128)(2,1)S(1)} %get-tuple-element.51), channel_id=1, source_target_pairs={{0,1},{1,0},{2,3},{3,2},{4,5},{5,4},{6,7},{7,6},{8,9},{9,8},{10,11... | collective-permute-start | bytes 786440 | tf_op jit(solution)/shard_map/ppermute | solution.py:44
  27.1 12.8 %collective-permute-start.9 = (f32[256,128]{1,0:T(8,128)S(1)}, f32[256,128]{1,0:T(8,128)S(1)}, u32[]{:S(2)}, u32[]{:S(2)}) collective-permute-start(f32[256,128]{1,0:T(8,128)S(1)} %get-tuple-element.53.refs_0_), channel_id=1, source_target_pairs={{0,4},{1,5},{2,6},{3,7},{4,0},{5,1},{6,2},{7,3},{8,12},{9,13},{10,... | collective-permute-start | bytes 393224 | tf_op jit(solution)/shard_map/ppermute | solution.py:44
  33.8 11.0 %collective-permute-start.10 = (bf16[256,512]{1,0:T(8,128)(2,1)S(1)}, bf16[256,512]{1,0:T(8,128)(2,1)S(1)}, u32[]{:S(2)}, u32[]{:S(2)}) collective-permute-start(bf16[256,512]{1,0:T(8,128)(2,1)S(1)} %get-tuple-element.52.after_ref), channel_id=1, source_target_pairs={{0,1},{1,0},{2,3},{3,2},{4,5},{5,4},{6,7},{7,6},{8,9},{9,8},{10,11... | collective-permute-start | bytes 786440 | tf_op jit(solution)/shard_map/ppermute | solution.py:44
  40.5 4.3 %collective-permute-start.11 = (bf16[256,128]{1,0:T(8,128)(2,1)S(1)}, bf16[256,128]{1,0:T(8,128)(2,1)S(1)}, u32[]{:S(2)}, u32[]{:S(2)}) collective-permute-start(bf16[256,128]{1,0:T(8,128)(2,1)S(1)} %get-tuple-element.58.refs_0_), channel_id=1, source_target_pairs={{0,16},{1,17},{2,18},{3,19},{4,20},{5,21},{6,22},{7,23},{8,24},{9,... | collective-permute-start | bytes 196616 | tf_op jit(solution)/shard_map/ppermute | solution.py:44
  42.0 13.9 %collective-permute-start.12 = (bf16[256,256]{1,0:T(8,128)(2,1)S(1)}, bf16[256,256]{1,0:T(8,128)(2,1)S(1)}, u32[]{:S(2)}, u32[]{:S(2)}) collective-permute-start(bf16[256,256]{1,0:T(8,128)(2,1)S(1)} %get-tuple-element.62), channel_id=1, source_target_pairs={{0,30},{1,31},{2,0},{3,1},{4,2},{5,3},{6,4},{7,5},{8,6},{9,7},{10,... | collective-permute-start | bytes 393224 | tf_op jit(solution)/shard_map/ppermute | solution.py:32
  43.2 12.7 %collective-permute-start.13 = (bf16[256,256]{1,0:T(8,128)(2,1)S(1)}, bf16[256,256]{1,0:T(8,128)(2,1)S(1)}, u32[]{:S(2)}, u32[]{:S(2)}) collective-permute-start(bf16[256,256]{1,0:T(8,128)(2,1)S(1)} %get-tuple-element.54.refs_5_), channel_id=1, source_target_pairs={{0,28},{1,29},{2,30},{3,31},{4,0},{5,1},{6,2},{7,3},{8,4},{9,5},{1... | collective-permute-start | bytes 393224 | tf_op jit(solution)/shard_map/ppermute | solution.py:32
  45.4 10.5 %collective-permute-start.14 = (bf16[256,256]{1,0:T(8,128)(2,1)S(1)}, bf16[256,256]{1,0:T(8,128)(2,1)S(1)}, u32[]{:S(2)}, u32[]{:S(2)}) collective-permute-start(bf16[256,256]{1,0:T(8,128)(2,1)S(1)} %get-tuple-element.63), channel_id=1, source_target_pairs={{0,26},{1,27},{2,28},{3,29},{4,30},{5,31},{6,0},{7,1},{8,2},{9,3},... | collective-permute-start | bytes 393224 | tf_op jit(solution)/shard_map/ppermute | solution.py:32
  48.5 7.5 %collective-permute-start.15 = (bf16[256,256]{1,0:T(8,128)(2,1)S(1)}, bf16[256,256]{1,0:T(8,128)(2,1)S(1)}, u32[]{:S(2)}, u32[]{:S(2)}) collective-permute-start(bf16[256,256]{1,0:T(8,128)(2,1)S(1)} %get-tuple-element.59.refs_10_), channel_id=1, source_target_pairs={{0,24},{1,25},{2,26},{3,27},{4,28},{5,29},{6,30},{7,31},{8,0},{9,1... | collective-permute-start | bytes 393224 | tf_op jit(solution)/shard_map/ppermute | solution.py:32
  49.0 7.0 %collective-permute-start.16 = (bf16[256,128]{1,0:T(8,128)(2,1)S(1)}, bf16[256,128]{1,0:T(8,128)(2,1)S(1)}, u32[]{:S(2)}, u32[]{:S(2)}) collective-permute-start(bf16[256,128]{1,0:T(8,128)(2,1)S(1)} %get-tuple-element.64.refs_5_), channel_id=1, source_target_pairs={{0,1},{1,0},{2,3},{3,2},{4,5},{5,4},{6,7},{7,6},{8,9},{9,8},{10,11... | collective-permute-start | bytes 196616 | tf_op jit(solution)/shard_map/ppermute | solution.py:44
  (3 other events, 12.7 us)
